TPU v7x, 256 devices: a whole 4x4x8 slice. The times are simulated.
256 devices in a mesh: row: 8 (over z_lo, core), col: 32 (over z_hi, x, y).
Axes of the slice: x: 4, y: 4, z: 8 (z_hi: 2, z_lo: 4; z = z_hi * 4 + z_lo), core: 2. Of those that a mesh axis runs over, the one named last changes fastest.
Arguments:
- kernel_codes: bfloat16 [24576, 49152], P('row', 'col'), may hold values from -4 to 4, as said below
- tile_scales: float32 [768, 1536], P('row', 'col'), as said below
- kernel_diagonal: float32 [49152], P('col'), may hold values from 0.5 to 1.5
- noise_variance: float32 [49152], P('col'), may hold values from 1 to 3
- targets: float32 [8, 49152], P(None, 'col'), may hold values from -25 to 25
Outputs:
- solution: float32 [8, 49152], P(None, 'col')
- residual: float32 [8, 49152], P(None, 'col')
Inputs may be any that keep to these rules, and one draw needn't show every extreme that they name: `kernel_codes`: in every slot (s, s), the entry at row i and column i of its first 768 columns is zero and unused. tile_scales lies between 0.15 / sqrt(49152) and 0.6 / sqrt(49152).
All inputs are finite; a program needn't handle non-finite values.
Results may differ from a plain program's by a relative error of at most 0.0098.
Values may be sent and summed in bfloat16 or wider, within the bound.
No kernel may reach another device: no remote copies, remote signals or barrier semaphores. Data moves between devices by JAX's collectives and lax.ppermute only.
A program may use at most 256 MiB of HBM per device.

v0:
```python
import jax
import jax.numpy as jnp
from jax import lax
from jax.sharding import PartitionSpec as P

ITERS = 2


def inner_grams(left, right):
    return jnp.dot(left, right.T, precision=lax.Precision.HIGHEST)


def solve_small(matrix, right_side):
    factor = jnp.linalg.cholesky(matrix)
    return jax.scipy.linalg.cho_solve((factor, True), right_side)


def dequantize(kernel_codes, tile_scales):
    row_count, col_count = kernel_codes.shape
    row_blocks, col_blocks = tile_scales.shape
    expanded = kernel_codes.astype(jnp.float32).reshape(
        row_blocks, row_count // row_blocks, col_blocks, col_count // col_blocks
    )
    expanded = expanded * tile_scales[:, None, :, None]
    return expanded.reshape(row_count, col_count).astype(jnp.bfloat16)


def fetch_block(rounded, row_index, row_count):
    gathered = lax.all_gather(rounded, "col", axis=1, tiled=True)
    return lax.dynamic_slice_in_dim(gathered, row_index * row_count, row_count, 1)


def local(kernel_codes, tile_scales, kernel_diagonal, noise_variance, targets):
    kernel = dequantize(kernel_codes, tile_scales)
    tile = kernel.shape[1]
    half = tile // 2
    slots = kernel.shape[0] // half
    slabs = kernel.reshape(slots, half, tile)
    row_index = lax.axis_index("row")
    col_index = lax.axis_index("col")
    firsts = row_index * slots + jnp.arange(slots, dtype=jnp.int32)
    below = (firsts < col_index)[None, :, None]
    above = (firsts > col_index)[None, :, None]
    offset = col_index - row_index * slots
    holds = (offset >= 0) & (offset < slots)
    pick = jnp.clip(offset, 0, slots - 1)
    diag_slab = lax.dynamic_index_in_dim(slabs, pick, 0, keepdims=False)
    local_diag = kernel_diagonal.astype(jnp.bfloat16)
    mixed = diag_slab[:, :half]
    upper = diag_slab[:, half:]
    index = jnp.arange(half, dtype=jnp.int32)
    lower_mask = index[:, None] > index[None, :]
    upper_mask = index[:, None] < index[None, :]
    diagonal_mask = index[:, None] == index[None, :]
    zero = jnp.zeros((), jnp.bfloat16)
    low = jnp.where(lower_mask, mixed, zero)
    high = jnp.where(upper_mask, mixed, zero)
    first_quarter = low + low.T + jnp.where(diagonal_mask, local_diag[None, :half], zero)
    last_quarter = high + high.T + jnp.where(diagonal_mask, local_diag[None, half:], zero)
    upper_turned = upper.T
    solution = jnp.zeros_like(targets)
    residual = targets
    direction = targets
    res_gram = lax.psum(inner_grams(residual, residual), "col")
    for iteration in range(ITERS):
        rounded = direction.astype(jnp.bfloat16)
        rhs_count = rounded.shape[0]
        remote = fetch_block(rounded, row_index, slots * tile).reshape(rhs_count, slots, tile)
        left = jnp.where(below, remote[:, :, :half], rounded[:, None, half:])
        first = jnp.einsum("rkh,khp->rkp", left, slabs, preferred_element_type=jnp.float32)
        right = jnp.where(below, rounded[:, None, :], remote)
        second = jnp.einsum("rkp,khp->rkh", right, slabs, preferred_element_type=jnp.float32)
        padding = jnp.zeros((rhs_count, half), jnp.float32)
        to_own = jnp.sum(jnp.where(below, first, 0.0), axis=1)
        to_own = to_own + jnp.concatenate(
            [padding, jnp.sum(jnp.where(above, second, 0.0), axis=1)], axis=1
        )
        slot_padding = jnp.zeros((rhs_count, slots, half), jnp.float32)
        to_rows = jnp.where(above, first, 0.0) + jnp.concatenate(
            [jnp.where(below, second, 0.0), slot_padding], axis=2
        )
        head = rounded[:, :half]
        tail = rounded[:, half:]
        diag_left = jnp.dot(head, first_quarter, preferred_element_type=jnp.float32) + jnp.dot(
            tail, upper_turned, preferred_element_type=jnp.float32
        )
        diag_right = jnp.dot(head, upper, preferred_element_type=jnp.float32) + jnp.dot(
            tail, last_quarter, preferred_element_type=jnp.float32
        )
        diag_term = jnp.concatenate([diag_left, diag_right], axis=1)
        mirror = lax.psum(to_rows.reshape(rhs_count, slots * tile), "col")
        own = lax.dynamic_slice_in_dim(mirror, pick * tile, tile, 1)
        partial_value = to_own + jnp.where(holds, diag_term + own, 0.0)
        applied = lax.psum(partial_value, "row") + noise_variance[None, :] * direction
        curvature = lax.psum(inner_grams(direction, applied), "col")
        step_weights = solve_small(curvature, res_gram)
        solution = solution + jnp.dot(step_weights.T, direction, precision=lax.Precision.HIGHEST)
        residual = residual - jnp.dot(step_weights.T, applied, precision=lax.Precision.HIGHEST)
        if iteration + 1 < ITERS:
            next_gram = lax.psum(inner_grams(residual, residual), "col")
            blend_weights = solve_small(res_gram, next_gram)
            direction = residual + jnp.dot(
                blend_weights.T, direction, precision=lax.Precision.HIGHEST
            )
            res_gram = next_gram
    return (solution, residual)


def solution(mesh):
    in_specs = (P("row", "col"), P("row", "col"), P("col"), P("col"), P(None, "col"))
    out_specs = (P(None, "col"), P(None, "col"))
    return jax.shard_map(local, mesh=mesh, in_specs=in_specs, out_specs=out_specs, check_vma=False)
```

profile of v0, /device:TPU:1, one launch (start us, length us, event | category | flops | bytes accessed | tf_op | source)
XLA Modules:
  0.0 1561.9 jit_solution(9212715203353536906)
XLA Ops:
  7.2 0.8 convert_element_type.17
  8.0 109.3 %all_gather.6 = bf16[8,49152]{1,0:T(8,128)(2,1)S(1)} all-gather(bf16[8,1536]{1,0:T(8,128)(2,1)S(1)} %convert_element_type.17), channel_id=1, replica_groups=mesh['row'=8,'col'=32] {'col'}, dimensions={1}, use_global_device_ids=true | all-gather | bytes 811008 | tf_op jit(solution)/shard_map/all_gather | solution.py:29
  117.3 0.8 copy.21
  118.1 23.8 %mul.38 = f32[96,32,48,32]{3,2,1,0:T(8,128)} broadcast(f32[96,48]{1,0:T(8,128)S(1)} %copy.21), dimensions={0,2} | broadcast | bytes 18892800 | tf_op jit(solution)/shard_map/mul | solution.py:24
  142.0 53.6 %mul.39 = f32[3072,1536]{1,0:T(8,128)} reshape(f32[96,32,48,32]{3,2,1,0:T(8,128)} %mul.38) | data formatting | bytes 37748736 | tf_op jit(solution)/shard_map/mul | solution.py:24
  195.6 14.2 multiply_convert_fusion
  209.8 5.2 select_reduce_fusion.1
  215.0 1.1 copy-done
  216.1 3.1 select_reduce_fusion.3
  219.3 0.7 bitcast_add_fusion.3
  220.1 1.8 dynamic-slice_bitcast_fusion
  221.9 0.9 fusion.11
  222.8 1.5 fusion.79
  224.3 2.4 copy.25
  226.7 2.4 copy.22
  229.1 2.4 fusion.2
  231.5 2.4 copy.24
  233.9 2.0 fusion.35
  235.9 1.1 fusion.7
  237.0 2.3 fusion.6
  239.3 0.2 fusion.86
  239.5 379.4 %all-reduce.8.cloned.1.call-done = f32[8,6144]{1,0:T(8,128)} async-done(((f32[8,6144]{1,0:T(8,128)}), f32[8,6144]{1,0:T(8,128)}) %all-reduce.8.cloned.1.call-update) | async-done | bytes 196624 | tf_op jit(solution)/shard_map/psum | solution.py:91
  618.9 1.5 fusion.23
  620.3 42.3 %psum.57 = f32[8,1536]{1,0:T(8,128)S(1)} all-reduce(f32[8,1536]{1,0:T(8,128)} %fusion.23), channel_id=1, replica_groups=mesh['row'=8,'col'=32] {'row'}, use_global_device_ids=true, to_apply=%region_3.4 | all-reduce | flops 12288 | bytes 98304 | tf_op jit(solution)/shard_map/psum | solution.py:94
  662.6 0.2 convolution_bitcast_fusion
  662.8 101.2 %all-reduce.4 = (f32[8,8]{0,1:T(8,128)S(1)}, f32[8,8]{0,1:T(8,128)S(1)}) all-reduce(f32[8,8]{0,1:T(8,128)S(1)} %fusion.86, f32[8,8]{0,1:T(8,128)S(1)} %convolution_bitcast_fusion), channel_id=1, replica_groups=mesh['row'=8,'col'=32] {'col'}, use_global_device_ids=true, to_apply=%region_7.9 | all-reduce | flops 128 | bytes 1024 | tf_op jit(solution)/shard_map/psum | solution.py:64
  764.2 0.6 fusion.63
  764.8 0.7 cholesky.59
  765.5 0.6 compare_reduce_fusion.2
  766.2 0.6 fusion.47
  766.8 0.6 custom-call.9
  767.5 0.2 fusion.58
  767.6 0.1 fusion.60
  767.8 1.0 convolution_subtract_fusion.1
  768.8 0.2 fusion.88
  768.9 94.2 %psum.60 = f32[8,8]{1,0:T(8,128)S(1)} all-reduce(f32[8,8]{1,0:T(8,128)S(1)} %fusion.88), channel_id=1, replica_groups=mesh['row'=8,'col'=32] {'col'}, use_global_device_ids=true, to_apply=%region_8.11 | all-reduce | flops 64 | bytes 512 | tf_op jit(solution)/shard_map/psum | solution.py:100
  863.2 1.4 cholesky.70
  864.6 0.6 compare_reduce_fusion.1
  865.2 0.6 fusion.48
  865.9 0.6 custom-call.10
  866.5 0.2 fusion.54
  866.8 0.3 fusion.81
  867.1 0.3 fusion.8
  867.4 2.1 fusion.33
  869.5 99.2 %all_gather.7 = bf16[8,49152]{1,0:T(8,128)(2,1)S(1)} all-gather(bf16[8,1536]{1,0:T(8,128)(2,1)S(1)} %get-tuple-element.16), channel_id=1, replica_groups=mesh['row'=8,'col'=32] {'col'}, dimensions={1}, use_global_device_ids=true | all-gather | bytes 811008 | tf_op jit(solution)/shard_map/all_gather | solution.py:29
  968.8 1.0 convolution_add_fusion.2
  969.7 1.1 convolution_add_fusion.3
  970.9 2.5 select_reduce_fusion.2
  973.5 1.4 select_reduce_fusion
  974.9 0.8 bitcast_add_fusion.2
  975.7 0.2 fusion.87
  975.9 431.2 %all-reduce.10.cloned.1.call-done = f32[8,6144]{1,0:T(8,128)} async-done(((f32[8,6144]{1,0:T(8,128)}), f32[8,6144]{1,0:T(8,128)}) %all-reduce.10.cloned.1.call-update) | async-done | bytes 196624 | tf_op jit(solution)/shard_map/psum | solution.py:91
  1407.2 0.8 fusion.25
  1408.0 41.7 %psum.62 = f32[8,1536]{1,0:T(8,128)S(1)} all-reduce(f32[8,1536]{1,0:T(8,128)S(1)} %fusion.25), channel_id=1, replica_groups=mesh['row'=8,'col'=32] {'row'}, use_global_device_ids=true, to_apply=%region_12.15 | all-reduce | flops 12288 | bytes 98304 | tf_op jit(solution)/shard_map/psum | solution.py:94
  1449.7 0.2 fusion.30
  1449.9 100.3 %psum.63 = f32[8,8]{0,1:T(8,128)S(1)} all-reduce(f32[8,8]{0,1:T(8,128)S(1)} %fusion.30), channel_id=1, replica_groups=mesh['row'=8,'col'=32] {'col'}, use_global_device_ids=true, to_apply=%region_13.16 | all-reduce | flops 64 | bytes 512 | tf_op jit(solution)/shard_map/psum | solution.py:95
  1550.3 0.7 cholesky.81
  1551.1 0.6 compare_reduce_fusion
  1551.7 0.6 fusion.49
  1552.4 0.6 custom-call.11
  1553.0 0.2 fusion.50
  1553.2 0.1 fusion.52
  1553.3 0.9 convolution_subtract_fusion
  1554.2 0.9 convolution_add_fusion
  (69 shorter events, 0.9 us)
Async XLA Ops:
  7.2 611.7 %all-reduce.8.cloned.1.call-start = ((), (), s32[]{:S(2)}) async-start(), calls=%async_computation | async-start | bytes 393216 | tf_op jit(solution)/shard_map/psum | solution.py:91
  8.0 133.9 %copy-start.3 = (bf16[8,1536]{1,0:T(8,128)(2,1)}, bf16[8,1536]{1,0:T(8,128)(2,1)S(1)}, u32[]{:S(2)}) copy-start(bf16[8,1536]{1,0:T(8,128)(2,1)S(1)} %convert_element_type.17) | copy-start | bytes 73732
  117.3 97.7 %copy-start.16 = (pred[4]{0:T(512)(128)(4,1)}, pred[4]{0:T(512)(128)(4,1)S(1)}, u32[]{:S(2)}) copy-start(pred[4]{0:T(512)(128)(4,1)S(1)} %fusion.66) | copy-start | bytes 16
  117.3 101.9 %copy-start.13 = (pred[4]{0:T(512)(128)(4,1)}, pred[4]{0:T(512)(128)(4,1)S(1)}, u32[]{:S(2)}) copy-start(pred[4]{0:T(512)(128)(4,1)S(1)} %fusion.65) | copy-start | bytes 16
  195.6 14.2 slice-start.3
  209.7 6.4 copy-start
  209.7 6.4 copy-start.4
  220.0 1187.1 %all-reduce.10.cloned.1.call-start = ((), (), s32[]{:S(2)}) async-start(), calls=%async_computation.1 | async-start | bytes 393216 | tf_op jit(solution)/shard_map/psum | solution.py:91
  222.8 3.9 copy-start.15
  226.7 7.2 copy-start.20
  226.7 10.2 copy-start.18
  237.0 2.4 copy-start.1
  237.0 425.6 %copy-start.5 = (f32[1536]{0:T(1024)S(1)}, f32[1536]{0:T(1024)}, u32[]{:S(2)}) copy-start(f32[1536]{0:T(1024)} %param.11) | copy-start | bytes 18436
  237.0 733.8 %slice-start = ((s8[9437184]{0:T(1024)(128)(4,1)}), s8[1048576]{0:T(1024)(128)(4,1)S(1)}, s32[]{:S(2)}) async-start(s8[9437184]{0:T(1024)(128)(4,1)} %bitcast.111), calls=%async_computation.2 | async-start | bytes 2097152
  767.8 1.0 copy-start.8
  863.1 3.6 copy-start.10
  867.1 103.7 %slice-start.1 = ((s8[9437184]{0:T(1024)(128)(4,1)}), s8[4194304]{0:T(1024)(128)(4,1)S(1)}, s32[]{:S(2)}) async-start(s8[9437184]{0:T(1024)(128)(4,1)} %bitcast.111), calls=%async_computation.3 | async-start | bytes 8388608
  867.4 101.4 %copy-start.2 = (bf16[768,768]{0,1:T(8,128)(2,1)S(1)}, bf16[768,768]{0,1:T(8,128)(2,1)}, u32[]{:S(2)}) copy-start(bf16[768,768]{0,1:T(8,128)(2,1)} %copy.25) | copy-start | bytes 3538948
  867.4 101.4 %copy-start.19 = (bf16[768]{0:T(1024)(128)(2,1)S(1)}, bf16[768]{0:T(1024)(128)(2,1)}, u32[]{:S(2)}) copy-start(bf16[768]{0:T(1024)(128)(2,1)} %copy-done.18) | copy-start | bytes 4612
  968.7 2.2 slice-start.2
  968.7 2.2 copy-start.14
  968.8 2.2 copy-start.17
  973.5 2.2 copy-start.9
  973.5 433.7 %copy-start.7 = (f32[8,768]{1,0:T(8,128)S(1)}, f32[8,768]{1,0:T(8,128)}, u32[]{:S(2)}) copy-start(f32[8,768]{1,0:T(8,128)} %convolution_add_fusion.3) | copy-start | bytes 73732
  973.5 433.7 %copy-start.12 = (f32[8,768]{1,0:T(8,128)S(1)}, f32[8,768]{1,0:T(8,128)}, u32[]{:S(2)}) copy-start(f32[8,768]{1,0:T(8,128)} %convolution_add_fusion.2) | copy-start | bytes 73732
  973.5 476.2 %copy-start.6 = (f32[1536]{0:T(1024)S(1)}, f32[1536]{0:T(1024)}, u32[]{:S(2)}) copy-start(f32[1536]{0:T(1024)} %param.11) | copy-start | bytes 18436
  973.5 579.5 %copy-start.11 = (f32[8,8]{1,0:T(8,128)S(1)}, f32[8,8]{1,0:T(8,128)}, u32[]{:S(2)}) copy-start(f32[8,8]{1,0:T(8,128)} %copy-done.10) | copy-start | bytes 772
Sparse Core Ops, SparseCore 0:
  220.1 398.6 all-reduce.7
  975.8 431.2 all-reduce.9
where the time goes:
time: 1580 us; the launch traced here: 1560 us
  waiting for transfers between devices  811 us (51%)
  blocking collectives  588 us (37%)
  local copies, waits for them, and re-layouts  88.8 us (6%)
  other arithmetic  32 us (2%)
  matrix products  27.8 us (2%)
    psum x2, waiting for transfers between devices, local(): mirror = lax.psum(to_rows.reshape(rhs_count, slots * tile), 'col')  811 us
    all_gather x2, blocking collectives, fetch_block(): gathered = lax.all_gather(rounded, 'col', axis=1, tiled=True)  208 us
    psum x1, blocking collectives, local(): res_gram = lax.psum(inner_grams(residual, residual), 'col')  101 us
    psum x1, blocking collectives, local(): curvature = lax.psum(inner_grams(direction, applied), 'col')  100 us
    psum x1, blocking collectives, local(): next_gram = lax.psum(inner_grams(residual, residual), 'col')  94.2 us
    psum x2, blocking collectives, local(): lax.psum(partial_value, 'row') + noise_variance[None, :] * direction  84 us
    mul x2, local copies, waits for them, and re-layouts, dequantize(): expanded = expanded * tile_scales[:, None, :, None]  77.4 us
  transfers between devices with their start and end apart: 2, of which 2 were waited for; matrix products, arithmetic and copies ran while one was open for 1% of the time, Pallas kernels for 0%

commit v1 on v0

v1 whole, which is shorter than its diff:
```python
import functools

import jax
import jax.numpy as jnp
from jax import lax
from jax.experimental import pallas as pl
from jax.experimental.pallas import tpu as pltpu
from jax.sharding import PartitionSpec as P

F32 = jnp.float32
BF16 = jnp.bfloat16
SHIFT = 3.0
VMEM_LIMIT = 56 * 1024 * 1024


def dequantize_slot(codes_ref, scales_ref, out_ref):
    block_rows, col_blocks = scales_ref.shape
    rows, cols = codes_ref.shape
    order = rows // block_rows
    lane_block = lax.broadcasted_iota(jnp.int32, (col_blocks, cols), 1) // (cols // col_blocks)
    own_block = lax.broadcasted_iota(jnp.int32, (col_blocks, cols), 0)
    spread = jnp.where(lane_block == own_block, 1.0, 0.0).astype(F32)
    wide = jnp.dot(
        scales_ref[...], spread, precision=lax.Precision.HIGHEST, preferred_element_type=F32
    )
    for block in range(block_rows):
        part = slice(block * order, (block + 1) * order)
        out_ref[part, :] = (codes_ref[part, :].astype(F32) * wide[block : block + 1, :]).astype(BF16)


def slot_products(slot, offset, slab_ref, rows_ref, own_ref, out_ref, total_ref):
    half, tile = slab_ref.shape
    nt = (((1,), (1,)), ((), ()))
    own = own_ref[...]
    lanes = pl.multiple_of(slot * tile, tile)
    seen = rows_ref[:, pl.ds(lanes, tile)]

    @pl.when(slot == 0)
    def _():
        total_ref[...] = jnp.zeros_like(total_ref)

    @pl.when(slot < offset)
    def _():
        slab = slab_ref[...]
        total_ref[...] += jnp.dot(seen[:, :half], slab, preferred_element_type=F32)
        second = lax.dot_general(own, slab, nt, preferred_element_type=F32)
        out_ref[:, pl.ds(lanes, half)] = second.astype(BF16)
        out_ref[:, pl.ds(lanes + half, half)] = jnp.zeros_like(second).astype(BF16)

    @pl.when(slot > offset)
    def _():
        slab = slab_ref[...]
        first = jnp.dot(own[:, half:], slab, preferred_element_type=F32)
        out_ref[:, pl.ds(lanes, tile)] = first.astype(BF16)
        total_ref[:, half:] += lax.dot_general(seen, slab, nt, preferred_element_type=F32)

    @pl.when(slot == offset)
    def _():
        mixed = slab_ref[:, :half]
        upper = slab_ref[:, half:]
        row = lax.broadcasted_iota(jnp.int32, (half, half), 0)
        col = lax.broadcasted_iota(jnp.int32, (half, half), 1)
        zero = jnp.zeros_like(mixed)
        low = jnp.where(row > col, mixed, zero)
        high = jnp.where(row < col, mixed, zero)
        head = own[:, :half]
        tail = own[:, half:]
        dot = functools.partial(jnp.dot, preferred_element_type=F32)
        dot_t = functools.partial(
            lax.dot_general, dimension_numbers=nt, preferred_element_type=F32
        )
        total_ref[:, :half] += dot(head, low) + dot_t(head, low) + dot_t(tail, upper)
        total_ref[:, half:] += dot(head, upper) + dot(tail, high) + dot_t(tail, high)
        out_ref[:, pl.ds(lanes, tile)] = jnp.zeros((own.shape[0], tile), BF16)

    @pl.when(slot == pl.num_programs(0) - 1)
    def _():
        out_ref[:, pl.ds(pl.num_programs(0) * tile, tile)] = total_ref[...].astype(BF16)


def first_kernel(offset_ref, codes_ref, scales_ref, rows_ref, own_ref, slab_ref, out_ref, total_ref):
    dequantize_slot(codes_ref, scales_ref, slab_ref)
    slot_products(
        pl.program_id(0), offset_ref[0], slab_ref, rows_ref, own_ref, out_ref, total_ref
    )


def second_kernel(offset_ref, slab_ref, rows_ref, own_ref, out_ref, gram_ref, total_ref):
    slot_products(
        pl.program_id(0), offset_ref[0], slab_ref, rows_ref, own_ref, out_ref, total_ref
    )

    @pl.when(pl.program_id(0) == pl.num_programs(0) - 1)
    def _():
        nt = (((1,), (1,)), ((), ()))
        split = rows_ref.shape[1]
        gram_ref[...] = lax.dot_general(
            out_ref[:, :split], rows_ref[...], nt, preferred_element_type=F32
        ) + lax.dot_general(out_ref[:, split:], own_ref[...], nt, preferred_element_type=F32)


def whole(shape):
    return pl.BlockSpec(shape, lambda slot: (0,) * len(shape))


def apply_first(offset, codes, scales, rows, own, slots):
    height, tile = codes.shape
    rhs = own.shape[0]
    half = height // slots
    block = pl.BlockSpec((half, tile), lambda slot: (slot, 0))
    scale_block = pl.BlockSpec((scales.shape[0] // slots, scales.shape[1]), lambda slot: (slot, 0))
    width = (slots + 1) * tile
    return pl.pallas_call(
        first_kernel,
        grid=(slots,),
        in_specs=[
            pl.BlockSpec(memory_space=pltpu.SMEM),
            block,
            scale_block,
            whole(rows.shape),
            whole(own.shape),
        ],
        out_specs=[block, whole((rhs, width))],
        out_shape=[
            jax.ShapeDtypeStruct(codes.shape, BF16),
            jax.ShapeDtypeStruct((rhs, width), BF16),
        ],
        scratch_shapes=[pltpu.VMEM((rhs, tile), F32)],
        compiler_params=pltpu.CompilerParams(vmem_limit_bytes=VMEM_LIMIT),
        name="first_product",
    )(offset, codes, scales, rows, own)


def apply_second(offset, slabs, rows, own, slots):
    height, tile = slabs.shape
    rhs = own.shape[0]
    half = height // slots
    width = (slots + 1) * tile
    return pl.pallas_call(
        second_kernel,
        grid=(slots,),
        in_specs=[
            pl.BlockSpec(memory_space=pltpu.SMEM),
            pl.BlockSpec((half, tile), lambda slot: (slot, 0)),
            whole(rows.shape),
            whole(own.shape),
        ],
        out_specs=[whole((rhs, width)), whole((rhs, rhs))],
        out_shape=[
            jax.ShapeDtypeStruct((rhs, width), BF16),
            jax.ShapeDtypeStruct((rhs, rhs), F32),
        ],
        scratch_shapes=[pltpu.VMEM((rhs, tile), F32)],
        compiler_params=pltpu.CompilerParams(vmem_limit_bytes=VMEM_LIMIT),
        name="second_product",
    )(offset, slabs, rows, own)


def times(left, right):
    total = left[:, 0:1] * right[0:1, :]
    for index in range(1, left.shape[1]):
        total = total + left[:, index : index + 1] * right[index : index + 1, :]
    return total


def inverses(matrices):
    size = matrices[0].shape[0]
    row = lax.broadcasted_iota(jnp.int32, (size, size), 0)
    col = lax.broadcasted_iota(jnp.int32, (size, size), 1)
    eye = jnp.where(row == col, 1.0, 0.0).astype(F32)
    work = [(matrix, eye) for matrix in matrices]
    for step in range(size):
        here = row == step
        following = []
        for left, right in work:
            scale = 1.0 / left[step : step + 1, step : step + 1]
            left_row = left[step : step + 1, :] * scale
            right_row = right[step : step + 1, :] * scale
            column = left[:, step : step + 1]
            following.append(
                (
                    jnp.where(here, left_row, left - column * left_row),
                    jnp.where(here, right_row, right - column * right_row),
                )
            )
        work = following
    return [right for left, right in work], eye


def final_kernel(gram_ref, base_ref, mid_ref, top_ref, solution_ref, residual_ref):
    rhs = base_ref.shape[0]
    gram = gram_ref[...]
    bb, yb, yy, wy = (gram[:, index * rhs : (index + 1) * rhs] for index in range(4))
    curvature = yb + SHIFT * bb
    (inverse_curvature, inverse_bb), eye = inverses([curvature, bb])
    step_t = times(bb, inverse_curvature)
    step = times(inverse_curvature, bb)
    a1, a1_t = eye - SHIFT * step_t, eye - SHIFT * step
    b1, b1_t = -step_t, -step

    def inner(a, a_t, b, b_t, first, cross, last):
        return times(times(a, first) + times(b, cross), a_t) + times(
            times(a, cross) + times(b, last), b_t
        )

    next_gram = inner(a1, a1_t, b1, b1_t, bb, yb, yy)
    a2 = a1 + times(next_gram, inverse_bb)
    a2_t = a1_t + times(inverse_bb, next_gram)
    curvature = inner(a2, a2_t, b1, b1_t, yb + SHIFT * bb, yy + SHIFT * yb, wy + SHIFT * yy)
    (inverse_curvature,), eye = inverses([curvature])
    last_t = times(next_gram, inverse_curvature)
    base, mid, top = base_ref[...], mid_ref[...], top_ref[...]
    from_mid = times(last_t, b1)
    from_base = times(last_t, a2)
    solution_ref[...] = times(step_t + from_base, base) + times(from_mid, mid)
    residual_ref[...] = (
        times(a1 - SHIFT * from_base, base)
        + times(b1 - from_base - SHIFT * from_mid, mid)
        - times(from_mid, top)
    )


def finish(gram, base, mid, top):
    shape = jax.ShapeDtypeStruct(base.shape, F32)
    return pl.pallas_call(final_kernel, out_shape=[shape, shape], name="small_solves")(
        gram, base, mid, top
    )


def split_three(values):
    first = lax.reduce_precision(values, 8, 7)
    rest = values - first
    second = lax.reduce_precision(rest, 8, 7)
    return jnp.concatenate([first, second, rest - second], axis=-1).astype(BF16)


def join_three(parts):
    wide = parts.astype(F32)
    size = wide.shape[-1] // 3
    return wide[..., :size] + (wide[..., size : 2 * size] + wide[..., 2 * size :])


def local(kernel_codes, tile_scales, kernel_diagonal, noise_variance, targets):
    rhs, tile = targets.shape
    half = tile // 2
    slots = kernel_codes.shape[0] // half
    row_index = lax.axis_index("row")
    col_index = lax.axis_index("col")
    row_count = lax.axis_size("row")
    col_count = lax.axis_size("col")
    offset = (col_index - row_index * slots).astype(jnp.int32).reshape(1)
    own_tile = (jnp.arange(col_count) == col_index)[:, None]
    shifted = lax.reduce_precision(kernel_diagonal, 8, 7) + (noise_variance - SHIFT)
    base_row = lax.dynamic_index_in_dim(targets, row_index, 0, keepdims=False)

    def exchange(values, axis):
        return lax.all_to_all(values, axis, 0, 0)

    def everywhere(values):
        return exchange(jnp.broadcast_to(values[None], (col_count,) + values.shape), "col")

    def tile_sums(received):
        rows = received[:, : slots * tile].astype(F32).reshape(col_count, tile)
        own = jnp.sum(received[:, slots * tile : (slots + 1) * tile].astype(F32), axis=0)
        return (rows + jnp.where(own_tile, own[None, :], 0.0)).astype(BF16)

    spread = everywhere(base_row.astype(BF16)).reshape(row_count, slots * tile)
    rows = exchange(spread, "row")
    slabs, sums = apply_first(
        offset, kernel_codes, tile_scales, rows, targets.astype(BF16), slots
    )
    sums = exchange(tile_sums(exchange(sums, "row")), "col")
    mid_row = jnp.sum(sums.astype(F32), axis=0) + shifted * base_row
    mid_high = lax.reduce_precision(mid_row, 8, 7)
    mid_low = (mid_row - mid_high).astype(BF16)
    mid_high = mid_high.astype(BF16)
    spread = everywhere(mid_high).reshape(row_count, slots * tile)
    own_pair = jnp.concatenate([mid_high, mid_low])
    spread = jnp.concatenate(
        [spread, jnp.broadcast_to(own_pair[None], (row_count, 2 * tile))], axis=1
    )
    rows = exchange(spread, "row")
    own_high = rows[:, slots * tile : (slots + 1) * tile]
    mid = own_high.astype(F32) + rows[:, (slots + 1) * tile :].astype(F32)
    sums, gram = apply_second(offset, slabs, rows[:, : slots * tile], own_high, slots)
    gram = jnp.pad(split_three(gram), ((0, 0), (0, 128 - 3 * rhs)))
    received = exchange(jnp.concatenate([sums, gram], axis=1), "row")
    gram_row = join_three(
        jnp.sum(received[:, (slots + 1) * tile :][:, : 3 * rhs].astype(F32), axis=0)
    )
    local_grams = jnp.dot(
        jnp.stack([base_row, mid_row, shifted * mid_row]),
        jnp.concatenate([targets, mid], axis=0).T,
        precision=lax.Precision.HIGHEST,
    )
    grams = jnp.concatenate(
        [
            local_grams[0, :rhs],
            local_grams[1, :rhs],
            local_grams[1, rhs:],
            local_grams[2, rhs:] + gram_row,
        ]
    )
    grams = jnp.pad(split_three(grams), (0, 128 - 12 * rhs))
    outgoing = jnp.concatenate(
        [tile_sums(received), jnp.broadcast_to(grams[None], (col_count, 128))], axis=1
    )
    sums = jnp.sum(exchange(outgoing, "col").astype(F32), axis=0)
    top_row = sums[:tile] + shifted * mid_row
    grams = jnp.pad(join_three(sums[tile : tile + 12 * rhs]), (0, 128 - 4 * rhs))
    last = exchange(
        jnp.broadcast_to(jnp.concatenate([top_row, grams])[None], (row_count, tile + 128)), "row"
    )
    return tuple(finish(last[:, tile : tile + 4 * rhs], targets, mid, last[:, :tile]))


def solution(mesh):
    in_specs = (P("row", "col"), P("row", "col"), P("col"), P("col"), P(None, "col"))
    out_specs = (P(None, "col"), P(None, "col"))
    return jax.shard_map(local, mesh=mesh, in_specs=in_specs, out_specs=out_specs, check_vma=False)
```

time: 1580 us -> 168 us (0.11); the launches traced: 1560 us -> 167 us
  waiting for transfers between devices: 811 us -> 31 us
  blocking collectives: 588 us -> 64 us
  local copies, waits for them, and re-layouts: 88.8 us -> 11.3 us
  matrix products: 27.8 us -> 0.18 us
  starting transfers between devices: 0.08 us -> 25.3 us
  Pallas kernels: 0 us -> 22 us
  other arithmetic: 32 us -> 12.4 us
    psum x2 -> x0, waiting for transfers between devices: 811 us -> none  [local(): mirror = lax.psum(to_rows.reshape(rhs_count, slots * tile), 'col')]
    psum x5 -> x0, blocking collectives: 380 us -> none  [the longest x1 101 us: local(): res_gram = lax.psum(inner_grams(residual, residual), 'col')]
    all_gather x2 -> x0, blocking collectives: 208 us -> none  [fetch_block(): gathered = lax.all_gather(rounded, 'col', axis=1, tiled=True)]
    mul x2 -> x0, local copies, waits for them, and re-layouts: 77.4 us -> none  [dequantize(): expanded = expanded * tile_scales[:, None, :, None]]
    all_to_all x0 -> x4, blocking collectives: none -> 64 us  [exchange(): return lax.all_to_all(values, axis, 0, 0)]
    all_to_all x0 -> x5, waiting for transfers between devices: none -> 31 us  [exchange(): return lax.all_to_all(values, axis, 0, 0)]
    dot_general x21 -> x1, matrix products: 26.8 us -> 0.18 us  [local(): jnp.dot(jnp.stack([base_row, mid_row, shifted * mid_row]), jnp.concatenat...]
    all_to_all x0 -> x5, starting transfers between devices: none -> 25.3 us  [exchange(): return lax.all_to_all(values, axis, 0, 0)]
  transfers between devices with their start and end apart: 2 -> 5, of which waited for: 2 -> 5; matrix products, arithmetic and copies ran while one was open for 1% -> 2% of each run, Pallas kernels for 0% -> 0%
where the time goes in v1:
time: 168 us; the launch traced here: 167 us
  blocking collectives  64 us (38%)
  waiting for transfers between devices  31 us (18%)
  starting transfers between devices  25.3 us (15%)
  Pallas kernels  22 us (13%)
  other arithmetic  12.4 us (7%)
  local copies, waits for them, and re-layouts  11.3 us (7%)
    all_to_all x4, blocking collectives, exchange(): return lax.all_to_all(values, axis, 0, 0)  64 us
    all_to_all x5, waiting for transfers between devices, exchange(): return lax.all_to_all(values, axis, 0, 0)  31 us
    all_to_all x5, starting transfers between devices, exchange(): return lax.all_to_all(values, axis, 0, 0)  25.3 us
    pallas_call x1, Pallas kernels, apply_first(): pl.pallas_call(first_kernel, grid=(slots,), in_specs=[pl.BlockSpec(memory...  10.9 us
    pallas_call x1, Pallas kernels, apply_second(): pl.pallas_call(second_kernel, grid=(slots,), in_specs=[pl.BlockSpec(memor...  7.49 us
    unnamed x30, local copies, waits for them, and re-layouts  6.89 us
    all_to_all x9, other arithmetic, exchange(): return lax.all_to_all(values, axis, 0, 0)  6.2 us
    pallas_call x1, Pallas kernels, finish(): pl.pallas_call(final_kernel, out_shape=[shape, shape], name='small_solves')  3.61 us
  transfers between devices with their start and end apart: 5, of which 5 were waited for; matrix products, arithmetic and copies ran while one was open for 2% of the time, Pallas kernels for 0%

profile of v1, /device:TPU:1, one launch (start us, length us, event | category | flops | bytes accessed | tf_op | source)
XLA Modules:
  0.0 167.1 jit_solution(18364110954363792612)
XLA Ops:
  0.7 0.8 fusion.20
  1.5 0.1 broadcast_in_dim.66
  1.6 0.6 broadcast.98
  2.2 1.2 reduce.7
  3.4 25.4 %all_to_all.83 = bf16[32,2,768]{2,1,0:T(2,128)(2,1)S(1)} all-to-all(bf16[32,2,768]{2,1,0:T(2,128)(2,1)S(1)} %reshape.134), channel_id=1, replica_groups=mesh['row'=8,'col'=32] {'col'}, dimensions={0} | all-to-all | bytes 196608 | tf_op jit(solution)/shard_map/all_to_all | solution.py:257
  28.9 0.1 reshape.135
  28.9 1.2 reduce.8
  30.1 0.7 reshape.136
  30.8 5.4 %all-to-all-start.1 = ((bf16[8,2,3072]{2,1,0:T(2,128)(2,1)}), bf16[8,2,3072]{2,1,0:T(2,128)(2,1)S(1)}, u32[]{:S(2)}, u32[]{:S(2)}) async-start(bf16[8,2,3072]{2,1,0:T(2,128)(2,1)} %reshape.136), calls=%async_computation.1 | async-start | bytes 196608 | tf_op jit(solution)/shard_map/all_to_all | solution.py:257
  36.1 1.4 convert_element_type.63.own_ref
  37.5 1.4 copy.21.scales_ref
  39.0 2.6 %all-to-all-done.1 = bf16[8,2,3072]{2,1,0:T(2,128)(2,1)S(1)} async-done(((bf16[8,2,3072]{2,1,0:T(2,128)(2,1)}), bf16[8,2,3072]{2,1,0:T(2,128)(2,1)S(1)}, u32[]{:S(2)}, u32[]{:S(2)}) %all-to-all-start.1) | async-done | bytes 98336 | tf_op jit(solution)/shard_map/all_to_all | solution.py:257
  41.6 0.1 reshape.137
  41.7 0.7 copy.40
  42.4 10.9 %first_product.1 = (bf16[3072,1536]{1,0:T(8,128)(2,1)}, bf16[8,7680]{1,0:T(8,128)(2,1)}) custom-call(s32[1]{0:T(128)} %bitcast.offset_ref, bf16[3072,1536]{1,0:T(8,128)(2,1)} %codes_ref.1, f32[96,48]{1,0:T(8,128)} %copy.21.scales_ref, bf16[8,6144]{1,0:T(8,128)(2,1)} %bitcast.41, bf16[8,1536]{1,0:T(8,128)(2,1)} %convert_element_type.63.own_ref), custom_call_target="tpu_custom_call" | custom-call | tf_op jit(solution)/shard_map/first_product/pallas_call | solution.py:113
  53.3 1.6 reduce.9
  54.9 0.7 reshape.138
  55.6 4.6 %all-to-all-start.2 = ((bf16[8,2,3840]{2,1,0:T(2,128)(2,1)}), bf16[8,2,3840]{2,1,0:T(2,128)(2,1)S(1)}, u32[]{:S(2)}, u32[]{:S(2)}) async-start(bf16[8,2,3840]{2,1,0:T(2,128)(2,1)} %reshape.138), calls=%async_computation.2 | async-start | bytes 245760 | tf_op jit(solution)/shard_map/all_to_all | solution.py:257
  60.2 5.8 %all-to-all-done.2 = bf16[8,2,3840]{2,1,0:T(2,128)(2,1)S(1)} async-done(((bf16[8,2,3840]{2,1,0:T(2,128)(2,1)}), bf16[8,2,3840]{2,1,0:T(2,128)(2,1)S(1)}, u32[]{:S(2)}, u32[]{:S(2)}) %all-to-all-start.2) | async-done | bytes 122912 | tf_op jit(solution)/shard_map/all_to_all | solution.py:257
  66.0 0.1 reshape.139
  66.2 0.1 add_convert_fusion.1
  66.3 0.6 reduce.10
  67.0 14.1 %all_to_all.84 = bf16[32,2,768]{2,1,0:T(2,128)(2,1)S(1)} all-to-all(bf16[32,2,768]{2,1,0:T(2,128)(2,1)S(1)} %reshape.140), channel_id=1, replica_groups=mesh['row'=8,'col'=32] {'col'}, dimensions={0} | all-to-all | bytes 196608 | tf_op jit(solution)/shard_map/all_to_all | solution.py:257
  81.1 0.1 reshape.141
  81.2 0.2 convert_reduce_fusion.1
  81.4 0.1 broadcast_in_dim.70
  81.6 1.2 reduce.11
  82.7 0.7 reshape.142
  83.4 3.9 %all-to-all-start.4 = ((bf16[32,2,768]{2,1,0:T(2,128)(2,1)}), bf16[32,2,768]{2,1,0:T(2,128)(2,1)S(1)}, u32[]{:S(2)}, u32[]{:S(2)}) async-start(bf16[32,2,768]{2,1,0:T(2,128)(2,1)} %reshape.142), calls=%async_computation.4 | async-start | bytes 196608 | tf_op jit(solution)/shard_map/all_to_all | solution.py:257
  87.3 11.1 %all-to-all-done.4 = bf16[32,2,768]{2,1,0:T(2,128)(2,1)S(1)} async-done(((bf16[32,2,768]{2,1,0:T(2,128)(2,1)}), bf16[32,2,768]{2,1,0:T(2,128)(2,1)S(1)}, u32[]{:S(2)}, u32[]{:S(2)}) %all-to-all-start.4) | async-done | bytes 98336 | tf_op jit(solution)/shard_map/all_to_all | solution.py:257
  98.4 0.1 reshape.143
  98.5 0.6 reduce.4
  99.1 0.1 reshape.120
  99.2 0.7 reduce.12
  99.8 0.8 reshape.144
  100.6 6.6 %all-to-all-start.5 = ((bf16[8,2,4608]{2,1,0:T(2,128)(2,1)}), bf16[8,2,4608]{2,1,0:T(2,128)(2,1)S(1)}, u32[]{:S(2)}, u32[]{:S(2)}) async-start(bf16[8,2,4608]{2,1,0:T(2,128)(2,1)} %reshape.144), calls=%async_computation.5 | async-start | bytes 294912 | tf_op jit(solution)/shard_map/all_to_all | solution.py:257
  107.2 5.9 %all-to-all-done.5 = bf16[8,2,4608]{2,1,0:T(2,128)(2,1)S(1)} async-done(((bf16[8,2,4608]{2,1,0:T(2,128)(2,1)}), bf16[8,2,4608]{2,1,0:T(2,128)(2,1)S(1)}, u32[]{:S(2)}, u32[]{:S(2)}) %all-to-all-start.5) | async-done | bytes 147488 | tf_op jit(solution)/shard_map/all_to_all | solution.py:257
  113.1 0.1 reshape.145
  113.3 0.6 slice.93.own_ref
  113.9 0.6 slice.92.rows_ref
  114.6 7.5 %second_product.1 = (bf16[8,7680]{1,0:T(8,128)(2,1)}, f32[8,8]{1,0:T(8,128)}) custom-call(s32[1]{0:T(128)} %bitcast.offset_ref, bf16[3072,1536]{1,0:T(8,128)(2,1)} %get-tuple-element.6.slab_ref, bf16[8,6144]{1,0:T(8,128)(2,1)} %slice.92.rows_ref, bf16[8,1536]{1,0:T(8,128)(2,1)} %slice.93.own_ref), custom_call_target="tpu_custom_call" | custom-call | tf_op jit(solution)/shard_map/second_product/pallas_call | solution.py:139
  122.1 0.7 reduce-precision_convert_fusion.2
  122.7 0.1 fusion.16
  122.8 0.9 maximum_bitcast_fusion.1
  123.7 0.6 reduce.13
  124.4 0.8 reshape.146
  125.2 4.9 %all-to-all-start.6 = ((bf16[8,2,3904]{2,1,0:T(2,128)(2,1)}), bf16[8,2,3904]{2,1,0:T(2,128)(2,1)S(1)}, u32[]{:S(2)}, u32[]{:S(2)}) async-start(bf16[8,2,3904]{2,1,0:T(2,128)(2,1)} %reshape.146), calls=%async_computation.6 | async-start | bytes 253952 | tf_op jit(solution)/shard_map/all_to_all | solution.py:257
  130.0 0.2 fusion
  130.2 0.1 slice_bitcast_fusion.2
  130.3 5.6 %all-to-all-done.6 = bf16[8,2,3904]{2,1,0:T(2,128)(2,1)S(1)} async-done(((bf16[8,2,3904]{2,1,0:T(2,128)(2,1)}), bf16[8,2,3904]{2,1,0:T(2,128)(2,1)S(1)}, u32[]{:S(2)}, u32[]{:S(2)}) %all-to-all-start.6) | async-done | bytes 124960 | tf_op jit(solution)/shard_map/all_to_all | solution.py:257
  135.9 0.2 reshape.147
  136.2 0.1 bitcast_add_fusion
  136.2 0.1 reduce-precision_convert_fusion.4
  136.4 0.1 select_maximum_fusion.1
  136.5 0.1 add_convert_fusion
  136.6 0.6 reduce.14
  137.2 0.2 reshape.148
  137.4 14.6 %all_to_all.85 = bf16[32,2,832]{2,1,0:T(2,128)(2,1)S(1)} all-to-all(bf16[32,2,832]{2,1,0:T(2,128)(2,1)S(1)} %reshape.148), channel_id=1, replica_groups=mesh['row'=8,'col'=32] {'col'}, dimensions={0} | all-to-all | bytes 212992 | tf_op jit(solution)/shard_map/all_to_all | solution.py:257
  152.0 0.2 reshape.149
  152.2 0.2 convert_reduce_fusion
  152.5 9.8 %all_to_all.86 = f32[8,1,1664]{2,1,0:T(1,128)S(1)} all-to-all(f32[8,1,1664]{2,1,0:T(1,128)S(1)} %broadcast_in_dim.76), channel_id=1, replica_groups=mesh['row'=8,'col'=32] {'row'}, dimensions={0} | all-to-all | bytes 106496 | tf_op jit(solution)/shard_map/all_to_all | solution.py:257
  162.3 0.6 slice.102.gram_ref
  162.9 0.6 slice.103.top_ref
  163.5 3.6 %small_solves.1 = (f32[8,1536]{1,0:T(8,128)}, f32[8,1536]{1,0:T(8,128)}) custom-call(f32[8,32]{1,0:T(8,128)} %slice.102.gram_ref, f32[8,1536]{1,0:T(8,128)} %base_ref.1, f32[8,1536]{1,0:T(8,128)} %copy-done.1, f32[8,1536]{1,0:T(8,128)} %slice.103.top_ref), custom_call_target="tpu_custom_call" | custom-call | tf_op jit(solution)/shard_map/small_solves/pallas_call | solution.py:225
  (37 shorter events, 0.6 us)
Async XLA Ops:
  0.6 80.8 %copy-start.2 = (f32[1536]{0:T(1024)S(1)}, f32[1536]{0:T(1024)}, u32[]{:S(2)}) copy-start(f32[1536]{0:T(1024)} %param.8) | copy-start | bytes 18436
  0.6 80.8 %copy-start.3 = (f32[1536]{0:T(1024)S(1)}, f32[1536]{0:T(1024)}, u32[]{:S(2)}) copy-start(f32[1536]{0:T(1024)} %param.7) | copy-start | bytes 18436
  30.8 10.9 %all-to-all-start.1 = ((bf16[8,2,3072]{2,1,0:T(2,128)(2,1)}), bf16[8,2,3072]{2,1,0:T(2,128)(2,1)S(1)}, u32[]{:S(2)}, u32[]{:S(2)}) async-start(bf16[8,2,3072]{2,1,0:T(2,128)(2,1)} %reshape.136), calls=%async_computation.1 | async-start | bytes 196608 | tf_op jit(solution)/shard_map/all_to_all | solution.py:257
  53.3 76.7 %copy-start = (f32[8,1536]{1,0:T(8,128)S(1)}, f32[8,1536]{1,0:T(8,128)}, u32[]{:S(2)}) copy-start(f32[8,1536]{1,0:T(8,128)} %base_ref.1) | copy-start | bytes 147460
  55.6 10.4 %all-to-all-start.2 = ((bf16[8,2,3840]{2,1,0:T(2,128)(2,1)}), bf16[8,2,3840]{2,1,0:T(2,128)(2,1)S(1)}, u32[]{:S(2)}, u32[]{:S(2)}) async-start(bf16[8,2,3840]{2,1,0:T(2,128)(2,1)} %reshape.138), calls=%async_computation.2 | async-start | bytes 245760 | tf_op jit(solution)/shard_map/all_to_all | solution.py:257
  83.4 15.0 %all-to-all-start.4 = ((bf16[32,2,768]{2,1,0:T(2,128)(2,1)}), bf16[32,2,768]{2,1,0:T(2,128)(2,1)S(1)}, u32[]{:S(2)}, u32[]{:S(2)}) async-start(bf16[32,2,768]{2,1,0:T(2,128)(2,1)} %reshape.142), calls=%async_computation.4 | async-start | bytes 196608 | tf_op jit(solution)/shard_map/all_to_all | solution.py:257
  100.6 12.5 %all-to-all-start.5 = ((bf16[8,2,4608]{2,1,0:T(2,128)(2,1)}), bf16[8,2,4608]{2,1,0:T(2,128)(2,1)S(1)}, u32[]{:S(2)}, u32[]{:S(2)}) async-start(bf16[8,2,4608]{2,1,0:T(2,128)(2,1)} %reshape.144), calls=%async_computation.5 | async-start | bytes 294912 | tf_op jit(solution)/shard_map/all_to_all | solution.py:257
  113.9 49.6 %copy-start.1 = (f32[8,1536]{1,0:T(8,128)}, f32[8,1536]{1,0:T(8,128)S(1)}, u32[]{:S(2)}) copy-start(f32[8,1536]{1,0:T(8,128)S(1)} %convert_add_fusion.mid_ref) | copy-start | bytes 147460
  125.2 10.7 %all-to-all-start.6 = ((bf16[8,2,3904]{2,1,0:T(2,128)(2,1)}), bf16[8,2,3904]{2,1,0:T(2,128)(2,1)S(1)}, u32[]{:S(2)}, u32[]{:S(2)}) async-start(bf16[8,2,3904]{2,1,0:T(2,128)(2,1)} %reshape.146), calls=%async_computation.6 | async-start | bytes 253952 | tf_op jit(solution)/shard_map/all_to_all | solution.py:257

commit v2 on v1

v2 whole, which is shorter than its diff:
```python
import jax
import jax.numpy as jnp
from jax import lax
from jax.experimental import pallas as pl
from jax.experimental.pallas import tpu as pltpu
from jax.sharding import PartitionSpec as P

F32 = jnp.float32
BF16 = jnp.bfloat16
SHIFT = 3.0
VMEM_LIMIT = 56 * 1024 * 1024


def dequantize_slot(codes_ref, scales_ref, out_ref):
    block_rows, col_blocks = scales_ref.shape
    rows, cols = codes_ref.shape
    order = rows // block_rows
    lane_block = lax.broadcasted_iota(jnp.int32, (col_blocks, cols), 1) // (cols // col_blocks)
    own_block = lax.broadcasted_iota(jnp.int32, (col_blocks, cols), 0)
    spread = jnp.where(lane_block == own_block, 1.0, 0.0).astype(F32)
    wide = jnp.dot(
        scales_ref[...], spread, precision=lax.Precision.HIGHEST, preferred_element_type=F32
    )
    for block in range(block_rows):
        part = slice(block * order, (block + 1) * order)
        out_ref[part, :] = (codes_ref[part, :].astype(F32) * wide[block : block + 1, :]).astype(BF16)


NT = (((1,), (1,)), ((), ()))


def dot(left, right):
    return jnp.dot(left, right, preferred_element_type=F32)


def dot_t(left, right):
    return lax.dot_general(left, right, NT, preferred_element_type=F32)


def triangles(slab_ref):
    half = slab_ref.shape[0]
    mixed = slab_ref[:, :half]
    row = lax.broadcasted_iota(jnp.int32, (half, half), 0)
    col = lax.broadcasted_iota(jnp.int32, (half, half), 1)
    zero = jnp.zeros_like(mixed)
    return jnp.where(row > col, mixed, zero), jnp.where(row < col, mixed, zero)


def toward_rows(slot, place_ref, slab_ref, own_ref, out_ref, extra_ref):
    half, tile = slab_ref.shape
    rhs = own_ref.shape[0]
    offset = place_ref[0]
    own = own_ref[...]
    row = lax.broadcasted_iota(jnp.int32, (rhs, tile), 0)
    share = jnp.sum(jnp.where(row == place_ref[1], own.astype(F32), 0.0), axis=0, keepdims=True)
    out_ref[0, :, tile:] = jnp.broadcast_to(share, (rhs, tile)).astype(BF16)

    @pl.when(slot == 0)
    def _():
        extra_ref[...] = jnp.zeros_like(extra_ref)

    @pl.when(slot < offset)
    def _():
        second = dot_t(own, slab_ref[...])
        out_ref[0, :, :half] = second.astype(BF16)
        out_ref[0, :, half:tile] = jnp.zeros((rhs, tile - half), BF16)

    @pl.when(slot > offset)
    def _():
        out_ref[0, :, :tile] = dot(own[:, half:], slab_ref[...]).astype(BF16)

    @pl.when(slot == offset)
    def _():
        low, high = triangles(slab_ref)
        head, tail = own[:, :half], own[:, half:]
        extra_ref[:, :half] = dot_t(head, low) + dot_t(tail, slab_ref[:, half:])
        extra_ref[:, half:] = dot_t(tail, high)
        out_ref[0, :, :tile] = jnp.zeros((rhs, tile), BF16)


def first_rows_kernel(place_ref, codes_ref, scales_ref, own_ref, slab_ref, out_ref, extra_ref):
    dequantize_slot(codes_ref, scales_ref, slab_ref)
    toward_rows(pl.program_id(0), place_ref, slab_ref, own_ref, out_ref, extra_ref)


def combine(received_ref, base, shifted):
    rhs, tile = base.shape
    rows = [
        jnp.sum(received_ref[:, part * tile : (part + 1) * tile].astype(F32), axis=0, keepdims=True)
        for part in range(rhs)
    ]
    others = received_ref[:, rhs * tile : (rhs + 1) * tile].astype(F32)
    return (jnp.concatenate(rows, axis=0) + others) + shifted * base


def second_rows_kernel(
    place_ref, slab_ref, received_ref, base_ref, shifted_ref, out_ref, extra_ref, mid_ref, own_ref
):
    @pl.when(pl.program_id(0) == 0)
    def _():
        mid = combine(received_ref, base_ref[...], shifted_ref[...])
        mid_ref[...] = mid
        own_ref[...] = mid.astype(BF16)

    toward_rows(pl.program_id(0), place_ref, slab_ref, own_ref, out_ref, extra_ref)


def toward_own_kernel(
    place_ref, slab_ref, rows_ref, own_ref, extra_ref, reduced_ref, out_ref, total_ref
):
    half, tile = slab_ref.shape
    rhs = own_ref.shape[0]
    slot = pl.program_id(0)
    offset = place_ref[0]
    lanes = pl.multiple_of(slot * tile, tile)

    @pl.when(slot == 0)
    def _():
        total_ref[...] = extra_ref[...]

    @pl.when(slot < offset)
    def _():
        total_ref[...] += dot(rows_ref[:, pl.ds(lanes, half)], slab_ref[...])

    @pl.when(slot > offset)
    def _():
        total_ref[:, half:] += dot_t(rows_ref[:, pl.ds(lanes, tile)], slab_ref[...])

    @pl.when(slot == offset)
    def _():
        low, high = triangles(slab_ref)
        own = own_ref[...]
        head, tail = own[:, :half], own[:, half:]
        total_ref[:, :half] += dot(head, low)
        total_ref[:, half:] += dot(head, slab_ref[:, half:]) + dot(tail, high)

    @pl.when(slot == pl.num_programs(0) - 1)
    def _():
        for part in range(rhs):
            out_ref[:, part * tile : (part + 1) * tile] = jnp.broadcast_to(
                total_ref[part : part + 1, :], (out_ref.shape[0], tile)
            ).astype(BF16)
        out_ref[:, rhs * tile :] = jnp.broadcast_to(
            reduced_ref[...], (out_ref.shape[0], tile)
        ).astype(BF16)


def whole(shape):
    return pl.BlockSpec(shape, lambda slot: (0,) * len(shape))


SMEM = pl.BlockSpec(memory_space=pltpu.SMEM)
PARAMS = pltpu.CompilerParams(vmem_limit_bytes=VMEM_LIMIT)


def block_specs(codes, rhs, slots):
    height, tile = codes.shape
    return (
        pl.BlockSpec((height // slots, tile), lambda slot: (slot, 0)),
        pl.BlockSpec((1, rhs, 2 * tile), lambda slot: (slot, 0, 0)),
    )


def first_rows(place, codes, scales, own, slots):
    rhs, tile = own.shape
    block, out_block = block_specs(codes, rhs, slots)
    scale_block = pl.BlockSpec((scales.shape[0] // slots, scales.shape[1]), lambda slot: (slot, 0))
    return pl.pallas_call(
        first_rows_kernel,
        grid=(slots,),
        in_specs=[SMEM, block, scale_block, whole(own.shape)],
        out_specs=[block, out_block, whole((rhs, tile))],
        out_shape=[
            jax.ShapeDtypeStruct(codes.shape, BF16),
            jax.ShapeDtypeStruct((slots, rhs, 2 * tile), BF16),
            jax.ShapeDtypeStruct((rhs, tile), F32),
        ],
        compiler_params=PARAMS,
        name="first_rows",
    )(place, codes, scales, own)


def second_rows(place, slabs, received, base, shifted, slots):
    rhs, tile = base.shape
    block, out_block = block_specs(slabs, rhs, slots)
    return pl.pallas_call(
        second_rows_kernel,
        grid=(slots,),
        in_specs=[SMEM, block, whole(received.shape), whole(base.shape), whole(shifted.shape)],
        out_specs=[out_block] + [whole((rhs, tile))] * 3,
        out_shape=[
            jax.ShapeDtypeStruct((slots, rhs, 2 * tile), BF16),
            jax.ShapeDtypeStruct((rhs, tile), F32),
            jax.ShapeDtypeStruct((rhs, tile), F32),
            jax.ShapeDtypeStruct((rhs, tile), BF16),
        ],
        compiler_params=PARAMS,
        name="second_rows",
    )(place, slabs, received, base, shifted)


def toward_own(place, slabs, rows, own, extra, reduced, slots, copies):
    rhs, tile = own.shape
    block, unused = block_specs(slabs, rhs, slots)
    width = (rhs + 1) * tile
    return pl.pallas_call(
        toward_own_kernel,
        grid=(slots,),
        in_specs=[
            SMEM,
            block,
            whole(rows.shape),
            whole(own.shape),
            whole(extra.shape),
            whole(reduced.shape),
        ],
        out_specs=whole((copies, width)),
        out_shape=jax.ShapeDtypeStruct((copies, width), BF16),
        scratch_shapes=[pltpu.VMEM((rhs, tile), F32)],
        compiler_params=PARAMS,
        name="toward_own",
    )(place, slabs, rows, own, extra, reduced)


def times(left, right):
    total = left[:, 0:1] * right[0:1, :]
    for index in range(1, left.shape[1]):
        total = total + left[:, index : index + 1] * right[index : index + 1, :]
    return total


def inverses(matrices):
    size = matrices[0].shape[0]
    row = lax.broadcasted_iota(jnp.int32, (size, size), 0)
    col = lax.broadcasted_iota(jnp.int32, (size, size), 1)
    eye = jnp.where(row == col, 1.0, 0.0).astype(F32)
    work = [(matrix, eye) for matrix in matrices]
    for step in range(size):
        here = row == step
        following = []
        for left, right in work:
            scale = 1.0 / left[step : step + 1, step : step + 1]
            left_row = left[step : step + 1, :] * scale
            right_row = right[step : step + 1, :] * scale
            column = left[:, step : step + 1]
            following.append(
                (
                    jnp.where(here, left_row, left - column * left_row),
                    jnp.where(here, right_row, right - column * right_row),
                )
            )
        work = following
    return [right for left, right in work], eye


def final_kernel(
    gram_ref, received_ref, base_ref, mid_ref, shifted_ref, solution_ref, residual_ref
):
    rhs = base_ref.shape[0]
    gram = gram_ref[...]
    half_wy, bb, yb, yy, wy = (gram[:, index * rhs : (index + 1) * rhs] for index in range(5))
    wy = wy + (half_wy + half_wy.T)
    curvature = yb + SHIFT * bb
    (inverse_curvature, inverse_bb), eye = inverses([curvature, bb])
    step_t = times(bb, inverse_curvature)
    step = times(inverse_curvature, bb)
    a1, a1_t = eye - SHIFT * step_t, eye - SHIFT * step
    b1, b1_t = -step_t, -step

    def inner(a, a_t, b, b_t, first, cross, last):
        return times(times(a, first) + times(b, cross), a_t) + times(
            times(a, cross) + times(b, last), b_t
        )

    next_gram = inner(a1, a1_t, b1, b1_t, bb, yb, yy)
    a2 = a1 + times(next_gram, inverse_bb)
    a2_t = a1_t + times(inverse_bb, next_gram)
    curvature = inner(a2, a2_t, b1, b1_t, yb + SHIFT * bb, yy + SHIFT * yb, wy + SHIFT * yy)
    (inverse_curvature,), eye = inverses([curvature])
    last_t = times(next_gram, inverse_curvature)
    base, mid = base_ref[...], mid_ref[...]
    top = combine(received_ref, mid, shifted_ref[...])
    from_mid = times(last_t, b1)
    from_base = times(last_t, a2)
    solution_ref[...] = times(step_t + from_base, base) + times(from_mid, mid)
    residual_ref[...] = (
        times(a1 - SHIFT * from_base, base)
        + times(b1 - from_base - SHIFT * from_mid, mid)
        - times(from_mid, top)
    )


def finish(gram, received, base, mid, shifted):
    shape = jax.ShapeDtypeStruct(base.shape, F32)
    return pl.pallas_call(
        final_kernel, out_shape=[shape, shape], compiler_params=PARAMS, name="small_solves"
    )(gram, received, base, mid, shifted)


def split_three(values):
    first = lax.reduce_precision(values, 8, 7)
    rest = values - first
    second = lax.reduce_precision(rest, 8, 7)
    return jnp.concatenate([first, second, rest - second], axis=-1).astype(BF16)


def join_three(parts):
    wide = parts.astype(F32)
    size = wide.shape[-1] // 3
    return wide[..., :size] + (wide[..., size : 2 * size] + wide[..., 2 * size :])


def local(kernel_codes, tile_scales, kernel_diagonal, noise_variance, targets):
    rhs, tile = targets.shape
    slots = kernel_codes.shape[0] // (tile // 2)
    row_index = lax.axis_index("row")
    col_index = lax.axis_index("col")
    row_count = lax.axis_size("row")
    col_count = lax.axis_size("col")
    place = jnp.stack([col_index - row_index * slots, row_index]).astype(jnp.int32)
    shifted = lax.reduce_precision(kernel_diagonal, 8, 7) + (noise_variance - SHIFT)
    moves = [
        (row * col_count + col, (col % rhs) * col_count + slots * row + col // rhs)
        for row in range(row_count)
        for col in range(col_count)
    ]

    def exchange(values, axis):
        return lax.all_to_all(values, axis, 0, 0)

    def bring(outgoing):
        received = exchange(outgoing.reshape(col_count, 2 * tile), "col")
        reduced = jnp.sum(received[:, :tile].astype(F32), axis=0, keepdims=True)
        reduced = lax.ppermute(reduced, ("row", "col"), moves)
        rows = exchange(received[:, tile:].reshape(row_count, slots * tile), "row")
        return rows, reduced

    def pick(values):
        return lax.dynamic_index_in_dim(values, row_index, 0, keepdims=True)

    own = targets.astype(BF16)
    slabs, outgoing, extra = first_rows(place, kernel_codes, tile_scales, own, slots)
    rows, reduced = bring(outgoing)
    message = toward_own(place, slabs, rows, own, extra, reduced, slots, row_count)
    received = exchange(message, "row")
    outgoing, extra, mid, own = second_rows(
        place, slabs, received, targets, shifted[None, :], slots
    )
    rows, reduced = bring(outgoing)
    mid_row = pick(mid)
    grams = jnp.dot(
        jnp.concatenate([reduced, pick(targets), mid_row, shifted[None, :] * mid_row]),
        jnp.concatenate([targets, mid]).T,
        precision=lax.Precision.HIGHEST,
    )
    grams = jnp.concatenate(
        [grams[0, rhs:], grams[1, :rhs], grams[2, :rhs], grams[2, rhs:], grams[3, rhs:]]
    )
    grams = jnp.pad(grams, (0, 128 - 5 * rhs))
    grams = exchange(jnp.broadcast_to(grams[None], (col_count, 128)), "col")
    grams = jnp.pad(split_three(jnp.sum(grams, axis=0)[: 5 * rhs]), (0, 128 - 15 * rhs))
    message = toward_own(place, slabs, rows, own, extra, reduced, slots, row_count)
    message = jnp.concatenate(
        [message, jnp.broadcast_to(grams[None], (row_count, 128))], axis=1
    )
    received = exchange(message, "row")
    grams = join_three(received[:, (rhs + 1) * tile :][:, : 15 * rhs])
    return tuple(finish(grams, received, targets, mid, shifted[None, :]))


def solution(mesh):
    in_specs = (P("row", "col"), P("row", "col"), P("col"), P("col"), P(None, "col"))
    out_specs = (P(None, "col"), P(None, "col"))
    return jax.shard_map(local, mesh=mesh, in_specs=in_specs, out_specs=out_specs, check_vma=False)
```

time: 168 us -> 179 us (1.065)
  blocking collectives: 64 us -> 36.7 us
  starting transfers between devices: 25.3 us -> 47.7 us
  Pallas kernels: 22 us -> 32.6 us
  waiting for transfers between devices: 31 us -> 35.8 us
    all_to_all x4 -> x2, blocking collectives: 64 us -> 36.7 us  [exchange(): return lax.all_to_all(values, axis, 0, 0)]
    all_to_all x5, starting transfers between devices: 25.3 us -> 40.2 us  [exchange(): return lax.all_to_all(values, axis, 0, 0)]
    pallas_call x3 -> x5, Pallas kernels: 22 us -> 32.6 us  [the longest x2 13.1 us: toward_own(): pl.pallas_call(toward_own_kernel, grid=(slots,), in_specs=[SMEM, block, w...]
    ppermute x0 -> x2, starting transfers between devices: none -> 7.53 us  [bring(): reduced = lax.ppermute(reduced, ('row', 'col'), moves)]
    all_to_all x5, waiting for transfers between devices: 31 us -> 35.6 us  [exchange(): return lax.all_to_all(values, axis, 0, 0)]
    all_to_all x9 -> x7, other arithmetic: 6.2 us -> 9.01 us  [exchange(): return lax.all_to_all(values, axis, 0, 0)]
    slice x4 -> x2, local copies, waits for them, and re-layouts: 2.48 us -> 0.02 us  [bring(): rows = exchange(received[:, tile:].reshape(row_count, slots * tile), 'row')]
    broadcast_in_dim x2 -> x0, other arithmetic: 2.34 us -> none  [everywhere(): jnp.broadcast_to(values[None], (col_count,) + values.shape)]
  transfers between devices with their start and end apart: 5 -> 7, of which waited for: 5 -> 6; matrix products, arithmetic and copies ran while one was open for 2% -> 2% of each run, Pallas kernels for 0% -> 0%
where the time goes in v2:
time: 179 us; the launch traced here: 178 us
  starting transfers between devices  47.7 us (27%)
  blocking collectives  36.7 us (21%)
  waiting for transfers between devices  35.8 us (20%)
  Pallas kernels  32.6 us (18%)
  other arithmetic  12.7 us (7%)
  local copies, waits for them, and re-layouts  10.7 us (6%)
    all_to_all x5, starting transfers between devices, exchange(): return lax.all_to_all(values, axis, 0, 0)  40.2 us
    all_to_all x2, blocking collectives, exchange(): return lax.all_to_all(values, axis, 0, 0)  36.7 us
    all_to_all x5, waiting for transfers between devices, exchange(): return lax.all_to_all(values, axis, 0, 0)  35.6 us
    pallas_call x2, Pallas kernels, toward_own(): pl.pallas_call(toward_own_kernel, grid=(slots,), in_specs=[SMEM, block, w...  13.1 us
    pallas_call x1, Pallas kernels, first_rows(): pl.pallas_call(first_rows_kernel, grid=(slots,), in_specs=[SMEM, block, s...  9.71 us
    all_to_all x7, other arithmetic, exchange(): return lax.all_to_all(values, axis, 0, 0)  9.01 us
    unnamed x31, local copies, waits for them, and re-layouts  8.54 us
    ppermute x2, starting transfers between devices, bring(): reduced = lax.ppermute(reduced, ('row', 'col'), moves)  7.53 us
  transfers between devices with their start and end apart: 7, of which 6 were waited for; matrix products, arithmetic and copies ran while one was open for 2% of the time, Pallas kernels for 0%

profile of v2, /device:TPU:1, one launch (start us, length us, event | category | flops | bytes accessed | tf_op | source)
XLA Modules:
  0.0 178.1 jit_solution(12133940592691756148)
XLA Ops:
  0.6 1.4 convert_element_type.17.own_ref
  2.0 1.4 copy.29.scales_ref
  3.5 0.6 pad_add_fusion.place_ref
  4.1 9.7 %first_rows.1 = (bf16[3072,1536]{1,0:T(8,128)(2,1)}, bf16[4,8,3072]{2,1,0:T(8,128)(2,1)}, f32[8,1536]{1,0:T(8,128)}) custom-call(s32[2]{0:T(128)} %pad_add_fusion.place_ref, bf16[3072,1536]{1,0:T(8,128)(2,1)} %codes_ref.1, f32[96,48]{1,0:T(8,128)} %copy.29.scales_ref, bf16[8,1536]{1,0:T(8,128)(2,1)} %convert_element_type.17.own_ref), custom_call_target="tpu_custom_call" | custom-call | tf_op jit(solution)/shard_map/first_rows/pallas_call | solution.py:168
  13.8 0.6 broadcast.23
  14.4 1.6 reduce.1
  16.0 0.1 reshape.32
  16.2 26.6 %all_to_all.76 = bf16[32,2,1536]{2,1,0:T(2,128)(2,1)S(1)} all-to-all(bf16[32,2,1536]{2,1,0:T(2,128)(2,1)S(1)} %reshape.32), channel_id=1, replica_groups=mesh['row'=8,'col'=32] {'col'}, dimensions={0} | all-to-all | bytes 393216 | tf_op jit(solution)/shard_map/all_to_all | solution.py:329
  42.7 0.1 reshape.33
  42.9 0.1 copy.52
  43.0 0.1 all_to_all.67
  43.0 1.2 reduce.2
  44.2 0.7 reshape.34
  44.9 6.4 %all-to-all-start.1 = ((bf16[8,2,3072]{2,1,0:T(2,128)(2,1)}), bf16[8,2,3072]{2,1,0:T(2,128)(2,1)S(1)}, u32[]{:S(2)}, u32[]{:S(2)}) async-start(bf16[8,2,3072]{2,1,0:T(2,128)(2,1)} %reshape.34), calls=%async_computation.1 | async-start | bytes 196608 | tf_op jit(solution)/shard_map/all_to_all | solution.py:329
  51.4 2.1 %collective-permute-start = (f32[1,1536]{1,0:T(1,128)S(1)}, f32[1,1536]{1,0:T(1,128)S(1)}, u32[]{:S(2)}, u32[]{:S(2)}) collective-permute-start(f32[1,1536]{1,0:T(1,128)S(1)} %broadcast_in_dim.10), channel_id=1, source_target_pairs={{0,0},{1,32},{2,64},{3,96},{4,128},{5,160},{6,192},{7,224},{8,1},{... | collective-permute-start | bytes 18440 | tf_op jit(solution)/shard_map/ppermute | solution.py:334
  53.5 3.3 %all-to-all-done.1 = bf16[8,2,3072]{2,1,0:T(2,128)(2,1)S(1)} async-done(((bf16[8,2,3072]{2,1,0:T(2,128)(2,1)}), bf16[8,2,3072]{2,1,0:T(2,128)(2,1)S(1)}, u32[]{:S(2)}, u32[]{:S(2)}) %all-to-all-start.1) | async-done | bytes 98336 | tf_op jit(solution)/shard_map/all_to_all | solution.py:329
  56.8 0.1 reshape.35
  56.9 0.7 copy.54
  57.6 0.0 collective-permute-done.reduced_ref
  57.6 0.6 copy-done.5
  58.2 6.5 %toward_own.2 = bf16[8,13824]{1,0:T(8,128)(2,1)} custom-call(s32[2]{0:T(128)} %pad_add_fusion.place_ref, bf16[3072,1536]{1,0:T(8,128)(2,1)} %get-tuple-element.9.slab_ref, bf16[8,6144]{1,0:T(8,128)(2,1)} %bitcast.44, bf16[8,1536]{1,0:T(8,128)(2,1)} %convert_element_type.17.own_ref, f32[8,1536]{1,0:T(8,128)} %get-tuple-element.11.extra_ref, f32[1,1536]{1,0:T(1,128)} %copy-done.5), custom_call_target="tpu_custom_call" | custom-call | tf_op jit(solution)/shard_map/toward_own/pallas_call | solution.py:206
  64.7 1.7 reduce.3
  66.4 0.8 reshape.36
  67.1 9.6 %all-to-all-start.2 = ((bf16[8,2,6912]{2,1,0:T(2,128)(2,1)}), bf16[8,2,6912]{2,1,0:T(2,128)(2,1)S(1)}, u32[]{:S(2)}, u32[]{:S(2)}) async-start(bf16[8,2,6912]{2,1,0:T(2,128)(2,1)} %reshape.36), calls=%async_computation.2 | async-start | bytes 442368 | tf_op jit(solution)/shard_map/all_to_all | solution.py:329
  76.7 0.0 copy-done.2
  76.7 0.6 broadcast_in_dim.11.shifted_ref
  77.3 6.2 %all-to-all-done.2 = bf16[8,2,6912]{2,1,0:T(2,128)(2,1)S(1)} async-done(((bf16[8,2,6912]{2,1,0:T(2,128)(2,1)}), bf16[8,2,6912]{2,1,0:T(2,128)(2,1)S(1)}, u32[]{:S(2)}, u32[]{:S(2)}) %all-to-all-start.2) | async-done | bytes 221216 | tf_op jit(solution)/shard_map/all_to_all | solution.py:329
  83.6 0.2 reshape.37
  83.7 0.7 copy.50
  84.5 5.9 %second_rows.1 = (bf16[4,8,3072]{2,1,0:T(8,128)(2,1)}, f32[8,1536]{1,0:T(8,128)}, f32[8,1536]{1,0:T(8,128)}, bf16[8,1536]{1,0:T(8,128)(2,1)}) custom-call(s32[2]{0:T(128)} %pad_add_fusion.place_ref, bf16[3072,1536]{1,0:T(8,128)(2,1)} %get-tuple-element.9.slab_ref, bf16[8,13824]{1,0:T(8,128)(2,1)} %bitcast.39, f32[8,1536]{1,0:T(8,128)} %base_ref.3, ...), custom_call_target="tpu_custom_call" | custom-call | tf_op jit(solution)/shard_map/second_rows/pallas_call | solution.py:186
  90.4 1.6 reduce.4
  92.0 0.8 reshape.38
  92.8 5.8 %all-to-all-start.3 = ((bf16[32,2,1536]{2,1,0:T(2,128)(2,1)}), bf16[32,2,1536]{2,1,0:T(2,128)(2,1)S(1)}, u32[]{:S(2)}, u32[]{:S(2)}) async-start(bf16[32,2,1536]{2,1,0:T(2,128)(2,1)} %reshape.38), calls=%async_computation.3 | async-start | bytes 393216 | tf_op jit(solution)/shard_map/all_to_all | solution.py:329
  98.6 11.7 %all-to-all-done.3 = bf16[32,2,1536]{2,1,0:T(2,128)(2,1)S(1)} async-done(((bf16[32,2,1536]{2,1,0:T(2,128)(2,1)}), bf16[32,2,1536]{2,1,0:T(2,128)(2,1)S(1)}, u32[]{:S(2)}, u32[]{:S(2)}) %all-to-all-start.3) | async-done | bytes 196640 | tf_op jit(solution)/shard_map/all_to_all | solution.py:329
  110.3 0.1 reshape.39
  110.4 0.1 copy.51
  110.6 5.4 %collective-permute-start.1 = (f32[1,1536]{1,0:T(1,128)S(1)}, f32[1,1536]{1,0:T(1,128)S(1)}, u32[]{:S(2)}, u32[]{:S(2)}) collective-permute-start(f32[1,1536]{1,0:T(1,128)S(1)} %broadcast_in_dim.12), channel_id=1, source_target_pairs={{0,0},{1,32},{2,64},{3,96},{4,128},{5,160},{6,192},{7,224},{8,1},{... | collective-permute-start | bytes 18440 | tf_op jit(solution)/shard_map/ppermute | solution.py:334
  116.0 0.0 copy-done.1
  116.0 0.8 fusion.13
  116.8 0.3 collective-permute-done.1.reduced_ref
  117.1 1.0 fusion
  118.1 0.1 slice_bitcast_fusion
  118.2 0.1 concatenate.18
  118.3 0.7 broadcast_in_dim.26
  118.9 10.4 %all-to-all-start.5 = ((f32[32,1,128]{2,1,0:T(1,128)}), f32[32,1,128]{2,1,0:T(1,128)S(1)}, u32[]{:S(2)}, u32[]{:S(2)}) async-start(f32[32,1,128]{2,1,0:T(1,128)} %broadcast_in_dim.26), calls=%async_computation.5 | async-start | bytes 32768 | tf_op jit(solution)/shard_map/all_to_all | solution.py:329
  129.3 0.1 all_to_all.68
  129.4 1.2 reduce.5
  130.5 0.7 reshape.40
  131.2 9.0 %all-to-all-done.5 = f32[32,1,128]{2,1,0:T(1,128)S(1)} async-done(((f32[32,1,128]{2,1,0:T(1,128)}), f32[32,1,128]{2,1,0:T(1,128)S(1)}, u32[]{:S(2)}, u32[]{:S(2)}) %all-to-all-start.5) | async-done | bytes 16416 | tf_op jit(solution)/shard_map/all_to_all | solution.py:329
  140.2 8.0 %all-to-all-start.4 = ((bf16[8,2,3072]{2,1,0:T(2,128)(2,1)}), bf16[8,2,3072]{2,1,0:T(2,128)(2,1)S(1)}, u32[]{:S(2)}, u32[]{:S(2)}) async-start(bf16[8,2,3072]{2,1,0:T(2,128)(2,1)} %reshape.40), calls=%async_computation.4 | async-start | bytes 196608 | tf_op jit(solution)/shard_map/all_to_all | solution.py:329
  148.2 0.1 select_maximum_fusion
  148.3 5.4 %all-to-all-done.4 = bf16[8,2,3072]{2,1,0:T(2,128)(2,1)S(1)} async-done(((bf16[8,2,3072]{2,1,0:T(2,128)(2,1)}), bf16[8,2,3072]{2,1,0:T(2,128)(2,1)S(1)}, u32[]{:S(2)}, u32[]{:S(2)}) %all-to-all-start.4) | async-done | bytes 98336 | tf_op jit(solution)/shard_map/all_to_all | solution.py:329
  153.7 0.1 reshape.41
  153.8 0.7 copy.53
  154.5 6.5 %toward_own.3 = bf16[8,13824]{1,0:T(8,128)(2,1)} custom-call(s32[2]{0:T(128)} %pad_add_fusion.place_ref, bf16[3072,1536]{1,0:T(8,128)(2,1)} %get-tuple-element.9.slab_ref, bf16[8,6144]{1,0:T(8,128)(2,1)} %bitcast.45, bf16[8,1536]{1,0:T(8,128)(2,1)} %get-tuple-element.13.own_ref, f32[8,1536]{1,0:T(8,128)} %get-tuple-element.14.extra_ref, f32[1,1536]{1,0:T(1,128)} %copy-done.4), custom_call_target="tpu_custom_call" | custom-call | tf_op jit(solution)/shard_map/toward_own/pallas_call | solution.py:206
  161.0 1.0 maximum_bitcast_fusion
  162.0 0.8 reduce.6
  162.8 0.2 reshape.42
  163.0 10.2 %all_to_all.77 = bf16[8,2,6976]{2,1,0:T(2,128)(2,1)S(1)} all-to-all(bf16[8,2,6976]{2,1,0:T(2,128)(2,1)S(1)} %reshape.42), channel_id=1, replica_groups=mesh['row'=8,'col'=32] {'row'}, dimensions={0} | all-to-all | bytes 446464 | tf_op jit(solution)/shard_map/all_to_all | solution.py:329
  173.2 0.3 reshape.43
  173.5 0.0 copy-start
  173.5 0.7 add_add_fusion.1.gram_ref
  174.2 0.0 copy-done
  174.2 3.9 %small_solves.1 = (f32[8,1536]{1,0:T(8,128)}, f32[8,1536]{1,0:T(8,128)}) custom-call(f32[8,40]{1,0:T(8,128)} %add_add_fusion.1.gram_ref, bf16[8,13952]{1,0:T(8,128)(2,1)} %bitcast.37, f32[8,1536]{1,0:T(8,128)} %base_ref.3, f32[8,1536]{1,0:T(8,128)} %get-tuple-element.15.mid_ref, f32[1,1536]{1,0:T(1,128)} %broadcast_in_dim.11.shifted_ref), custom_call_target="tpu_custom_call" | custom-call | tf_op jit(solution)/shard_map/small_solves/pallas_call | solution.py:295
  (20 shorter events, 0.2 us)
Async XLA Ops:
  13.8 62.9 %copy-start.2 = (f32[1536]{0:T(1024)S(1)}, f32[1536]{0:T(1024)}, u32[]{:S(2)}) copy-start(f32[1536]{0:T(1024)} %param.8) | copy-start | bytes 18436
  13.8 62.9 %copy-start.3 = (f32[1536]{0:T(1024)S(1)}, f32[1536]{0:T(1024)}, u32[]{:S(2)}) copy-start(f32[1536]{0:T(1024)} %param.7) | copy-start | bytes 18436
  44.9 11.9 %all-to-all-start.1 = ((bf16[8,2,3072]{2,1,0:T(2,128)(2,1)}), bf16[8,2,3072]{2,1,0:T(2,128)(2,1)S(1)}, u32[]{:S(2)}, u32[]{:S(2)}) async-start(bf16[8,2,3072]{2,1,0:T(2,128)(2,1)} %reshape.34), calls=%async_computation.1 | async-start | bytes 196608 | tf_op jit(solution)/shard_map/all_to_all | solution.py:329
  51.4 6.2 %collective-permute-start = (f32[1,1536]{1,0:T(1,128)S(1)}, f32[1,1536]{1,0:T(1,128)S(1)}, u32[]{:S(2)}, u32[]{:S(2)}) collective-permute-start(f32[1,1536]{1,0:T(1,128)S(1)} %broadcast_in_dim.10), channel_id=1, source_target_pairs={{0,0},{1,32},{2,64},{3,96},{4,128},{5,160},{6,192},{7,224},{8,1},{... | collective-permute-start | bytes 18440 | tf_op jit(solution)/shard_map/ppermute | solution.py:334
  57.6 0.6 copy-start.5
  64.7 51.3 %copy-start.1 = (f32[8,1536]{1,0:T(8,128)S(1)}, f32[8,1536]{1,0:T(8,128)}, u32[]{:S(2)}) copy-start(f32[8,1536]{1,0:T(8,128)} %base_ref.3) | copy-start | bytes 147460
  67.1 16.4 %all-to-all-start.2 = ((bf16[8,2,6912]{2,1,0:T(2,128)(2,1)}), bf16[8,2,6912]{2,1,0:T(2,128)(2,1)S(1)}, u32[]{:S(2)}, u32[]{:S(2)}) async-start(bf16[8,2,6912]{2,1,0:T(2,128)(2,1)} %reshape.36), calls=%async_computation.2 | async-start | bytes 442368 | tf_op jit(solution)/shard_map/all_to_all | solution.py:329
  92.8 17.4 %all-to-all-start.3 = ((bf16[32,2,1536]{2,1,0:T(2,128)(2,1)}), bf16[32,2,1536]{2,1,0:T(2,128)(2,1)S(1)}, u32[]{:S(2)}, u32[]{:S(2)}) async-start(bf16[32,2,1536]{2,1,0:T(2,128)(2,1)} %reshape.38), calls=%async_computation.3 | async-start | bytes 393216 | tf_op jit(solution)/shard_map/all_to_all | solution.py:329
  110.6 6.5 %collective-permute-start.1 = (f32[1,1536]{1,0:T(1,128)S(1)}, f32[1,1536]{1,0:T(1,128)S(1)}, u32[]{:S(2)}, u32[]{:S(2)}) collective-permute-start(f32[1,1536]{1,0:T(1,128)S(1)} %broadcast_in_dim.12), channel_id=1, source_target_pairs={{0,0},{1,32},{2,64},{3,96},{4,128},{5,160},{6,192},{7,224},{8,1},{... | collective-permute-start | bytes 18440 | tf_op jit(solution)/shard_map/ppermute | solution.py:334
  117.1 37.4 %copy-start.4 = (f32[1,1536]{1,0:T(1,128)}, f32[1,1536]{1,0:T(1,128)S(1)}, u32[]{:S(2)}) copy-start(f32[1,1536]{1,0:T(1,128)S(1)} %collective-permute-done.1.reduced_ref) | copy-start | bytes 18436
  118.9 21.3 %all-to-all-start.5 = ((f32[32,1,128]{2,1,0:T(1,128)}), f32[32,1,128]{2,1,0:T(1,128)S(1)}, u32[]{:S(2)}, u32[]{:S(2)}) async-start(f32[32,1,128]{2,1,0:T(1,128)} %broadcast_in_dim.26), calls=%async_computation.5 | async-start | bytes 32768 | tf_op jit(solution)/shard_map/all_to_all | solution.py:329
  140.2 13.5 %all-to-all-start.4 = ((bf16[8,2,3072]{2,1,0:T(2,128)(2,1)}), bf16[8,2,3072]{2,1,0:T(2,128)(2,1)S(1)}, u32[]{:S(2)}, u32[]{:S(2)}) async-start(bf16[8,2,3072]{2,1,0:T(2,128)(2,1)} %reshape.40), calls=%async_computation.4 | async-start | bytes 196608 | tf_op jit(solution)/shard_map/all_to_all | solution.py:329
  173.5 0.7 copy-start

commit v3 on v2

v3 whole, which is shorter than its diff:
```python
import functools

import jax
import jax.numpy as jnp
from jax import lax
from jax.experimental import pallas as pl
from jax.experimental.pallas import tpu as pltpu
from jax.sharding import PartitionSpec as P

F32 = jnp.float32
BF16 = jnp.bfloat16
SHIFT = 3.0
VMEM_LIMIT = 56 * 1024 * 1024


def dequantize_slot(codes_ref, scales_ref, out_ref):
    block_rows, col_blocks = scales_ref.shape
    rows, cols = codes_ref.shape
    order = rows // block_rows
    lane_block = lax.broadcasted_iota(jnp.int32, (col_blocks, cols), 1) // (cols // col_blocks)
    own_block = lax.broadcasted_iota(jnp.int32, (col_blocks, cols), 0)
    spread = jnp.where(lane_block == own_block, 1.0, 0.0).astype(F32)
    wide = jnp.dot(
        scales_ref[...], spread, precision=lax.Precision.HIGHEST, preferred_element_type=F32
    )
    for block in range(block_rows):
        part = slice(block * order, (block + 1) * order)
        out_ref[part, :] = (codes_ref[part, :].astype(F32) * wide[block : block + 1, :]).astype(BF16)


NT = (((1,), (1,)), ((), ()))


def dot(left, right):
    return jnp.dot(left, right, preferred_element_type=F32)


def dot_t(left, right):
    return lax.dot_general(left, right, NT, preferred_element_type=F32)


def triangles(slab_ref):
    half = slab_ref.shape[0]
    mixed = slab_ref[:, :half]
    row = lax.broadcasted_iota(jnp.int32, (half, half), 0)
    col = lax.broadcasted_iota(jnp.int32, (half, half), 1)
    zero = jnp.zeros_like(mixed)
    return jnp.where(row > col, mixed, zero), jnp.where(row < col, mixed, zero)


LANES = 128


def to_tiles(values):
    count = values.shape[1] // LANES
    return jnp.concatenate(
        [values[:, part * LANES : (part + 1) * LANES] for part in range(count)], axis=0
    )


def from_tiles(tiles, rhs):
    count = tiles.shape[0] // rhs
    return jnp.concatenate(
        [tiles[part * rhs : (part + 1) * rhs, :] for part in range(count)], axis=1
    )


def row_tiles(values):
    return values.reshape(values.shape[0], values.shape[1] // LANES, LANES)


def flat_rows(tiles):
    return tiles.reshape(tiles.shape[0], tiles.shape[1] * LANES)


def share_of(values, row_index):
    tiles = row_tiles(values)
    row = lax.broadcasted_iota(jnp.int32, tiles.shape, 0)
    return jnp.sum(jnp.where(row == row_index, tiles, 0.0), axis=0)


def toward_rows(slot, offset, slab_ref, own, put, extra_ref):
    half, tile = slab_ref.shape
    rhs = own.shape[0]

    @pl.when(slot == 0)
    def _():
        extra_ref[...] = jnp.zeros_like(extra_ref)

    @pl.when(slot < offset)
    def _():
        second = dot_t(own, slab_ref[...])
        put(jnp.concatenate([second, jnp.zeros((rhs, tile - half), F32)], axis=1))

    @pl.when(slot > offset)
    def _():
        put(dot(own[:, half:], slab_ref[...]))

    @pl.when(slot == offset)
    def _():
        low, high = triangles(slab_ref)
        head, tail = own[:, :half], own[:, half:]
        extra_ref[:, :half] = dot_t(head, low) + dot_t(tail, slab_ref[:, half:])
        extra_ref[:, half:] = dot_t(tail, high)
        put(jnp.zeros((rhs, tile), F32))


def first_rows_kernel(place_ref, codes_ref, scales_ref, base_ref, slab_ref, out_ref, extra_ref):
    dequantize_slot(codes_ref, scales_ref, slab_ref)
    rhs, tile = base_ref.shape
    size = rhs * tile // LANES
    base = base_ref[...]
    share = share_of(base, place_ref[1]).astype(BF16)
    for copy in range(out_ref.shape[0]):
        out_ref[copy, 0, size:, :] = share

    def put(values):
        tiles = to_tiles(values).astype(BF16)
        for copy in range(out_ref.shape[0]):
            out_ref[copy, 0, :size, :] = tiles

    toward_rows(pl.program_id(0), place_ref[0], slab_ref, base.astype(BF16), put, extra_ref)


def second_rows_kernel(place_ref, slab_ref, own_ref, out_ref, extra_ref):
    def put(values):
        out_ref[0, :, :] = values.astype(BF16)

    toward_rows(pl.program_id(0), place_ref[0], slab_ref, own_ref[...], put, extra_ref)


def relay_kernel(received_ref, out_ref):
    senders, height, lanes = received_ref.shape
    copies, parts, width, lanes = out_ref.shape
    size = height - width
    slots = parts - 1
    rhs = size // width
    reduced = received_ref[0, :size, :].astype(F32)
    for sender in range(1, senders):
        reduced = reduced + received_ref[sender, :size, :].astype(F32)
    rows = row_tiles(from_tiles(reduced, rhs)).astype(BF16)
    for copy in range(copies):
        first = (copy % (senders // slots)) * slots
        out_ref[copy, :slots, :, :] = received_ref[first : first + slots, size:, :]
        out_ref[copy, slots, :, :] = rows[copy % rhs]


def gather_rows(place_ref, received_ref, rows_ref, tile, slots):
    rhs = rows_ref.shape[0]
    start = place_ref[5] * rhs
    for part in range(slots):
        piece = received_ref[pl.ds(start, rhs), part, :, :].astype(F32)
        rows_ref[:, part * tile : (part + 1) * tile] = flat_rows(piece).astype(BF16)


def toward_own(slot, offset, slab_ref, rows_ref, own, total_ref):
    half, tile = slab_ref.shape
    lanes = pl.multiple_of(slot * tile, tile)

    @pl.when(slot < offset)
    def _():
        total_ref[...] += dot(rows_ref[:, pl.ds(lanes, half)], slab_ref[...])

    @pl.when(slot > offset)
    def _():
        total_ref[:, half:] += dot_t(rows_ref[:, pl.ds(lanes, tile)], slab_ref[...])

    @pl.when(slot == offset)
    def _():
        low, high = triangles(slab_ref)
        head, tail = own[:, :half], own[:, half:]
        total_ref[:, :half] += dot(head, low)
        total_ref[:, half:] += dot(head, slab_ref[:, half:]) + dot(tail, high)


def first_own_kernel(
    place_ref, slab_ref, received_ref, base_ref, extra_ref, out_ref, total_ref, rows_ref
):
    slot, slots = pl.program_id(0), rows_ref.shape[1] // base_ref.shape[1]
    rhs, tile = base_ref.shape

    @pl.when(slot == 0)
    def _():
        total_ref[...] = extra_ref[...]
        gather_rows(place_ref, received_ref, rows_ref, tile, slots)

    toward_own(slot, place_ref[0], slab_ref, rows_ref, base_ref[...].astype(BF16), total_ref)

    @pl.when(slot == slots - 1)
    def _():
        size = rhs * tile // LANES
        source = place_ref[6]
        planes = received_ref.shape[0] // rhs
        reduced = received_ref[source, slots, :, :].astype(F32)
        for plane in range(1, planes):
            reduced = reduced + received_ref[plane * rhs + source, slots, :, :].astype(F32)
        reduced = reduced.astype(BF16)
        tiles = to_tiles(total_ref[...]).astype(BF16)
        for copy in range(out_ref.shape[0]):
            out_ref[copy, :size, :] = tiles
            out_ref[copy, size:, :] = reduced


def combine_kernel(place_ref, received_ref, base_ref, shifted_ref, mid_ref, own_ref, out_ref):
    rhs, tile = base_ref.shape
    size = rhs * tile // LANES
    total = received_ref[0, :size, :].astype(F32)
    for sender in range(1, received_ref.shape[0]):
        total = total + received_ref[sender, :size, :].astype(F32)
    others = flat_rows(received_ref[:, size:, :].astype(F32))
    mid = (from_tiles(total, rhs) + others) + shifted_ref[...] * base_ref[...]
    mid_ref[...] = mid
    own_ref[...] = mid.astype(BF16)
    share = share_of(mid, place_ref[1]).astype(BF16)
    for copy in range(out_ref.shape[0]):
        out_ref[copy, :, :] = share


def three_parts(values):
    first = values.astype(BF16).astype(F32)
    rest = values - first
    second = rest.astype(BF16).astype(F32)
    return first, second, rest - second


def second_own_kernel(
    place_ref, slab_ref, received_ref, own_ref, extra_ref, sent_ref, grams_ref,
    out_ref, total_ref, rows_ref, sums_ref,
):
    slot = pl.program_id(0)
    rhs, tile = own_ref.shape
    slots = rows_ref.shape[1] // tile

    @pl.when(slot == 0)
    def _():
        total_ref[...] = extra_ref[...]
        gather_rows(place_ref, received_ref, rows_ref, tile, slots)

    toward_own(slot, place_ref[0], slab_ref, rows_ref, own_ref[...], total_ref)

    @pl.when(slot == slots - 1)
    def _():
        blank = jnp.zeros((rhs, out_ref.shape[2] * LANES - tile), F32)
        pair = dot_t(extra_ref[...].astype(BF16), own_ref[...])
        for part in range(slots):
            pair = pair + dot_t(sent_ref[part], rows_ref[:, part * tile : (part + 1) * tile])
            piece = jnp.concatenate([sent_ref[part].astype(F32), blank], axis=1)
            piece = row_tiles(piece).astype(BF16)
            for first in range(0, out_ref.shape[0], rhs):
                out_ref[first : first + rhs, part, :, :] = piece
        sums_ref[...] = grams_ref[...]
        sums_ref[:, :rhs] = pair
        pieces = [total_ref[...], *three_parts(sums_ref[...])]
        pieces.append(blank[:, (len(pieces) - 1) * LANES :])
        piece = row_tiles(jnp.concatenate(pieces, axis=1)).astype(BF16)
        for first in range(0, out_ref.shape[0], rhs):
            out_ref[first : first + rhs, slots, :, :] = piece


def joined(values, width):
    return (values[width : width + 1] + values[width + 1 : width + 2]) + values[width + 2 : width + 3]


def reduce_kernel(width, place_ref, received_ref, out_ref):
    senders, parts, height, lanes = received_ref.shape
    slots = parts - 1
    plane, own_place = place_ref[2], place_ref[4]
    count = out_ref.shape[0]
    planes = count // (slots * slots) * 2
    rhs = senders // planes
    row = lax.broadcasted_iota(jnp.int32, (height, lanes), 0)

    def take(sender, part):
        return received_ref[sender, part, :, :].astype(F32)

    own = take(plane * rhs, slots)
    rest = take((planes - 1 - plane) * rhs, slots)
    for sender in range(1, rhs):
        own = own + take(plane * rhs + sender, slots)
        rest = rest + take((planes - 1 - plane) * rhs + sender, slots)
    first, second, third = three_parts(joined(own + rest, width))
    grams = jnp.where(
        row == width, first, jnp.where(row == width + 1, second, jnp.where(row == width + 2, third, 0.0))
    )
    for target in range(count):
        sender = plane * (rhs // planes) + target // slots
        value = take(sender, target % slots) + take(rhs + sender, target % slots)
        value = value + jnp.where(own_place == target, own, 0.0)
        out_ref[target, :, :] = jnp.where(row < width, value, grams).astype(BF16)


def finish_reduce_kernel(width, received_ref, out_ref):
    total = received_ref[0, :, :].astype(F32)
    for sender in range(1, received_ref.shape[0]):
        total = total + received_ref[sender, :, :].astype(F32)
    row = lax.broadcasted_iota(jnp.int32, total.shape, 0)
    value = jnp.where(row < width, total, jnp.broadcast_to(joined(total, width), total.shape))
    for copy in range(out_ref.shape[0]):
        out_ref[copy, :, :] = value


def whole(shape):
    return pl.BlockSpec(shape, lambda slot: (0,) * len(shape))


SMEM = pl.BlockSpec(memory_space=pltpu.SMEM)
PARAMS = pltpu.CompilerParams(vmem_limit_bytes=VMEM_LIMIT)


def struct(shape, dtype):
    return jax.ShapeDtypeStruct(shape, dtype)


def plain(kernel, outs, name, *operands, scalars=True):
    specs = [pl.BlockSpec(memory_space=pltpu.VMEM)] * len(operands)
    if scalars:
        specs[0] = SMEM
    return pl.pallas_call(
        kernel, in_specs=specs, out_shape=outs, compiler_params=PARAMS, name=name
    )(*operands)


def slab_spec(codes, slots):
    return pl.BlockSpec((codes.shape[0] // slots, codes.shape[1]), lambda slot: (slot, 0))


def times(left, right):
    total = left[:, 0:1] * right[0:1, :]
    for index in range(1, left.shape[1]):
        total = total + left[:, index : index + 1] * right[index : index + 1, :]
    return total


def inverses(matrices):
    size = matrices[0].shape[0]
    row = lax.broadcasted_iota(jnp.int32, (size, size), 0)
    col = lax.broadcasted_iota(jnp.int32, (size, size), 1)
    eye = jnp.where(row == col, 1.0, 0.0).astype(F32)
    work = [(matrix, eye) for matrix in matrices]
    for step in range(size):
        here = row == step
        following = []
        for left, right in work:
            scale = 1.0 / left[step : step + 1, step : step + 1]
            left_row = left[step : step + 1, :] * scale
            right_row = right[step : step + 1, :] * scale
            column = left[:, step : step + 1]
            following.append(
                (
                    jnp.where(here, left_row, left - column * left_row),
                    jnp.where(here, right_row, right - column * right_row),
                )
            )
        work = following
    return [right for left, right in work], eye


def final_kernel(
    received_ref, base_ref, mid_ref, shifted_ref, solution_ref, residual_ref
):
    rhs, tile = base_ref.shape
    received = flat_rows(received_ref[...])
    gram = received[:, tile : tile + LANES]
    half_wy, bb, yb, yy, wy = (gram[:, index * rhs : (index + 1) * rhs] for index in range(5))
    wy = wy + (half_wy + half_wy.T)
    curvature = yb + SHIFT * bb
    (inverse_curvature, inverse_bb), eye = inverses([curvature, bb])
    step_t = times(bb, inverse_curvature)
    step = times(inverse_curvature, bb)
    a1, a1_t = eye - SHIFT * step_t, eye - SHIFT * step
    b1, b1_t = -step_t, -step

    def inner(a, a_t, b, b_t, first, cross, last):
        return times(times(a, first) + times(b, cross), a_t) + times(
            times(a, cross) + times(b, last), b_t
        )

    next_gram = inner(a1, a1_t, b1, b1_t, bb, yb, yy)
    a2 = a1 + times(next_gram, inverse_bb)
    a2_t = a1_t + times(inverse_bb, next_gram)
    curvature = inner(a2, a2_t, b1, b1_t, yb + SHIFT * bb, yy + SHIFT * yb, wy + SHIFT * yy)
    (inverse_curvature,), eye = inverses([curvature])
    last_t = times(next_gram, inverse_curvature)
    base, mid = base_ref[...], mid_ref[...]
    top = received[:, :tile] + shifted_ref[...] * mid
    from_mid = times(last_t, b1)
    from_base = times(last_t, a2)
    solution_ref[...] = times(step_t + from_base, base) + times(from_mid, mid)
    residual_ref[...] = (
        times(a1 - SHIFT * from_base, base)
        + times(b1 - from_base - SHIFT * from_mid, mid)
        - times(from_mid, top)
    )


def local(kernel_codes, tile_scales, kernel_diagonal, noise_variance, targets):
    rhs, tile = targets.shape
    slots = kernel_codes.shape[0] // (tile // 2)
    width = tile // LANES
    size = rhs * width
    row_count = lax.axis_size("row")
    col_count = lax.axis_size("col")
    side = slots * slots
    planes = col_count // side
    row_index = lax.axis_index("row")
    col_index = lax.axis_index("col")
    plane, spot = col_index // side, col_index % side
    place = jnp.stack(
        [
            col_index - row_index * slots,
            row_index,
            plane,
            spot // slots,
            spot,
            row_index // (row_count // planes),
            plane * (row_count // planes) + spot // slots,
        ]
    ).astype(jnp.int32)
    near = [[first * side + index for index in range(side)] for first in range(planes)]
    deep = [
        [row * col_count + first * side + index for first in range(planes) for row in range(row_count)]
        for index in range(side)
    ]
    deep_count = planes * row_count
    shifted = (lax.reduce_precision(kernel_diagonal, 8, 7) + (noise_variance - SHIFT))[None, :]

    def exchange_near(values):
        return lax.all_to_all(values, "col", 0, 0, axis_index_groups=near)

    def exchange_deep(values):
        return lax.all_to_all(values, ("row", "col"), 0, 0, axis_index_groups=deep)

    def exchange_row(values):
        return lax.all_to_all(values, "row", 0, 0)

    slab = slab_spec(kernel_codes, slots)
    vector = whole((rhs, tile))
    scale_block = (tile_scales.shape[0] // slots, tile_scales.shape[1])
    slabs, outgoing, extra = pl.pallas_call(
        first_rows_kernel,
        grid=(slots,),
        in_specs=[SMEM, slab, pl.BlockSpec(scale_block, lambda slot: (slot, 0)), vector],
        out_specs=[
            slab,
            pl.BlockSpec((slots, 1, size + width, LANES), lambda slot: (0, slot, 0, 0)),
            vector,
        ],
        out_shape=[
            struct(kernel_codes.shape, BF16),
            struct((slots, slots, size + width, LANES), BF16),
            struct((rhs, tile), F32),
        ],
        compiler_params=PARAMS,
        name="first_rows",
    )(place, kernel_codes, tile_scales, targets)
    received = exchange_near(outgoing.reshape(side, size + width, LANES))
    relayed = plain(
        relay_kernel,
        struct((deep_count, slots + 1, width, LANES), BF16),
        "relay",
        received,
        scalars=False,
    )
    received = exchange_deep(relayed)
    message = pl.pallas_call(
        first_own_kernel,
        grid=(slots,),
        in_specs=[SMEM, slab, whole(received.shape), vector, vector],
        out_specs=whole((row_count, size + width, LANES)),
        out_shape=struct((row_count, size + width, LANES), BF16),
        scratch_shapes=[pltpu.VMEM((rhs, tile), F32), pltpu.VMEM((rhs, slots * tile), BF16)],
        compiler_params=PARAMS,
        name="first_own",
    )(place, slabs, received, targets, extra)
    received = exchange_row(message)
    mid, own, outgoing = plain(
        combine_kernel,
        [struct((rhs, tile), F32), struct((rhs, tile), BF16), struct((side, width, LANES), BF16)],
        "combine",
        place,
        received,
        targets,
        shifted,
    )
    received = exchange_near(outgoing)
    sent, extra = pl.pallas_call(
        second_rows_kernel,
        grid=(slots,),
        in_specs=[SMEM, slab, vector],
        out_specs=[pl.BlockSpec((1, rhs, tile), lambda slot: (slot, 0, 0)), vector],
        out_shape=[struct((slots, rhs, tile), BF16), struct((rhs, tile), F32)],
        compiler_params=PARAMS,
        name="second_rows",
    )(place, slabs, own)
    on_mid = jnp.dot(
        jnp.concatenate([mid, shifted * mid]), mid.T, precision=lax.Precision.HIGHEST
    )
    on_base = jnp.dot(
        jnp.concatenate([targets, mid]), targets.T, precision=lax.Precision.HIGHEST
    )
    grams = jnp.concatenate(
        [jnp.zeros((rhs, rhs), F32), on_base[:rhs], on_base[rhs:], on_mid[:rhs], on_mid[rhs:]], axis=1
    )
    grams = jnp.pad(grams * (1.0 / row_count), ((0, 0), (0, LANES - 5 * rhs)))
    relayed = jnp.broadcast_to(
        received.reshape(1, slots, slots, width, LANES),
        (deep_count // slots, slots, slots, width, LANES),
    ).reshape(deep_count, slots, width, LANES)
    received = exchange_deep(relayed)
    height = width + 4
    outgoing = pl.pallas_call(
        second_own_kernel,
        grid=(slots,),
        in_specs=[
            SMEM,
            slab,
            whole(received.shape),
            vector,
            vector,
            whole(sent.shape),
            whole(grams.shape),
        ],
        out_specs=whole((deep_count, slots + 1, height, LANES)),
        out_shape=struct((deep_count, slots + 1, height, LANES), BF16),
        scratch_shapes=[
            pltpu.VMEM((rhs, tile), F32),
            pltpu.VMEM((rhs, slots * tile), BF16),
            pltpu.VMEM((rhs, LANES), F32),
        ],
        compiler_params=PARAMS,
        name="second_own",
    )(place, slabs, received, own, extra, sent, grams)
    received = exchange_deep(outgoing)
    outgoing = plain(
        functools.partial(reduce_kernel, width),
        struct((side, height, LANES), BF16),
        "reduce_planes",
        place,
        received,
    )
    received = exchange_near(outgoing)
    outgoing = plain(
        functools.partial(finish_reduce_kernel, width),
        struct((row_count, height, LANES), F32),
        "reduce_tiles",
        received,
        scalars=False,
    )
    received = exchange_row(outgoing)
    return tuple(
        plain(
            final_kernel,
            [struct((rhs, tile), F32)] * 2,
            "small_solves",
            received,
            targets,
            mid,
            shifted,
            scalars=False,
        )
    )


def solution(mesh):
    in_specs = (P("row", "col"), P("row", "col"), P("col"), P("col"), P(None, "col"))
    out_specs = (P(None, "col"), P(None, "col"))
    return jax.shard_map(local, mesh=mesh, in_specs=in_specs, out_specs=out_specs, check_vma=False)
```

time: 179 us -> 159 us (0.89)
  blocking collectives: 36.7 us -> 79 us
  starting transfers between devices: 47.7 us -> 12.4 us
  waiting for transfers between devices: 35.8 us -> 17.3 us
  other arithmetic: 12.7 us -> 0.82 us
  Pallas kernels: 32.6 us -> 39.8 us
  local copies, waits for them, and re-layouts: 10.7 us -> 5.56 us
    all_to_all x2 -> x5, blocking collectives: 36.7 us -> 79 us  [the longest x2 40.6 us: exchange_deep(): return lax.all_to_all(values, ('row', 'col'), 0, 0, axis_index_groups=deep)]
    all_to_all x5 -> x3, starting transfers between devices: 40.2 us -> 12.4 us  [the longest x1 5.53 us: exchange_deep(): return lax.all_to_all(values, ('row', 'col'), 0, 0, axis_index_groups=deep)]
    all_to_all x5 -> x3, waiting for transfers between devices: 35.6 us -> 17.3 us  [the longest x1 6.89 us: exchange_row(): return lax.all_to_all(values, 'row', 0, 0)]
    all_to_all x7 -> x0, other arithmetic: 9.01 us -> none  [exchange(): return lax.all_to_all(values, axis, 0, 0)]
    ppermute x2 -> x0, starting transfers between devices: 7.53 us -> none  [bring(): reduced = lax.ppermute(reduced, ('row', 'col'), moves)]
    pallas_call x5 -> x9, Pallas kernels: 32.6 us -> 39.8 us  [the longest x5 10.4 us: plain(): pl.pallas_call(kernel, in_specs=specs, out_shape=outs, compiler_params=PA...]
    unnamed x31 -> x9, local copies, waits for them, and re-layouts: 8.54 us -> 2.16 us
  transfers between devices with their start and end apart: 7 -> 3, of which waited for: 6 -> 3; matrix products, arithmetic and copies ran while one was open for 2% -> 1% of each run, Pallas kernels for 0% -> 4%
where the time goes in v3:
time: 159 us; the launch traced here: 158 us
  blocking collectives  79 us (50%)
  Pallas kernels  39.8 us (25%)
  waiting for transfers between devices  17.3 us (11%)
  starting transfers between devices  12.4 us (8%)
  local copies, waits for them, and re-layouts  5.56 us (3%)
  matrix products  2.11 us (1%)
    all_to_all x2, blocking collectives, exchange_deep(): return lax.all_to_all(values, ('row', 'col'), 0, 0, axis_index_groups=deep)  40.6 us
    all_to_all x2, blocking collectives, exchange_near(): return lax.all_to_all(values, 'col', 0, 0, axis_index_groups=near)  28.9 us
    pallas_call x5, Pallas kernels, plain(): pl.pallas_call(kernel, in_specs=specs, out_shape=outs, compiler_params=PA...  10.4 us
    pallas_call x1, Pallas kernels, local(): pl.pallas_call(first_rows_kernel, grid=(slots,), in_specs=[SMEM, slab, pl...  10.2 us
    all_to_all x1, blocking collectives, exchange_row(): return lax.all_to_all(values, 'row', 0, 0)  9.48 us
    all_to_all x1, waiting for transfers between devices, exchange_row(): return lax.all_to_all(values, 'row', 0, 0)  6.89 us
    pallas_call x1, Pallas kernels, local(): pl.pallas_call(second_own_kernel, grid=(slots,), in_specs=[SMEM, slab, wh...  6.84 us
    pallas_call x1, Pallas kernels, local(): pl.pallas_call(first_own_kernel, grid=(slots,), in_specs=[SMEM, slab, who...  6.57 us
  transfers between devices with their start and end apart: 3, of which 3 were waited for; matrix products, arithmetic and copies ran while one was open for 1% of the time, Pallas kernels for 4%

profile of v3, /device:TPU:1, one launch (start us, length us, event | category | flops | bytes accessed | tf_op | source)
XLA Modules:
  0.0 157.8 jit_solution(3054322931606808264)
XLA Ops:
  0.7 1.4 copy.12.scales_ref
  2.1 0.6 stack.31.place_ref
  2.7 0.0 copy-start.2
  2.7 0.0 copy-start.3
  2.7 0.0 copy-start
  2.7 10.2 %first_rows.1 = (bf16[3072,1536]{1,0:T(8,128)(2,1)}, bf16[4,4,108,128]{3,2,1,0:T(8,128)(2,1)}, f32[8,1536]{1,0:T(8,128)}) custom-call(s32[7]{0:T(128)} %stack.31.place_ref, bf16[3072,1536]{1,0:T(8,128)(2,1)} %codes_ref.1, f32[96,48]{1,0:T(8,128)} %copy.12.scales_ref, f32[8,1536]{1,0:T(8,128)} %base_ref.7), custom_call_target="tpu_custom_call" | custom-call | tf_op jit(solution)/shard_map/first_rows/pallas_call | solution.py:439
  13.0 17.9 %all_to_all.40.received_ref = bf16[16,108,128]{2,1,0:T(8,128)(2,1)} all-to-all(bf16[16,108,128]{2,1,0:T(8,128)(2,1)} %bitcast.12), channel_id=1, replica_groups={{0,1,2,3,4,5,6,7,8,9,10,11,12,13,14,15},{16,17,18,19,20,21,22,23,24,25,..., dimensions={0} | all-to-all | bytes 884736 | tf_op jit(solution)/shard_map/all_to_all | solution.py:428
  30.8 1.8 %relay.1 = bf16[16,5,12,128]{3,2,1,0:T(8,128)(2,1)} custom-call(bf16[16,108,128]{2,1,0:T(8,128)(2,1)} %all_to_all.40.received_ref), custom_call_target="tpu_custom_call" | custom-call | tf_op jit(solution)/shard_map/relay/pallas_call | solution.py:318
  32.7 23.8 %all_to_all.41.received_ref = bf16[16,5,12,128]{3,2,1,0:T(8,128)(2,1)} all-to-all(bf16[16,5,12,128]{3,2,1,0:T(8,128)(2,1)} %relay.1), channel_id=1, replica_groups={{0,32,64,96,128,160,192,224,16,48,80,112,144,176,208,240},{1,33,65,97,1..., dimensions={0} | all-to-all | bytes 491520 | tf_op jit(solution)/shard_map/all_to_all | solution.py:431
  56.5 6.6 %first_own.1 = bf16[8,108,128]{2,1,0:T(8,128)(2,1)} custom-call(s32[7]{0:T(128)} %stack.31.place_ref, bf16[3072,1536]{1,0:T(8,128)(2,1)} %get-tuple-element.10.slab_ref, bf16[16,5,12,128]{3,2,1,0:T(8,128)(2,1)} %all_to_all.41.received_ref, f32[8,1536]{1,0:T(8,128)} %base_ref.7, f32[8,1536]{1,0:T(8,128)} %get-tuple-element.12.extra_ref), custom_call_target="tpu_custom_call" | custom-call | tf_op jit(solution)/shard_map/first_own/pallas_call | solution.py:465
  63.1 3.4 %all-to-all-start.2 = ((bf16[8,108,128]{2,1,0:T(8,128)(2,1)}), bf16[8,108,128]{2,1,0:T(8,128)(2,1)S(1)}, u32[]{:S(2)}, u32[]{:S(2)}) async-start(bf16[8,108,128]{2,1,0:T(8,128)(2,1)} %first_own.1), calls=%async_computation.2 | async-start | bytes 458752 | tf_op jit(solution)/shard_map/all_to_all | solution.py:434
  66.4 0.0 copy-done.2
  66.4 0.0 copy-done.3
  66.5 0.6 broadcast_in_dim.13.shifted_ref
  67.0 6.9 %all-to-all-done.2.received_ref = bf16[8,108,128]{2,1,0:T(8,128)(2,1)S(1)} async-done(((bf16[8,108,128]{2,1,0:T(8,128)(2,1)}), bf16[8,108,128]{2,1,0:T(8,128)(2,1)S(1)}, u32[]{:S(2)}, u32[]{:S(2)}) %all-to-all-start.2) | async-done | bytes 221216 | tf_op jit(solution)/shard_map/all_to_all | solution.py:434
  73.9 0.0 copy-start.1
  73.9 0.7 copy-done.1
  74.6 1.7 %combine.1 = (f32[8,1536]{1,0:T(8,128)}, bf16[8,1536]{1,0:T(8,128)(2,1)}, bf16[16,12,128]{2,1,0:T(8,128)(2,1)}) custom-call(s32[7]{0:T(128)} %stack.31.place_ref, bf16[8,108,128]{2,1,0:T(8,128)(2,1)} %copy-done.1, f32[8,1536]{1,0:T(8,128)} %base_ref.7, f32[1,1536]{1,0:T(1,128)} %broadcast_in_dim.13.shifted_ref), custom_call_target="tpu_custom_call" | custom-call | tf_op jit(solution)/shard_map/combine/pallas_call | solution.py:318
  76.3 0.8 broadcast_multiply_fusion
  77.1 0.0 copy-done
  77.1 1.0 fusion
  78.1 1.1 fusion.4
  79.2 3.5 %all-to-all-start.3 = ((bf16[16,12,128]{2,1,0:T(8,128)(2,1)}), bf16[16,12,128]{2,1,0:T(8,128)(2,1)S(1)}, u32[]{:S(2)}, u32[]{:S(2)}) async-start(bf16[16,12,128]{2,1,0:T(8,128)(2,1)} %get-tuple-element.13), calls=%async_computation.3 | async-start | bytes 131072 | tf_op jit(solution)/shard_map/all_to_all | solution.py:428
  82.8 6.4 %all-to-all-done.3 = bf16[16,12,128]{2,1,0:T(8,128)(2,1)S(1)} async-done(((bf16[16,12,128]{2,1,0:T(8,128)(2,1)}), bf16[16,12,128]{2,1,0:T(8,128)(2,1)S(1)}, u32[]{:S(2)}, u32[]{:S(2)}) %all-to-all-start.3) | async-done | bytes 49184 | tf_op jit(solution)/shard_map/all_to_all | solution.py:428
  89.3 0.7 broadcast_in_dim.15
  90.0 5.5 %all-to-all-start.4 = ((bf16[16,4,12,128]{3,1,2,0:T(4,128)(2,1)}), bf16[16,4,12,128]{3,1,2,0:T(4,128)(2,1)S(1)}, u32[]{:S(2)}, u32[]{:S(2)}) async-start(bf16[16,4,12,128]{3,1,2,0:T(4,128)(2,1)} %bitcast.9), calls=%async_computation.4 | async-start | bytes 393216 | tf_op jit(solution)/shard_map/all_to_all | solution.py:431
  95.6 0.1 concatenate.11
  95.7 0.6 pad.4.grams_ref
  96.3 5.7 %second_rows.1 = (bf16[4,8,1536]{2,1,0:T(8,128)(2,1)}, f32[8,1536]{1,0:T(8,128)}) custom-call(s32[7]{0:T(128)} %stack.31.place_ref, bf16[3072,1536]{1,0:T(8,128)(2,1)} %get-tuple-element.10.slab_ref, bf16[8,1536]{1,0:T(8,128)(2,1)} %get-tuple-element.14.own_ref), custom_call_target="tpu_custom_call" | custom-call | tf_op jit(solution)/shard_map/second_rows/pallas_call | solution.py:486
  102.0 3.9 %all-to-all-done.4 = bf16[16,4,12,128]{3,1,2,0:T(4,128)(2,1)S(1)} async-done(((bf16[16,4,12,128]{3,1,2,0:T(4,128)(2,1)}), bf16[16,4,12,128]{3,1,2,0:T(4,128)(2,1)S(1)}, u32[]{:S(2)}, u32[]{:S(2)}) %all-to-all-start.4) | async-done | bytes 196640 | tf_op jit(solution)/shard_map/all_to_all | solution.py:431
  105.9 0.8 copy.18.received_ref
  106.7 6.8 %second_own.1 = bf16[16,5,16,128]{3,2,1,0:T(8,128)(2,1)} custom-call(s32[7]{0:T(128)} %stack.31.place_ref, bf16[3072,1536]{1,0:T(8,128)(2,1)} %get-tuple-element.10.slab_ref, bf16[16,4,12,128]{3,2,1,0:T(8,128)(2,1)} %copy.18.received_ref, bf16[8,1536]{1,0:T(8,128)(2,1)} %get-tuple-element.14.own_ref, f32[8,1536]{1,0:T(8,128)} %get-tuple-element.15.extra_ref, ...), custom_call_target="tpu_custom_call" | custom-call | tf_op jit(solution)/shard_map/second_own/pallas_call | solution.py:511
  113.5 16.8 %all_to_all.42.received_ref = bf16[16,5,16,128]{3,2,1,0:T(8,128)(2,1)} all-to-all(bf16[16,5,16,128]{3,2,1,0:T(8,128)(2,1)} %second_own.1), channel_id=1, replica_groups={{0,32,64,96,128,160,192,224,16,48,80,112,144,176,208,240},{1,33,65,97,1..., dimensions={0} | all-to-all | bytes 655360 | tf_op jit(solution)/shard_map/all_to_all | solution.py:431
  130.4 1.6 %reduce_planes.1 = bf16[16,16,128]{2,1,0:T(8,128)(2,1)} custom-call(s32[7]{0:T(128)} %stack.31.place_ref, bf16[16,5,16,128]{3,2,1,0:T(8,128)(2,1)} %all_to_all.42.received_ref), custom_call_target="tpu_custom_call" | custom-call | tf_op jit(solution)/shard_map/reduce_planes/pallas_call | solution.py:318
  132.0 11.0 %all_to_all.43.received_ref = bf16[16,16,128]{2,1,0:T(8,128)(2,1)} all-to-all(bf16[16,16,128]{2,1,0:T(8,128)(2,1)} %reduce_planes.1), channel_id=1, replica_groups={{0,1,2,3,4,5,6,7,8,9,10,11,12,13,14,15},{16,17,18,19,20,21,22,23,24,25,..., dimensions={0} | all-to-all | bytes 131072 | tf_op jit(solution)/shard_map/all_to_all | solution.py:428
  143.0 1.5 reduce_tiles.1
  144.5 9.5 %all_to_all.44.received_ref = f32[8,16,128]{2,1,0:T(8,128)} all-to-all(f32[8,16,128]{2,1,0:T(8,128)} %reduce_tiles.1), channel_id=1, replica_groups=mesh['row'=8,'col'=32] {'row'}, dimensions={0} | all-to-all | bytes 131072 | tf_op jit(solution)/shard_map/all_to_all | solution.py:434
  154.0 3.8 %small_solves.1 = (f32[8,1536]{1,0:T(8,128)}, f32[8,1536]{1,0:T(8,128)}) custom-call(f32[8,16,128]{2,1,0:T(8,128)} %all_to_all.44.received_ref, f32[8,1536]{1,0:T(8,128)} %base_ref.7, f32[8,1536]{1,0:T(8,128)} %get-tuple-element.17.mid_ref, f32[1,1536]{1,0:T(1,128)} %broadcast_in_dim.13.shifted_ref), custom_call_target="tpu_custom_call" | custom-call | tf_op jit(solution)/shard_map/small_solves/pallas_call | solution.py:318
  (6 shorter events, 0.0 us)
Async XLA Ops:
  2.7 63.7 %copy-start.2 = (f32[1536]{0:T(1024)S(1)}, f32[1536]{0:T(1024)}, u32[]{:S(2)}) copy-start(f32[1536]{0:T(1024)} %param.8) | copy-start | bytes 18436
  2.7 63.7 %copy-start.3 = (f32[1536]{0:T(1024)S(1)}, f32[1536]{0:T(1024)}, u32[]{:S(2)}) copy-start(f32[1536]{0:T(1024)} %param.7) | copy-start | bytes 18436
  2.7 74.4 %copy-start = (f32[8,1536]{1,0:T(8,128)S(1)}, f32[8,1536]{1,0:T(8,128)}, u32[]{:S(2)}) copy-start(f32[8,1536]{1,0:T(8,128)} %base_ref.7) | copy-start | bytes 147460
  63.1 10.9 %all-to-all-start.2 = ((bf16[8,108,128]{2,1,0:T(8,128)(2,1)}), bf16[8,108,128]{2,1,0:T(8,128)(2,1)S(1)}, u32[]{:S(2)}, u32[]{:S(2)}) async-start(bf16[8,108,128]{2,1,0:T(8,128)(2,1)} %first_own.1), calls=%async_computation.2 | async-start | bytes 458752 | tf_op jit(solution)/shard_map/all_to_all | solution.py:434
  73.9 0.7 copy-start.1
  79.2 10.0 %all-to-all-start.3 = ((bf16[16,12,128]{2,1,0:T(8,128)(2,1)}), bf16[16,12,128]{2,1,0:T(8,128)(2,1)S(1)}, u32[]{:S(2)}, u32[]{:S(2)}) async-start(bf16[16,12,128]{2,1,0:T(8,128)(2,1)} %get-tuple-element.13), calls=%async_computation.3 | async-start | bytes 131072 | tf_op jit(solution)/shard_map/all_to_all | solution.py:428
  90.0 15.9 %all-to-all-start.4 = ((bf16[16,4,12,128]{3,1,2,0:T(4,128)(2,1)}), bf16[16,4,12,128]{3,1,2,0:T(4,128)(2,1)S(1)}, u32[]{:S(2)}, u32[]{:S(2)}) async-start(bf16[16,4,12,128]{3,1,2,0:T(4,128)(2,1)} %bitcast.9), calls=%async_computation.4 | async-start | bytes 393216 | tf_op jit(solution)/shard_map/all_to_all | solution.py:431

commit v4 on v3

--- a/solution.py
+++ b/solution.py
@@ -13,16 +13,27 @@
 VMEM_LIMIT = 56 * 1024 * 1024
 
 
-def dequantize_slot(codes_ref, scales_ref, out_ref):
-    block_rows, col_blocks = scales_ref.shape
-    rows, cols = codes_ref.shape
-    order = rows // block_rows
+def spread_scales(scales_ref, wide_ref):
+    col_blocks = scales_ref.shape[0]
+    cols = wide_ref.shape[1]
     lane_block = lax.broadcasted_iota(jnp.int32, (col_blocks, cols), 1) // (cols // col_blocks)
     own_block = lax.broadcasted_iota(jnp.int32, (col_blocks, cols), 0)
     spread = jnp.where(lane_block == own_block, 1.0, 0.0).astype(F32)
-    wide = jnp.dot(
-        scales_ref[...], spread, precision=lax.Precision.HIGHEST, preferred_element_type=F32
-    )
+    wide_ref[...] = lax.dot_general(
+        scales_ref[...],
+        spread,
+        (((0,), (0,)), ((), ())),
+        precision=lax.Precision.HIGHEST,
+        preferred_element_type=F32,
+    )
+
+
+def dequantize_slot(slot, codes_ref, wide_ref, out_ref):
+    rows = codes_ref.shape[0]
+    block_rows = wide_ref.shape[0] // pl.num_programs(0)
+    order = rows // block_rows
+    start = pl.multiple_of(slot * block_rows, 8)
+    wide = wide_ref[pl.ds(start, block_rows), :]
     for block in range(block_rows):
         part = slice(block * order, (block + 1) * order)
         out_ref[part, :] = (codes_ref[part, :].astype(F32) * wide[block : block + 1, :]).astype(BF16)
@@ -105,8 +116,14 @@
         put(jnp.zeros((rhs, tile), F32))
 
 
-def first_rows_kernel(place_ref, codes_ref, scales_ref, base_ref, slab_ref, out_ref, extra_ref):
-    dequantize_slot(codes_ref, scales_ref, slab_ref)
+def first_rows_kernel(
+    place_ref, codes_ref, scales_ref, base_ref, slab_ref, out_ref, extra_ref, wide_ref
+):
+    @pl.when(pl.program_id(0) == 0)
+    def _():
+        spread_scales(scales_ref, wide_ref)
+
+    dequantize_slot(pl.program_id(0), codes_ref, wide_ref, slab_ref)
     rhs, tile = base_ref.shape
     size = rhs * tile // LANES
     base = base_ref[...]
@@ -122,7 +139,26 @@
     toward_rows(pl.program_id(0), place_ref[0], slab_ref, base.astype(BF16), put, extra_ref)
 
 
-def second_rows_kernel(place_ref, slab_ref, own_ref, out_ref, extra_ref):
+def second_rows_kernel(
+    copies, place_ref, slab_ref, own_ref, base_ref, mid_ref, shifted_ref, out_ref, extra_ref, sums_ref
+):
+    rhs = own_ref.shape[0]
+
+    @pl.when(pl.program_id(0) == 0)
+    def _():
+        base, mid = base_ref[...], mid_ref[...]
+        exact = functools.partial(
+            lax.dot_general,
+            dimension_numbers=NT,
+            precision=lax.Precision.HIGHEST,
+            preferred_element_type=F32,
+        )
+        on_base = exact(jnp.concatenate([base, mid]), base)
+        on_mid = exact(jnp.concatenate([mid, shifted_ref[...] * mid]), mid)
+        sums_ref[...] = jnp.zeros_like(sums_ref)
+        for part, value in enumerate((on_base[:rhs], on_base[rhs:], on_mid[:rhs], on_mid[rhs:])):
+            sums_ref[:, (part + 1) * rhs : (part + 2) * rhs] = value * (1.0 / copies)
+
     def put(values):
         out_ref[0, :, :] = values.astype(BF16)
 
@@ -223,80 +259,72 @@
     return first, second, rest - second
 
 
-def second_own_kernel(
-    place_ref, slab_ref, received_ref, own_ref, extra_ref, sent_ref, grams_ref,
-    out_ref, total_ref, rows_ref, sums_ref,
+def pack_sums(values, used):
+    parts = [part[:, :used] for part in three_parts(values)]
+    blank = jnp.zeros((values.shape[0], LANES - 3 * used), F32)
+    return jnp.concatenate(parts + [blank], axis=1).astype(BF16)
+
+
+def unpack_sums(values, used):
+    return (values[:, :used] + values[:, used : 2 * used]) + values[:, 2 * used : 3 * used]
+
+
+def pair_kernel(
+    place_ref, received_ref, own_ref, extra_ref, sent_ref, grams_ref, out_ref, rows_ref, sums_ref
 ):
+    rhs, tile = own_ref.shape
+    slots = sent_ref.shape[0]
+    size = rhs * tile // LANES
+    gather_rows(place_ref, received_ref, rows_ref, tile, slots)
+    pair = dot_t(extra_ref[...].astype(BF16), own_ref[...])
+    for part in range(slots):
+        pair = pair + dot_t(sent_ref[part], rows_ref[:, part * tile : (part + 1) * tile])
+    sums_ref[...] = grams_ref[...]
+    sums_ref[:, :rhs] = pair
+    packed = pack_sums(sums_ref[...], 5 * rhs)
+    for target in range(out_ref.shape[0]):
+        out_ref[target, size:, :] = packed
+    for part in range(slots):
+        tiles = to_tiles(sent_ref[part].astype(F32)).astype(BF16)
+        for target in range(part, out_ref.shape[0], slots):
+            out_ref[target, :size, :] = tiles
+
+
+def second_own_kernel(place_ref, slab_ref, rows_ref, own_ref, extra_ref, out_ref, total_ref):
     slot = pl.program_id(0)
-    rhs, tile = own_ref.shape
-    slots = rows_ref.shape[1] // tile
 
     @pl.when(slot == 0)
     def _():
         total_ref[...] = extra_ref[...]
-        gather_rows(place_ref, received_ref, rows_ref, tile, slots)
 
     toward_own(slot, place_ref[0], slab_ref, rows_ref, own_ref[...], total_ref)
 
-    @pl.when(slot == slots - 1)
-    def _():
-        blank = jnp.zeros((rhs, out_ref.shape[2] * LANES - tile), F32)
-        pair = dot_t(extra_ref[...].astype(BF16), own_ref[...])
-        for part in range(slots):
-            pair = pair + dot_t(sent_ref[part], rows_ref[:, part * tile : (part + 1) * tile])
-            piece = jnp.concatenate([sent_ref[part].astype(F32), blank], axis=1)
-            piece = row_tiles(piece).astype(BF16)
-            for first in range(0, out_ref.shape[0], rhs):
-                out_ref[first : first + rhs, part, :, :] = piece
-        sums_ref[...] = grams_ref[...]
-        sums_ref[:, :rhs] = pair
-        pieces = [total_ref[...], *three_parts(sums_ref[...])]
-        pieces.append(blank[:, (len(pieces) - 1) * LANES :])
-        piece = row_tiles(jnp.concatenate(pieces, axis=1)).astype(BF16)
-        for first in range(0, out_ref.shape[0], rhs):
-            out_ref[first : first + rhs, slots, :, :] = piece
-
-
-def joined(values, width):
-    return (values[width : width + 1] + values[width + 1 : width + 2]) + values[width + 2 : width + 3]
-
-
-def reduce_kernel(width, place_ref, received_ref, out_ref):
-    senders, parts, height, lanes = received_ref.shape
-    slots = parts - 1
-    plane, own_place = place_ref[2], place_ref[4]
-    count = out_ref.shape[0]
-    planes = count // (slots * slots) * 2
-    rhs = senders // planes
-    row = lax.broadcasted_iota(jnp.int32, (height, lanes), 0)
-
-    def take(sender, part):
-        return received_ref[sender, part, :, :].astype(F32)
-
-    own = take(plane * rhs, slots)
-    rest = take((planes - 1 - plane) * rhs, slots)
-    for sender in range(1, rhs):
-        own = own + take(plane * rhs + sender, slots)
-        rest = rest + take((planes - 1 - plane) * rhs + sender, slots)
-    first, second, third = three_parts(joined(own + rest, width))
-    grams = jnp.where(
-        row == width, first, jnp.where(row == width + 1, second, jnp.where(row == width + 2, third, 0.0))
-    )
-    for target in range(count):
-        sender = plane * (rhs // planes) + target // slots
-        value = take(sender, target % slots) + take(rhs + sender, target % slots)
-        value = value + jnp.where(own_place == target, own, 0.0)
-        out_ref[target, :, :] = jnp.where(row < width, value, grams).astype(BF16)
-
-
-def finish_reduce_kernel(width, received_ref, out_ref):
+    @pl.when(slot == pl.num_programs(0) - 1)
+    def _():
+        out_ref[...] = to_tiles(total_ref[...])
+
+
+def summed(received_ref):
     total = received_ref[0, :, :].astype(F32)
     for sender in range(1, received_ref.shape[0]):
         total = total + received_ref[sender, :, :].astype(F32)
-    row = lax.broadcasted_iota(jnp.int32, total.shape, 0)
-    value = jnp.where(row < width, total, jnp.broadcast_to(joined(total, width), total.shape))
-    for copy in range(out_ref.shape[0]):
-        out_ref[copy, :, :] = value
+    return total
+
+
+def join_kernel(place_ref, received_ref, own_ref, out_ref):
+    size, lanes = own_ref.shape
+    rhs = out_ref.shape[1] - size
+    total = summed(received_ref)
+    packed = pack_sums(unpack_sums(total[size:, :], 5 * rhs), 5 * rhs)
+    planes = out_ref.shape[0] // rhs
+    for plane in range(planes):
+        for_own = place_ref[2] == plane
+        for_row = jnp.logical_and(place_ref[5] == plane, place_ref[3] == place_ref[7])
+        value = jnp.where(for_own, own_ref[...], 0.0) + jnp.where(for_row, total[:size, :], 0.0)
+        value = value.astype(BF16)
+        for copy in range(rhs):
+            out_ref[plane * rhs + copy, :size, :] = value
+            out_ref[plane * rhs + copy, size:, :] = packed
 
 
 def whole(shape):
@@ -359,8 +387,9 @@
     received_ref, base_ref, mid_ref, shifted_ref, solution_ref, residual_ref
 ):
     rhs, tile = base_ref.shape
-    received = flat_rows(received_ref[...])
-    gram = received[:, tile : tile + LANES]
+    size = rhs * tile // LANES
+    total = summed(received_ref)
+    gram = unpack_sums(total[size:, :], 5 * rhs)
     half_wy, bb, yb, yy, wy = (gram[:, index * rhs : (index + 1) * rhs] for index in range(5))
     wy = wy + (half_wy + half_wy.T)
     curvature = yb + SHIFT * bb
@@ -382,7 +411,7 @@
     (inverse_curvature,), eye = inverses([curvature])
     last_t = times(next_gram, inverse_curvature)
     base, mid = base_ref[...], mid_ref[...]
-    top = received[:, :tile] + shifted_ref[...] * mid
+    top = from_tiles(total[:size, :], rhs) + shifted_ref[...] * mid
     from_mid = times(last_t, b1)
     from_base = times(last_t, a2)
     solution_ref[...] = times(step_t + from_base, base) + times(from_mid, mid)
@@ -414,6 +443,7 @@
             spot,
             row_index // (row_count // planes),
             plane * (row_count // planes) + spot // slots,
+            row_index % (row_count // planes),
         ]
     ).astype(jnp.int32)
     near = [[first * side + index for index in range(side)] for first in range(planes)]
@@ -435,11 +465,11 @@
 
     slab = slab_spec(kernel_codes, slots)
     vector = whole((rhs, tile))
-    scale_block = (tile_scales.shape[0] // slots, tile_scales.shape[1])
+    scales = tile_scales.T
     slabs, outgoing, extra = pl.pallas_call(
         first_rows_kernel,
         grid=(slots,),
-        in_specs=[SMEM, slab, pl.BlockSpec(scale_block, lambda slot: (slot, 0)), vector],
+        in_specs=[SMEM, slab, whole(scales.shape), vector],
         out_specs=[
             slab,
             pl.BlockSpec((slots, 1, size + width, LANES), lambda slot: (0, slot, 0, 0)),
@@ -450,9 +480,10 @@
             struct((slots, slots, size + width, LANES), BF16),
             struct((rhs, tile), F32),
         ],
+        scratch_shapes=[pltpu.VMEM((tile_scales.shape[0], tile), F32)],
         compiler_params=PARAMS,
         name="first_rows",
-    )(place, kernel_codes, tile_scales, targets)
+    )(place, kernel_codes, scales, targets)
     received = exchange_near(outgoing.reshape(side, size + width, LANES))
     relayed = plain(
         relay_kernel,
@@ -483,70 +514,59 @@
         shifted,
     )
     received = exchange_near(outgoing)
-    sent, extra = pl.pallas_call(
-        second_rows_kernel,
+    sent, extra, grams = pl.pallas_call(
+        functools.partial(second_rows_kernel, row_count),
         grid=(slots,),
-        in_specs=[SMEM, slab, vector],
-        out_specs=[pl.BlockSpec((1, rhs, tile), lambda slot: (slot, 0, 0)), vector],
-        out_shape=[struct((slots, rhs, tile), BF16), struct((rhs, tile), F32)],
+        in_specs=[SMEM, slab, vector, vector, vector, whole(shifted.shape)],
+        out_specs=[
+            pl.BlockSpec((1, rhs, tile), lambda slot: (slot, 0, 0)),
+            vector,
+            whole((rhs, LANES)),
+        ],
+        out_shape=[
+            struct((slots, rhs, tile), BF16),
+            struct((rhs, tile), F32),
+            struct((rhs, LANES), F32),
+        ],
         compiler_params=PARAMS,
         name="second_rows",
-    )(place, slabs, own)
-    on_mid = jnp.dot(
-        jnp.concatenate([mid, shifted * mid]), mid.T, precision=lax.Precision.HIGHEST
-    )
-    on_base = jnp.dot(
-        jnp.concatenate([targets, mid]), targets.T, precision=lax.Precision.HIGHEST
-    )
-    grams = jnp.concatenate(
-        [jnp.zeros((rhs, rhs), F32), on_base[:rhs], on_base[rhs:], on_mid[:rhs], on_mid[rhs:]], axis=1
-    )
-    grams = jnp.pad(grams * (1.0 / row_count), ((0, 0), (0, LANES - 5 * rhs)))
+    )(place, slabs, own, targets, mid, shifted)
     relayed = jnp.broadcast_to(
         received.reshape(1, slots, slots, width, LANES),
         (deep_count // slots, slots, slots, width, LANES),
     ).reshape(deep_count, slots, width, LANES)
     received = exchange_deep(relayed)
-    height = width + 4
-    outgoing = pl.pallas_call(
+    outgoing, rows = pl.pallas_call(
+        pair_kernel,
+        in_specs=[SMEM] + [pl.BlockSpec(memory_space=pltpu.VMEM)] * 5,
+        out_shape=[
+            struct((side, size + rhs, LANES), BF16),
+            struct((rhs, slots * tile), BF16),
+        ],
+        scratch_shapes=[pltpu.VMEM((rhs, LANES), F32)],
+        compiler_params=PARAMS,
+        name="pair",
+    )(place, received, own, extra, sent, grams)
+    received = exchange_near(outgoing)
+    total = pl.pallas_call(
         second_own_kernel,
         grid=(slots,),
-        in_specs=[
-            SMEM,
-            slab,
-            whole(received.shape),
-            vector,
-            vector,
-            whole(sent.shape),
-            whole(grams.shape),
-        ],
-        out_specs=whole((deep_count, slots + 1, height, LANES)),
-        out_shape=struct((deep_count, slots + 1, height, LANES), BF16),
-        scratch_shapes=[
-            pltpu.VMEM((rhs, tile), F32),
-            pltpu.VMEM((rhs, slots * tile), BF16),
-            pltpu.VMEM((rhs, LANES), F32),
-        ],
+        in_specs=[SMEM, slab, whole(rows.shape), vector, vector],
+        out_specs=whole((size, LANES)),
+        out_shape=struct((size, LANES), F32),
+        scratch_shapes=[pltpu.VMEM((rhs, tile), F32)],
         compiler_params=PARAMS,
         name="second_own",
-    )(place, slabs, received, own, extra, sent, grams)
-    received = exchange_deep(outgoing)
+    )(place, slabs, rows, own, extra)
     outgoing = plain(
-        functools.partial(reduce_kernel, width),
-        struct((side, height, LANES), BF16),
-        "reduce_planes",
+        join_kernel,
+        struct((deep_count, size + rhs, LANES), BF16),
+        "join",
         place,
         received,
-    )
-    received = exchange_near(outgoing)
-    outgoing = plain(
-        functools.partial(finish_reduce_kernel, width),
-        struct((row_count, height, LANES), F32),
-        "reduce_tiles",
-        received,
-        scalars=False,
-    )
-    received = exchange_row(outgoing)
+        total,
+    )
+    received = exchange_deep(outgoing)
     return tuple(
         plain(
             final_kernel,

time: 159 us -> 146 us (0.918)
  blocking collectives: 79 us -> 71.8 us
  matrix products: 2.11 us -> 0 us
  waiting for transfers between devices: 17.3 us -> 15.5 us
    all_to_all x1 -> x0, blocking collectives: 9.48 us -> none  [exchange_row(): return lax.all_to_all(values, 'row', 0, 0)]
    all_to_all x2, blocking collectives: 40.6 us -> 43.7 us  [exchange_deep(): return lax.all_to_all(values, ('row', 'col'), 0, 0, axis_index_groups=deep)]
    pallas_call x2 -> x3, Pallas kernels: 16 us -> 18.1 us  [the longest x1 9.82 us: local(): pl.pallas_call(first_rows_kernel, grid=(slots,), in_specs=[SMEM, slab, wh...]
    dot_general x2 -> x0, matrix products: 2.11 us -> none  [the longest x1 1.12 us: local(): jnp.dot(jnp.concatenate([mid, shifted * mid]), mid.T, precision=lax.Preci...]
    all_to_all x1, waiting for transfers between devices: 6.44 us -> 4.4 us  [exchange_near(): return lax.all_to_all(values, 'col', 0, 0, axis_index_groups=near)]
    pallas_call x5 -> x4, Pallas kernels: 10.4 us -> 9.48 us  [plain(): pl.pallas_call(kernel, in_specs=specs, out_shape=outs, compiler_params=PA...]
  transfers between devices with their start and end apart: 3 -> 3, of which waited for: 3 -> 3; matrix products, arithmetic and copies ran while one was open for 1% -> 0% of each run, Pallas kernels for 4% -> 9%
where the time goes in v4:
time: 146 us; the launch traced here: 145 us
  blocking collectives  71.8 us (49%)
  Pallas kernels  40.6 us (28%)
  waiting for transfers between devices  15.5 us (11%)
  starting transfers between devices  12.4 us (8%)
  local copies, waits for them, and re-layouts  4.12 us (3%)
    all_to_all x2, blocking collectives, exchange_deep(): return lax.all_to_all(values, ('row', 'col'), 0, 0, axis_index_groups=deep)  43.7 us
    all_to_all x2, blocking collectives, exchange_near(): return lax.all_to_all(values, 'col', 0, 0, axis_index_groups=near)  28.1 us
    pallas_call x1, Pallas kernels, local(): pl.pallas_call(first_rows_kernel, grid=(slots,), in_specs=[SMEM, slab, wh...  9.82 us
    pallas_call x4, Pallas kernels, plain(): pl.pallas_call(kernel, in_specs=specs, out_shape=outs, compiler_params=PA...  9.48 us
    all_to_all x1, waiting for transfers between devices, exchange_row(): return lax.all_to_all(values, 'row', 0, 0)  6.89 us
    pallas_call x1, Pallas kernels, local(): pl.pallas_call(first_own_kernel, grid=(slots,), in_specs=[SMEM, slab, who...  6.56 us
    pallas_call x1, Pallas kernels, local(): pl.pallas_call(second_own_kernel, grid=(slots,), in_specs=[SMEM, slab, wh...  6.42 us
    pallas_call x1, Pallas kernels, local(): pl.pallas_call(functools.partial(second_rows_kernel, row_count), grid=(sl...  6.16 us
  transfers between devices with their start and end apart: 3, of which 3 were waited for; matrix products, arithmetic and copies ran while one was open for 0% of the time, Pallas kernels for 9%

profile of v4, /device:TPU:1, one launch (start us, length us, event | category | flops | bytes accessed | tf_op | source)
XLA Modules:
  0.0 145.2 jit_solution(8572441581377682663)
XLA Ops:
  0.7 0.6 stack.35.place_ref
  1.3 0.0 copy-start.2
  1.3 0.0 copy-start.3
  1.3 9.8 %first_rows.1 = (bf16[3072,1536]{1,0:T(8,128)(2,1)}, bf16[4,4,108,128]{3,2,1,0:T(8,128)(2,1)}, f32[8,1536]{1,0:T(8,128)}) custom-call(s32[8]{0:T(128)} %stack.35.place_ref, bf16[3072,1536]{1,0:T(8,128)(2,1)} %codes_ref.1, f32[48,96]{1,0:T(8,128)} %bitcast.14, f32[8,1536]{1,0:T(8,128)} %base_ref.9), custom_call_target="tpu_custom_call" | custom-call | tf_op jit(solution)/shard_map/first_rows/pallas_call | solution.py:469
  11.1 18.1 %all_to_all.35.received_ref = bf16[16,108,128]{2,1,0:T(8,128)(2,1)} all-to-all(bf16[16,108,128]{2,1,0:T(8,128)(2,1)} %bitcast.12), channel_id=1, replica_groups={{0,1,2,3,4,5,6,7,8,9,10,11,12,13,14,15},{16,17,18,19,20,21,22,23,24,25,..., dimensions={0} | all-to-all | bytes 884736 | tf_op jit(solution)/shard_map/all_to_all | solution.py:458
  29.2 1.8 %relay.1 = bf16[16,5,12,128]{3,2,1,0:T(8,128)(2,1)} custom-call(bf16[16,108,128]{2,1,0:T(8,128)(2,1)} %all_to_all.35.received_ref), custom_call_target="tpu_custom_call" | custom-call | tf_op jit(solution)/shard_map/relay/pallas_call | solution.py:346
  31.1 23.8 %all_to_all.36.received_ref = bf16[16,5,12,128]{3,2,1,0:T(8,128)(2,1)} all-to-all(bf16[16,5,12,128]{3,2,1,0:T(8,128)(2,1)} %relay.1), channel_id=1, replica_groups={{0,32,64,96,128,160,192,224,16,48,80,112,144,176,208,240},{1,33,65,97,1..., dimensions={0} | all-to-all | bytes 491520 | tf_op jit(solution)/shard_map/all_to_all | solution.py:461
  54.9 6.6 %first_own.1 = bf16[8,108,128]{2,1,0:T(8,128)(2,1)} custom-call(s32[8]{0:T(128)} %stack.35.place_ref, bf16[3072,1536]{1,0:T(8,128)(2,1)} %get-tuple-element.13.slab_ref, bf16[16,5,12,128]{3,2,1,0:T(8,128)(2,1)} %all_to_all.36.received_ref, f32[8,1536]{1,0:T(8,128)} %base_ref.9, f32[8,1536]{1,0:T(8,128)} %get-tuple-element.15.extra_ref), custom_call_target="tpu_custom_call" | custom-call | tf_op jit(solution)/shard_map/first_own/pallas_call | solution.py:496
  61.4 3.4 %all-to-all-start.2 = ((bf16[8,108,128]{2,1,0:T(8,128)(2,1)}), bf16[8,108,128]{2,1,0:T(8,128)(2,1)S(1)}, u32[]{:S(2)}, u32[]{:S(2)}) async-start(bf16[8,108,128]{2,1,0:T(8,128)(2,1)} %first_own.1), calls=%async_computation.2 | async-start | bytes 458752 | tf_op jit(solution)/shard_map/all_to_all | solution.py:464
  64.8 0.0 copy-done.2
  64.8 0.0 copy-done.3
  64.8 0.6 broadcast_in_dim.10.shifted_ref
  65.4 6.9 %all-to-all-done.2.received_ref = bf16[8,108,128]{2,1,0:T(8,128)(2,1)S(1)} async-done(((bf16[8,108,128]{2,1,0:T(8,128)(2,1)}), bf16[8,108,128]{2,1,0:T(8,128)(2,1)S(1)}, u32[]{:S(2)}, u32[]{:S(2)}) %all-to-all-start.2) | async-done | bytes 221216 | tf_op jit(solution)/shard_map/all_to_all | solution.py:464
  72.3 0.0 copy-start.1
  72.3 0.7 copy-done.1
  73.0 1.7 %combine.1 = (f32[8,1536]{1,0:T(8,128)}, bf16[8,1536]{1,0:T(8,128)(2,1)}, bf16[16,12,128]{2,1,0:T(8,128)(2,1)}) custom-call(s32[8]{0:T(128)} %stack.35.place_ref, bf16[8,108,128]{2,1,0:T(8,128)(2,1)} %copy-done.1, f32[8,1536]{1,0:T(8,128)} %base_ref.9, f32[1,1536]{1,0:T(1,128)} %broadcast_in_dim.10.shifted_ref), custom_call_target="tpu_custom_call" | custom-call | tf_op jit(solution)/shard_map/combine/pallas_call | solution.py:346
  74.7 9.9 %all_to_all.37 = bf16[16,12,128]{2,1,0:T(8,128)(2,1)S(1)} all-to-all(bf16[16,12,128]{2,1,0:T(8,128)(2,1)} %get-tuple-element.16), channel_id=1, replica_groups={{0,1,2,3,4,5,6,7,8,9,10,11,12,13,14,15},{16,17,18,19,20,21,22,23,24,25,..., dimensions={0} | all-to-all | bytes 98304 | tf_op jit(solution)/shard_map/all_to_all | solution.py:458
  84.6 0.7 broadcast_in_dim.12
  85.4 5.5 %all-to-all-start.4 = ((bf16[16,4,12,128]{3,1,2,0:T(4,128)(2,1)}), bf16[16,4,12,128]{3,1,2,0:T(4,128)(2,1)S(1)}, u32[]{:S(2)}, u32[]{:S(2)}) async-start(bf16[16,4,12,128]{3,1,2,0:T(4,128)(2,1)} %bitcast.11), calls=%async_computation.4 | async-start | bytes 393216 | tf_op jit(solution)/shard_map/all_to_all | solution.py:461
  90.9 6.2 %second_rows.1 = (bf16[4,8,1536]{2,1,0:T(8,128)(2,1)}, f32[8,1536]{1,0:T(8,128)}, f32[8,128]{1,0:T(8,128)}) custom-call(s32[8]{0:T(128)} %stack.35.place_ref, bf16[3072,1536]{1,0:T(8,128)(2,1)} %get-tuple-element.13.slab_ref, bf16[8,1536]{1,0:T(8,128)(2,1)} %get-tuple-element.17.own_ref, f32[8,1536]{1,0:T(8,128)} %base_ref.9, ...), custom_call_target="tpu_custom_call" | custom-call | tf_op jit(solution)/shard_map/second_rows/pallas_call | solution.py:517
  97.1 4.2 %all-to-all-done.4 = bf16[16,4,12,128]{3,1,2,0:T(4,128)(2,1)S(1)} async-done(((bf16[16,4,12,128]{3,1,2,0:T(4,128)(2,1)}), bf16[16,4,12,128]{3,1,2,0:T(4,128)(2,1)S(1)}, u32[]{:S(2)}, u32[]{:S(2)}) %all-to-all-start.4) | async-done | bytes 196640 | tf_op jit(solution)/shard_map/all_to_all | solution.py:461
  101.3 0.8 copy.8.received_ref
  102.0 2.1 %pair.1 = (bf16[16,104,128]{2,1,0:T(8,128)(2,1)}, bf16[8,6144]{1,0:T(8,128)(2,1)}) custom-call(s32[8]{0:T(128)} %stack.35.place_ref, bf16[16,4,12,128]{3,2,1,0:T(8,128)(2,1)} %copy.8.received_ref, bf16[8,1536]{1,0:T(8,128)(2,1)} %get-tuple-element.17.own_ref, f32[8,1536]{1,0:T(8,128)} %get-tuple-element.19.extra_ref, ...), custom_call_target="tpu_custom_call" | custom-call | tf_op jit(solution)/shard_map/pair/pallas_call | solution.py:539
  104.2 3.6 %all-to-all-start.5 = ((bf16[16,104,128]{2,1,0:T(8,128)(2,1)}), bf16[16,104,128]{2,1,0:T(8,128)(2,1)S(1)}, u32[]{:S(2)}, u32[]{:S(2)}) async-start(bf16[16,104,128]{2,1,0:T(8,128)(2,1)} %get-tuple-element.22), calls=%async_computation.5 | async-start | bytes 851968 | tf_op jit(solution)/shard_map/all_to_all | solution.py:458
  107.7 6.4 %second_own.1.own_ref = f32[96,128]{1,0:T(8,128)} custom-call(s32[8]{0:T(128)} %stack.35.place_ref, bf16[3072,1536]{1,0:T(8,128)(2,1)} %get-tuple-element.13.slab_ref, bf16[8,6144]{1,0:T(8,128)(2,1)} %get-tuple-element.23.rows_ref, bf16[8,1536]{1,0:T(8,128)(2,1)} %get-tuple-element.17.own_ref, f32[8,1536]{1,0:T(8,128)} %get-tuple-element.19.extra_ref), custom_call_target="tpu_custom_call" | custom-call | tf_op jit(solution)/shard_map/second_own/pallas_call | solution.py:551
  114.2 4.4 %all-to-all-done.5.received_ref = bf16[16,104,128]{2,1,0:T(8,128)(2,1)S(1)} async-done(((bf16[16,104,128]{2,1,0:T(8,128)(2,1)}), bf16[16,104,128]{2,1,0:T(8,128)(2,1)S(1)}, u32[]{:S(2)}, u32[]{:S(2)}) %all-to-all-start.5) | async-done | bytes 426016 | tf_op jit(solution)/shard_map/all_to_all | solution.py:458
  118.6 0.0 copy-start
  118.6 0.8 copy-done
  119.3 1.9 %join.1 = bf16[16,104,128]{2,1,0:T(8,128)(2,1)} custom-call(s32[8]{0:T(128)} %stack.35.place_ref, bf16[16,104,128]{2,1,0:T(8,128)(2,1)} %copy-done, f32[96,128]{1,0:T(8,128)} %second_own.1.own_ref), custom_call_target="tpu_custom_call" | custom-call | tf_op jit(solution)/shard_map/join/pallas_call | solution.py:346
  121.3 19.9 %all_to_all.38.received_ref = bf16[16,104,128]{2,1,0:T(8,128)(2,1)} all-to-all(bf16[16,104,128]{2,1,0:T(8,128)(2,1)} %join.1), channel_id=1, replica_groups={{0,32,64,96,128,160,192,224,16,48,80,112,144,176,208,240},{1,33,65,97,1..., dimensions={0} | all-to-all | bytes 851968 | tf_op jit(solution)/shard_map/all_to_all | solution.py:461
  141.1 4.0 %small_solves.1 = (f32[8,1536]{1,0:T(8,128)}, f32[8,1536]{1,0:T(8,128)}) custom-call(bf16[16,104,128]{2,1,0:T(8,128)(2,1)} %all_to_all.38.received_ref, f32[8,1536]{1,0:T(8,128)} %base_ref.9, f32[8,1536]{1,0:T(8,128)} %get-tuple-element.18.mid_ref, f32[1,1536]{1,0:T(1,128)} %broadcast_in_dim.10.shifted_ref), custom_call_target="tpu_custom_call" | custom-call | tf_op jit(solution)/shard_map/small_solves/pallas_call | solution.py:346
  (2 shorter events, 0.0 us)
Async XLA Ops:
  1.3 63.5 %copy-start.2 = (f32[1536]{0:T(1024)S(1)}, f32[1536]{0:T(1024)}, u32[]{:S(2)}) copy-start(f32[1536]{0:T(1024)} %param.8) | copy-start | bytes 18436
  1.3 63.6 %copy-start.3 = (f32[1536]{0:T(1024)S(1)}, f32[1536]{0:T(1024)}, u32[]{:S(2)}) copy-start(f32[1536]{0:T(1024)} %param.7) | copy-start | bytes 18436
  61.4 10.9 %all-to-all-start.2 = ((bf16[8,108,128]{2,1,0:T(8,128)(2,1)}), bf16[8,108,128]{2,1,0:T(8,128)(2,1)S(1)}, u32[]{:S(2)}, u32[]{:S(2)}) async-start(bf16[8,108,128]{2,1,0:T(8,128)(2,1)} %first_own.1), calls=%async_computation.2 | async-start | bytes 458752 | tf_op jit(solution)/shard_map/all_to_all | solution.py:464
  72.3 0.7 copy-start.1
  85.4 15.9 %all-to-all-start.4 = ((bf16[16,4,12,128]{3,1,2,0:T(4,128)(2,1)}), bf16[16,4,12,128]{3,1,2,0:T(4,128)(2,1)S(1)}, u32[]{:S(2)}, u32[]{:S(2)}) async-start(bf16[16,4,12,128]{3,1,2,0:T(4,128)(2,1)} %bitcast.11), calls=%async_computation.4 | async-start | bytes 393216 | tf_op jit(solution)/shard_map/all_to_all | solution.py:461
  104.2 14.4 %all-to-all-start.5 = ((bf16[16,104,128]{2,1,0:T(8,128)(2,1)}), bf16[16,104,128]{2,1,0:T(8,128)(2,1)S(1)}, u32[]{:S(2)}, u32[]{:S(2)}) async-start(bf16[16,104,128]{2,1,0:T(8,128)(2,1)} %get-tuple-element.22), calls=%async_computation.5 | async-start | bytes 851968 | tf_op jit(solution)/shard_map/all_to_all | solution.py:458
  118.6 0.8 copy-start

commit v5 on v4

--- a/solution.py
+++ b/solution.py
@@ -10,7 +10,7 @@
 F32 = jnp.float32
 BF16 = jnp.bfloat16
 SHIFT = 3.0
-VMEM_LIMIT = 56 * 1024 * 1024
+VMEM_LIMIT = 32 * 1024 * 1024
 
 
 def spread_scales(scales_ref, wide_ref):
@@ -28,15 +28,14 @@
     )
 
 
-def dequantize_slot(slot, codes_ref, wide_ref, out_ref):
-    rows = codes_ref.shape[0]
-    block_rows = wide_ref.shape[0] // pl.num_programs(0)
+def dequantize_slot(slot, slots, codes_ref, wide_ref, slab_ref):
+    rows = codes_ref.shape[0] // slots
+    block_rows = wide_ref.shape[0] // slots
     order = rows // block_rows
-    start = pl.multiple_of(slot * block_rows, 8)
-    wide = wide_ref[pl.ds(start, block_rows), :]
-    for block in range(block_rows):
+    for block in range(slot * block_rows, (slot + 1) * block_rows):
         part = slice(block * order, (block + 1) * order)
-        out_ref[part, :] = (codes_ref[part, :].astype(F32) * wide[block : block + 1, :]).astype(BF16)
+        wide = wide_ref[block : block + 1, :]
+        slab_ref[part, :] = (codes_ref[part, :].astype(F32) * wide).astype(BF16)
 
 
 NT = (((1,), (1,)), ((), ()))
@@ -90,22 +89,21 @@
     return jnp.sum(jnp.where(row == row_index, tiles, 0.0), axis=0)
 
 
-def toward_rows(slot, offset, slab_ref, own, put, extra_ref):
+def toward_rows(slot, offset, slab_ref, own, put, extra_ref, beside):
     half, tile = slab_ref.shape
     rhs = own.shape[0]
-
-    @pl.when(slot == 0)
-    def _():
-        extra_ref[...] = jnp.zeros_like(extra_ref)
 
     @pl.when(slot < offset)
     def _():
         second = dot_t(own, slab_ref[...])
+        beside()
         put(jnp.concatenate([second, jnp.zeros((rhs, tile - half), F32)], axis=1))
 
     @pl.when(slot > offset)
     def _():
-        put(dot(own[:, half:], slab_ref[...]))
+        first = dot(own[:, half:], slab_ref[...])
+        beside()
+        put(first)
 
     @pl.when(slot == offset)
     def _():
@@ -113,80 +111,152 @@
         head, tail = own[:, :half], own[:, half:]
         extra_ref[:, :half] = dot_t(head, low) + dot_t(tail, slab_ref[:, half:])
         extra_ref[:, half:] = dot_t(tail, high)
+        beside()
         put(jnp.zeros((rhs, tile), F32))
 
 
+def slot_copies(source_ref, target_ref, semaphores):
+    slots = semaphores.shape[0]
+    half = source_ref.shape[0] // slots
+    copies = []
+    for slot in range(slots):
+        part = pl.ds(slot * half, half)
+        copies.append(
+            pltpu.make_async_copy(
+                source_ref.at[part, :], target_ref.at[part, :], semaphores.at[slot]
+            )
+        )
+    return copies
+
+
+def slot_of(slab_ref, slot, half):
+    return slab_ref.at[pl.ds(slot * half, half), :]
+
+
 def first_rows_kernel(
-    place_ref, codes_ref, scales_ref, base_ref, slab_ref, out_ref, extra_ref, wide_ref
+    place_ref,
+    codes_hbm,
+    scales_ref,
+    base_ref,
+    shifted_ref,
+    slab_ref,
+    stored_hbm,
+    out_ref,
+    extra_ref,
+    scaled_ref,
+    wide_ref,
+    codes_ref,
+    arrived,
+    stored,
 ):
-    @pl.when(pl.program_id(0) == 0)
-    def _():
-        spread_scales(scales_ref, wide_ref)
-
-    dequantize_slot(pl.program_id(0), codes_ref, wide_ref, slab_ref)
+    slots = out_ref.shape[1]
+    half = slab_ref.shape[0] // slots
+    copies = slot_copies(codes_hbm, codes_ref, arrived)
+    stores = slot_copies(slab_ref, stored_hbm, stored)
+    for copy in copies:
+        copy.start()
+    spread_scales(scales_ref, wide_ref)
     rhs, tile = base_ref.shape
     size = rhs * tile // LANES
     base = base_ref[...]
+    scaled_ref[...] = shifted_ref[...] * base
+    own = base.astype(BF16)
     share = share_of(base, place_ref[1]).astype(BF16)
-    for copy in range(out_ref.shape[0]):
-        out_ref[copy, 0, size:, :] = share
-
-    def put(values):
-        tiles = to_tiles(values).astype(BF16)
-        for copy in range(out_ref.shape[0]):
-            out_ref[copy, 0, :size, :] = tiles
-
-    toward_rows(pl.program_id(0), place_ref[0], slab_ref, base.astype(BF16), put, extra_ref)
+    for copy in range(slots):
+        for slot in range(slots):
+            out_ref[copy, slot, size:, :] = share
+    extra_ref[...] = jnp.zeros_like(extra_ref)
+    copies[0].wait()
+    dequantize_slot(0, slots, codes_ref, wide_ref, slab_ref)
+    stores[0].start()
+    for slot in range(slots):
+        if slot + 1 < slots:
+            copies[slot + 1].wait()
+
+        def beside(slot=slot):
+            if slot + 1 < slots:
+                dequantize_slot(slot + 1, slots, codes_ref, wide_ref, slab_ref)
+
+        def put(values, slot=slot):
+            tiles = to_tiles(values).astype(BF16)
+            for copy in range(slots):
+                out_ref[copy, slot, :size, :] = tiles
+
+        view = slot_of(slab_ref, slot, half)
+        toward_rows(slot, place_ref[0], view, own, put, extra_ref, beside)
+        if slot + 1 < slots:
+            stores[slot + 1].start()
+    for store in stores:
+        store.wait()
 
 
 def second_rows_kernel(
-    copies, place_ref, slab_ref, own_ref, base_ref, mid_ref, shifted_ref, out_ref, extra_ref, sums_ref
+    copies, place_ref, slab_hbm, own_ref, base_ref, mid_ref, shifted_ref,
+    out_ref, extra_ref, sums_ref, slab_ref, arrived
 ):
+    fetches = slot_copies(slab_hbm, slab_ref, arrived)
+    for fetch in fetches:
+        fetch.start()
     rhs = own_ref.shape[0]
-
-    @pl.when(pl.program_id(0) == 0)
-    def _():
-        base, mid = base_ref[...], mid_ref[...]
-        exact = functools.partial(
-            lax.dot_general,
-            dimension_numbers=NT,
-            precision=lax.Precision.HIGHEST,
-            preferred_element_type=F32,
-        )
-        on_base = exact(jnp.concatenate([base, mid]), base)
-        on_mid = exact(jnp.concatenate([mid, shifted_ref[...] * mid]), mid)
-        sums_ref[...] = jnp.zeros_like(sums_ref)
-        for part, value in enumerate((on_base[:rhs], on_base[rhs:], on_mid[:rhs], on_mid[rhs:])):
-            sums_ref[:, (part + 1) * rhs : (part + 2) * rhs] = value * (1.0 / copies)
-
-    def put(values):
-        out_ref[0, :, :] = values.astype(BF16)
-
-    toward_rows(pl.program_id(0), place_ref[0], slab_ref, own_ref[...], put, extra_ref)
-
-
-def relay_kernel(received_ref, out_ref):
+    base, mid = base_ref[...], mid_ref[...]
+    exact = functools.partial(
+        lax.dot_general,
+        dimension_numbers=NT,
+        precision=lax.Precision.HIGHEST,
+        preferred_element_type=F32,
+    )
+    on_base = exact(jnp.concatenate([base, mid]), base)
+    on_mid = exact(jnp.concatenate([mid, shifted_ref[...] * mid]), mid)
+    sums_ref[...] = jnp.zeros_like(sums_ref)
+    for part, value in enumerate((on_base[:rhs], on_base[rhs:], on_mid[:rhs], on_mid[rhs:])):
+        sums_ref[:, (part + 1) * rhs : (part + 2) * rhs] = value * (1.0 / copies)
+    extra_ref[...] = jnp.zeros_like(extra_ref)
+    for slot in range(out_ref.shape[0]):
+
+        def put(values, slot=slot):
+            out_ref[slot, :, :] = values.astype(BF16)
+
+        half = slab_ref.shape[0] // out_ref.shape[0]
+        view = slot_of(slab_ref, slot, half)
+        fetches[slot].wait()
+        toward_rows(slot, place_ref[0], view, own_ref[...], put, extra_ref, lambda: None)
+
+
+def relay_kernel(width, received_ref, out_ref):
     senders, height, lanes = received_ref.shape
-    copies, parts, width, lanes = out_ref.shape
+    copies, full, lanes = out_ref.shape
     size = height - width
-    slots = parts - 1
+    slots = full // width - 1
     rhs = size // width
     reduced = received_ref[0, :size, :].astype(F32)
     for sender in range(1, senders):
         reduced = reduced + received_ref[sender, :size, :].astype(F32)
     rows = row_tiles(from_tiles(reduced, rhs)).astype(BF16)
+    groups = []
+    for first in range(0, senders, slots):
+        pieces = [received_ref[first + part, size:, :].astype(F32) for part in range(slots)]
+        groups.append(jnp.concatenate(pieces, axis=0).astype(BF16))
     for copy in range(copies):
-        first = (copy % (senders // slots)) * slots
-        out_ref[copy, :slots, :, :] = received_ref[first : first + slots, size:, :]
-        out_ref[copy, slots, :, :] = rows[copy % rhs]
+        out_ref[copy, : slots * width, :] = groups[copy % len(groups)]
+        out_ref[copy, slots * width :, :] = rows[copy % rhs]
+
+
+def spread_kernel(received_ref, out_ref):
+    senders, width, lanes = received_ref.shape
+    slots = out_ref.shape[1] // width
+    for first in range(0, senders, slots):
+        pieces = [received_ref[first + part].astype(F32) for part in range(slots)]
+        group = jnp.concatenate(pieces, axis=0).astype(BF16)
+        for copy in range(first // slots, out_ref.shape[0], senders // slots):
+            out_ref[copy, :, :] = group
 
 
 def gather_rows(place_ref, received_ref, rows_ref, tile, slots):
     rhs = rows_ref.shape[0]
     start = place_ref[5] * rhs
-    for part in range(slots):
-        piece = received_ref[pl.ds(start, rhs), part, :, :].astype(F32)
-        rows_ref[:, part * tile : (part + 1) * tile] = flat_rows(piece).astype(BF16)
+    size = slots * tile // LANES
+    piece = received_ref[pl.ds(start, rhs), :size, :].astype(F32)
+    rows_ref[...] = flat_rows(piece).astype(BF16)
 
 
 def toward_own(slot, offset, slab_ref, rows_ref, own, total_ref):
@@ -209,42 +279,46 @@
         total_ref[:, half:] += dot(head, slab_ref[:, half:]) + dot(tail, high)
 
 
+def all_toward_own(place_ref, slab_ref, rows_ref, own, total_ref, fetches=None):
+    slots = rows_ref.shape[1] // own.shape[1]
+    half = slab_ref.shape[0] // slots
+    for slot in range(slots):
+        if fetches is not None:
+            fetches[slot].wait()
+        toward_own(slot, place_ref[0], slot_of(slab_ref, slot, half), rows_ref, own, total_ref)
+
+
 def first_own_kernel(
     place_ref, slab_ref, received_ref, base_ref, extra_ref, out_ref, total_ref, rows_ref
 ):
-    slot, slots = pl.program_id(0), rows_ref.shape[1] // base_ref.shape[1]
     rhs, tile = base_ref.shape
-
-    @pl.when(slot == 0)
-    def _():
-        total_ref[...] = extra_ref[...]
-        gather_rows(place_ref, received_ref, rows_ref, tile, slots)
-
-    toward_own(slot, place_ref[0], slab_ref, rows_ref, base_ref[...].astype(BF16), total_ref)
-
-    @pl.when(slot == slots - 1)
-    def _():
-        size = rhs * tile // LANES
-        source = place_ref[6]
-        planes = received_ref.shape[0] // rhs
-        reduced = received_ref[source, slots, :, :].astype(F32)
-        for plane in range(1, planes):
-            reduced = reduced + received_ref[plane * rhs + source, slots, :, :].astype(F32)
-        reduced = reduced.astype(BF16)
-        tiles = to_tiles(total_ref[...]).astype(BF16)
-        for copy in range(out_ref.shape[0]):
-            out_ref[copy, :size, :] = tiles
-            out_ref[copy, size:, :] = reduced
-
-
-def combine_kernel(place_ref, received_ref, base_ref, shifted_ref, mid_ref, own_ref, out_ref):
-    rhs, tile = base_ref.shape
+    slots = rows_ref.shape[1] // tile
+    width = tile // LANES
+    total_ref[...] = extra_ref[...]
+    gather_rows(place_ref, received_ref, rows_ref, tile, slots)
+    all_toward_own(place_ref, slab_ref, rows_ref, base_ref[...].astype(BF16), total_ref)
+    size = rhs * tile // LANES
+    source = place_ref[6]
+    planes = received_ref.shape[0] // rhs
+    part = slice(slots * width, (slots + 1) * width)
+    reduced = received_ref[source, part, :].astype(F32)
+    for plane in range(1, planes):
+        reduced = reduced + received_ref[plane * rhs + source, part, :].astype(F32)
+    reduced = reduced.astype(BF16)
+    tiles = to_tiles(total_ref[...]).astype(BF16)
+    for copy in range(out_ref.shape[0]):
+        out_ref[copy, :size, :] = tiles
+        out_ref[copy, size:, :] = reduced
+
+
+def combine_kernel(place_ref, received_ref, scaled_ref, mid_ref, own_ref, out_ref):
+    rhs, tile = scaled_ref.shape
     size = rhs * tile // LANES
     total = received_ref[0, :size, :].astype(F32)
     for sender in range(1, received_ref.shape[0]):
         total = total + received_ref[sender, :size, :].astype(F32)
     others = flat_rows(received_ref[:, size:, :].astype(F32))
-    mid = (from_tiles(total, rhs) + others) + shifted_ref[...] * base_ref[...]
+    mid = (from_tiles(total, rhs) + others) + scaled_ref[...]
     mid_ref[...] = mid
     own_ref[...] = mid.astype(BF16)
     share = share_of(mid, place_ref[1]).astype(BF16)
@@ -290,18 +364,15 @@
             out_ref[target, :size, :] = tiles
 
 
-def second_own_kernel(place_ref, slab_ref, rows_ref, own_ref, extra_ref, out_ref, total_ref):
-    slot = pl.program_id(0)
-
-    @pl.when(slot == 0)
-    def _():
-        total_ref[...] = extra_ref[...]
-
-    toward_own(slot, place_ref[0], slab_ref, rows_ref, own_ref[...], total_ref)
-
-    @pl.when(slot == pl.num_programs(0) - 1)
-    def _():
-        out_ref[...] = to_tiles(total_ref[...])
+def second_own_kernel(
+    place_ref, slab_hbm, rows_ref, own_ref, extra_ref, out_ref, total_ref, slab_ref, arrived
+):
+    fetches = slot_copies(slab_hbm, slab_ref, arrived)
+    for fetch in fetches:
+        fetch.start()
+    total_ref[...] = extra_ref[...]
+    all_toward_own(place_ref, slab_ref, rows_ref, own_ref[...], total_ref, fetches)
+    out_ref[...] = to_tiles(total_ref[...])
 
 
 def summed(received_ref):
@@ -327,10 +398,6 @@
             out_ref[plane * rhs + copy, size:, :] = packed
 
 
-def whole(shape):
-    return pl.BlockSpec(shape, lambda slot: (0,) * len(shape))
-
-
 SMEM = pl.BlockSpec(memory_space=pltpu.SMEM)
 PARAMS = pltpu.CompilerParams(vmem_limit_bytes=VMEM_LIMIT)
 
@@ -339,17 +406,28 @@
     return jax.ShapeDtypeStruct(shape, dtype)
 
 
-def plain(kernel, outs, name, *operands, scalars=True):
+def in_place(values):
+    return pltpu.with_memory_space_constraint(values, pltpu.VMEM)
+
+
+def in_hbm(values):
+    return pltpu.with_memory_space_constraint(values, pltpu.HBM)
+
+
+def plain(kernel, outs, name, *operands, scalars=True, scratch=(), in_memory=()):
     specs = [pl.BlockSpec(memory_space=pltpu.VMEM)] * len(operands)
     if scalars:
         specs[0] = SMEM
+    for index in in_memory:
+        specs[index] = pl.BlockSpec(memory_space=pltpu.HBM)
     return pl.pallas_call(
-        kernel, in_specs=specs, out_shape=outs, compiler_params=PARAMS, name=name
+        kernel,
+        in_specs=specs,
+        out_shape=outs,
+        scratch_shapes=scratch,
+        compiler_params=PARAMS,
+        name=name,
     )(*operands)
-
-
-def slab_spec(codes, slots):
-    return pl.BlockSpec((codes.shape[0] // slots, codes.shape[1]), lambda slot: (slot, 0))
 
 
 def times(left, right):
@@ -463,46 +541,46 @@
     def exchange_row(values):
         return lax.all_to_all(values, "row", 0, 0)
 
-    slab = slab_spec(kernel_codes, slots)
-    vector = whole((rhs, tile))
     scales = tile_scales.T
-    slabs, outgoing, extra = pl.pallas_call(
+    out_shape = (slots, slots, size + width, LANES)
+    in_vmem = pltpu.VMEM(kernel_codes.shape, BF16)
+    slabs, stored, outgoing, extra, scaled = pl.pallas_call(
         first_rows_kernel,
-        grid=(slots,),
-        in_specs=[SMEM, slab, whole(scales.shape), vector],
-        out_specs=[
-            slab,
-            pl.BlockSpec((slots, 1, size + width, LANES), lambda slot: (0, slot, 0, 0)),
-            vector,
+        in_specs=[SMEM, pl.BlockSpec(memory_space=pltpu.HBM)]
+        + [pl.BlockSpec(memory_space=pltpu.VMEM)] * 3,
+        out_specs=[pl.BlockSpec(memory_space=pltpu.VMEM), pl.BlockSpec(memory_space=pltpu.HBM)]
+        + [pl.BlockSpec(memory_space=pltpu.VMEM)] * 3,
+        out_shape=[in_vmem, pltpu.HBM(kernel_codes.shape, BF16), struct(out_shape, BF16)]
+        + [struct((rhs, tile), F32)] * 2,
+        scratch_shapes=[
+            pltpu.VMEM((tile_scales.shape[0], tile), F32),
+            pltpu.VMEM(kernel_codes.shape, BF16),
+            pltpu.SemaphoreType.DMA((slots,)),
+            pltpu.SemaphoreType.DMA((slots,)),
         ],
-        out_shape=[
-            struct(kernel_codes.shape, BF16),
-            struct((slots, slots, size + width, LANES), BF16),
-            struct((rhs, tile), F32),
-        ],
-        scratch_shapes=[pltpu.VMEM((tile_scales.shape[0], tile), F32)],
         compiler_params=PARAMS,
         name="first_rows",
-    )(place, kernel_codes, scales, targets)
+    )(place, in_hbm(kernel_codes), scales, in_hbm(targets), shifted)
     received = exchange_near(outgoing.reshape(side, size + width, LANES))
     relayed = plain(
-        relay_kernel,
-        struct((deep_count, slots + 1, width, LANES), BF16),
+        functools.partial(relay_kernel, width),
+        struct((deep_count, (slots + 1) * width, LANES), BF16),
         "relay",
         received,
         scalars=False,
     )
     received = exchange_deep(relayed)
-    message = pl.pallas_call(
+    message = plain(
         first_own_kernel,
-        grid=(slots,),
-        in_specs=[SMEM, slab, whole(received.shape), vector, vector],
-        out_specs=whole((row_count, size + width, LANES)),
-        out_shape=struct((row_count, size + width, LANES), BF16),
-        scratch_shapes=[pltpu.VMEM((rhs, tile), F32), pltpu.VMEM((rhs, slots * tile), BF16)],
-        compiler_params=PARAMS,
-        name="first_own",
-    )(place, slabs, received, targets, extra)
+        struct((row_count, size + width, LANES), BF16),
+        "first_own",
+        place,
+        in_place(slabs),
+        received,
+        targets,
+        extra,
+        scratch=[pltpu.VMEM((rhs, tile), F32), pltpu.VMEM((rhs, slots * tile), BF16)],
+    )
     received = exchange_row(message)
     mid, own, outgoing = plain(
         combine_kernel,
@@ -510,31 +588,34 @@
         "combine",
         place,
         received,
-        targets,
-        shifted,
+        scaled,
     )
     received = exchange_near(outgoing)
-    sent, extra, grams = pl.pallas_call(
+    fetched = [pltpu.VMEM(kernel_codes.shape, BF16), pltpu.SemaphoreType.DMA((slots,))]
+    sent, extra, grams = plain(
         functools.partial(second_rows_kernel, row_count),
-        grid=(slots,),
-        in_specs=[SMEM, slab, vector, vector, vector, whole(shifted.shape)],
-        out_specs=[
-            pl.BlockSpec((1, rhs, tile), lambda slot: (slot, 0, 0)),
-            vector,
-            whole((rhs, LANES)),
-        ],
-        out_shape=[
+        [
             struct((slots, rhs, tile), BF16),
             struct((rhs, tile), F32),
             struct((rhs, LANES), F32),
         ],
-        compiler_params=PARAMS,
-        name="second_rows",
-    )(place, slabs, own, targets, mid, shifted)
-    relayed = jnp.broadcast_to(
-        received.reshape(1, slots, slots, width, LANES),
-        (deep_count // slots, slots, slots, width, LANES),
-    ).reshape(deep_count, slots, width, LANES)
+        "second_rows",
+        place,
+        in_hbm(stored),
+        own,
+        targets,
+        mid,
+        shifted,
+        scratch=fetched,
+        in_memory=(1,),
+    )
+    relayed = plain(
+        spread_kernel,
+        struct((deep_count, slots * width, LANES), BF16),
+        "spread",
+        received,
+        scalars=False,
+    )
     received = exchange_deep(relayed)
     outgoing, rows = pl.pallas_call(
         pair_kernel,
@@ -548,16 +629,18 @@
         name="pair",
     )(place, received, own, extra, sent, grams)
     received = exchange_near(outgoing)
-    total = pl.pallas_call(
+    total = plain(
         second_own_kernel,
-        grid=(slots,),
-        in_specs=[SMEM, slab, whole(rows.shape), vector, vector],
-        out_specs=whole((size, LANES)),
-        out_shape=struct((size, LANES), F32),
-        scratch_shapes=[pltpu.VMEM((rhs, tile), F32)],
-        compiler_params=PARAMS,
-        name="second_own",
-    )(place, slabs, rows, own, extra)
+        struct((size, LANES), F32),
+        "second_own",
+        place,
+        in_hbm(stored),
+        rows,
+        own,
+        extra,
+        scratch=[pltpu.VMEM((rhs, tile), F32), *fetched],
+        in_memory=(1,),
+    )
     outgoing = plain(
         join_kernel,
         struct((deep_count, size + rhs, LANES), BF16),

time: 146 us -> 130 us (0.89)
  Pallas kernels: 40.6 us -> 29 us
  blocking collectives: 71.8 us -> 77.2 us
  waiting for transfers between devices: 15.5 us -> 11.1 us
  local copies, waits for them, and re-layouts: 4.12 us -> 0.84 us
  starting transfers between devices: 12.4 us -> 9.29 us
    pallas_call x8 -> x9, Pallas kernels: 38.4 us -> 27.4 us  [the longest x8 18.8 us: plain(): pl.pallas_call(kernel, in_specs=specs, out_shape=outs, scratch_shapes=scr...]
    all_to_all x0 -> x1, blocking collectives: none -> 10.6 us  [exchange_row(): return lax.all_to_all(values, 'row', 0, 0)]
    all_to_all x1 -> x0, waiting for transfers between devices: 6.89 us -> none  [exchange_row(): return lax.all_to_all(values, 'row', 0, 0)]
    all_to_all x1 -> x0, starting transfers between devices: 3.35 us -> none  [exchange_row(): return lax.all_to_all(values, 'row', 0, 0)]
    all_to_all x2, blocking collectives: 43.7 us -> 40.4 us  [exchange_deep(): return lax.all_to_all(values, ('row', 'col'), 0, 0, axis_index_groups=deep)]
    all_to_all x2, blocking collectives: 28.1 us -> 26.1 us  [exchange_near(): return lax.all_to_all(values, 'col', 0, 0, axis_index_groups=near)]
  transfers between devices with their start and end apart: 3 -> 2, of which waited for: 3 -> 2; matrix products, arithmetic and copies ran while one was open for 0% -> 0% of each run, Pallas kernels for 9% -> 8%
where the time goes in v5:
time: 130 us; the launch traced here: 129 us
  blocking collectives  77.2 us (59%)
  Pallas kernels  29 us (22%)
  waiting for transfers between devices  11.1 us (9%)
  starting transfers between devices  9.29 us (7%)
    all_to_all x2, blocking collectives, exchange_deep(): return lax.all_to_all(values, ('row', 'col'), 0, 0, axis_index_groups=deep)  40.4 us
    all_to_all x2, blocking collectives, exchange_near(): return lax.all_to_all(values, 'col', 0, 0, axis_index_groups=near)  26.1 us
    pallas_call x8, Pallas kernels, plain(): pl.pallas_call(kernel, in_specs=specs, out_shape=outs, scratch_shapes=scr...  18.8 us
    all_to_all x1, blocking collectives, exchange_row(): return lax.all_to_all(values, 'row', 0, 0)  10.6 us
    pallas_call x1, Pallas kernels, local(): pl.pallas_call(first_rows_kernel, in_specs=[SMEM, pl.BlockSpec(memory_spa...  8.63 us
    all_to_all x1, starting transfers between devices, exchange_deep(): return lax.all_to_all(values, ('row', 'col'), 0, 0, axis_index_groups=deep)  5.74 us
    all_to_all x1, waiting for transfers between devices, exchange_near(): return lax.all_to_all(values, 'col', 0, 0, axis_index_groups=near)  5.64 us
    all_to_all x1, waiting for transfers between devices, exchange_deep(): return lax.all_to_all(values, ('row', 'col'), 0, 0, axis_index_groups=deep)  5.44 us
  transfers between devices with their start and end apart: 2, of which 2 were waited for; matrix products, arithmetic and copies ran while one was open for 0% of the time, Pallas kernels for 8%

profile of v5, /device:TPU:1, one launch (start us, length us, event | category | flops | bytes accessed | tf_op | source)
XLA Modules:
  0.0 129.0 jit_solution(18274735443765870029)
XLA Ops:
  0.6 0.0 copy-start
  0.7 0.7 add_add_fusion
  1.5 0.1 stack.35.place_ref
  1.5 0.0 copy-start.1
  1.5 0.7 copy-done.1
  2.3 8.6 %first_rows.1 = (bf16[3072,1536]{1,0:T(8,128)(2,1)S(1)}, bf16[3072,1536]{1,0:T(8,128)(2,1)}, bf16[4,4,108,128]{3,2,1,0:T(8,128)(2,1)S(1)}, f32[8,1536]{1,0:T(8,128)S(1)}, f32[8,1536]{1,0:T(8,128)S(1)}) custom-call(s32[8]{0:T(128)S(1)} %stack.35.place_ref, bf16[3072,1536]{1,0:T(8,128)(2,1)} %codes_hbm.1, f32[48,96]{1,0:T(8,128)S(1)} %bitcast.11, ...), custom_call_target="tpu_custom_call" | custom-call | tf_op jit(solution)/shard_map/first_rows/pallas_call | solution.py:547
  10.9 16.6 %all_to_all.35.received_ref = bf16[16,108,128]{2,1,0:T(8,128)(2,1)S(1)} all-to-all(bf16[16,108,128]{2,1,0:T(8,128)(2,1)S(1)} %bitcast.10), channel_id=1, replica_groups={{0,1,2,3,4,5,6,7,8,9,10,11,12,13,14,15},{16,17,18,19,20,21,22,23,24,25,..., dimensions={0} | all-to-all | bytes 884736 | tf_op jit(solution)/shard_map/all_to_all | solution.py:536
  27.5 0.1 relay.1
  27.6 22.2 %all_to_all.36.received_ref = bf16[16,60,128]{2,1,0:T(8,128)(2,1)S(1)} all-to-all(bf16[16,60,128]{2,1,0:T(8,128)(2,1)S(1)} %relay.1), channel_id=1, replica_groups={{0,32,64,96,128,160,192,224,16,48,80,112,144,176,208,240},{1,33,65,97,1..., dimensions={0} | all-to-all | bytes 491520 | tf_op jit(solution)/shard_map/all_to_all | solution.py:539
  49.8 0.0 copy-done
  49.8 3.6 %first_own.1 = bf16[8,108,128]{2,1,0:T(8,128)(2,1)S(1)} custom-call(s32[8]{0:T(128)S(1)} %stack.35.place_ref, bf16[3072,1536]{1,0:T(8,128)(2,1)S(1)} %get-tuple-element.15.slab_ref, bf16[16,60,128]{2,1,0:T(8,128)(2,1)S(1)} %all_to_all.36.received_ref, f32[8,1536]{1,0:T(8,128)S(1)} %copy-done, f32[8,1536]{1,0:T(8,128)S(1)} %get-tuple-element.17.extra_ref), custom_call_target="tpu_custom_call" | custom-call | tf_op jit(solution)/shard_map/first_own/pallas_call | solution.py:423
  53.4 10.6 %all_to_all.37.received_ref = bf16[8,108,128]{2,1,0:T(8,128)(2,1)S(1)} all-to-all(bf16[8,108,128]{2,1,0:T(8,128)(2,1)S(1)} %first_own.1), channel_id=1, replica_groups=mesh['row'=8,'col'=32] {'row'}, dimensions={0} | all-to-all | bytes 442368 | tf_op jit(solution)/shard_map/all_to_all | solution.py:542
  64.0 0.6 combine.1
  64.6 9.5 %all_to_all.38.received_ref = bf16[16,12,128]{2,1,0:T(8,128)(2,1)S(1)} all-to-all(bf16[16,12,128]{2,1,0:T(8,128)(2,1)S(1)} %get-tuple-element.19), channel_id=1, replica_groups={{0,1,2,3,4,5,6,7,8,9,10,11,12,13,14,15},{16,17,18,19,20,21,22,23,24,25,..., dimensions={0} | all-to-all | bytes 98304 | tf_op jit(solution)/shard_map/all_to_all | solution.py:536
  74.2 0.7 spread.1
  74.8 5.7 %all-to-all-start.4 = ((bf16[16,48,128]{2,1,0:T(8,128)(2,1)}), bf16[16,48,128]{2,1,0:T(8,128)(2,1)S(1)}, u32[]{:S(2)}, u32[]{:S(2)}) async-start(bf16[16,48,128]{2,1,0:T(8,128)(2,1)} %spread.1), calls=%async_computation.4 | async-start | bytes 393216 | tf_op jit(solution)/shard_map/all_to_all | solution.py:539
  80.6 4.9 %second_rows.1 = (bf16[4,8,1536]{2,1,0:T(8,128)(2,1)S(1)}, f32[8,1536]{1,0:T(8,128)S(1)}, f32[8,128]{1,0:T(8,128)S(1)}) custom-call(s32[8]{0:T(128)S(1)} %stack.35.place_ref, bf16[3072,1536]{1,0:T(8,128)(2,1)} %get-tuple-element.21.slab_hbm, bf16[8,1536]{1,0:T(8,128)(2,1)S(1)} %get-tuple-element.20.own_ref, f32[8,1536]{1,0:T(8,128)S(1)} %copy-done, ...), custom_call_target="tpu_custom_call" | custom-call | tf_op jit(solution)/shard_map/second_rows/pallas_call | solution.py:423
  85.5 5.4 %all-to-all-done.4.received_ref = bf16[16,48,128]{2,1,0:T(8,128)(2,1)S(1)} async-done(((bf16[16,48,128]{2,1,0:T(8,128)(2,1)}), bf16[16,48,128]{2,1,0:T(8,128)(2,1)S(1)}, u32[]{:S(2)}, u32[]{:S(2)}) %all-to-all-start.4) | async-done | bytes 196640 | tf_op jit(solution)/shard_map/all_to_all | solution.py:539
  91.0 1.6 %pair.1 = (bf16[16,104,128]{2,1,0:T(8,128)(2,1)}, bf16[8,6144]{1,0:T(8,128)(2,1)S(1)}) custom-call(s32[8]{0:T(128)S(1)} %stack.35.place_ref, bf16[16,48,128]{2,1,0:T(8,128)(2,1)S(1)} %all-to-all-done.4.received_ref, bf16[8,1536]{1,0:T(8,128)(2,1)S(1)} %get-tuple-element.20.own_ref, f32[8,1536]{1,0:T(8,128)S(1)} %get-tuple-element.23.extra_ref, ...), custom_call_target="tpu_custom_call" | custom-call | tf_op jit(solution)/shard_map/pair/pallas_call | solution.py:620
  92.6 3.6 %all-to-all-start.5 = ((bf16[16,104,128]{2,1,0:T(8,128)(2,1)}), bf16[16,104,128]{2,1,0:T(8,128)(2,1)S(1)}, u32[]{:S(2)}, u32[]{:S(2)}) async-start(bf16[16,104,128]{2,1,0:T(8,128)(2,1)} %get-tuple-element.26), calls=%async_computation.5 | async-start | bytes 851968 | tf_op jit(solution)/shard_map/all_to_all | solution.py:536
  96.2 5.2 %second_own.1.own_ref = f32[96,128]{1,0:T(8,128)S(1)} custom-call(s32[8]{0:T(128)S(1)} %stack.35.place_ref, bf16[3072,1536]{1,0:T(8,128)(2,1)} %get-tuple-element.21.slab_hbm, bf16[8,6144]{1,0:T(8,128)(2,1)S(1)} %get-tuple-element.27.rows_ref, bf16[8,1536]{1,0:T(8,128)(2,1)S(1)} %get-tuple-element.20.own_ref, f32[8,1536]{1,0:T(8,128)S(1)} %get-tuple-element.23.extra_ref), custom_call_target="tpu_custom_call" | custom-call | tf_op jit(solution)/shard_map/second_own/pallas_call | solution.py:423
  101.3 5.6 %all-to-all-done.5.received_ref = bf16[16,104,128]{2,1,0:T(8,128)(2,1)S(1)} async-done(((bf16[16,104,128]{2,1,0:T(8,128)(2,1)}), bf16[16,104,128]{2,1,0:T(8,128)(2,1)S(1)}, u32[]{:S(2)}, u32[]{:S(2)}) %all-to-all-start.5) | async-done | bytes 426016 | tf_op jit(solution)/shard_map/all_to_all | solution.py:536
  107.0 0.7 join.1
  107.7 18.3 %all_to_all.39.received_ref = bf16[16,104,128]{2,1,0:T(8,128)(2,1)S(1)} all-to-all(bf16[16,104,128]{2,1,0:T(8,128)(2,1)S(1)} %join.1), channel_id=1, replica_groups={{0,32,64,96,128,160,192,224,16,48,80,112,144,176,208,240},{1,33,65,97,1..., dimensions={0} | all-to-all | bytes 851968 | tf_op jit(solution)/shard_map/all_to_all | solution.py:539
  125.9 3.0 %small_solves.1 = (f32[8,1536]{1,0:T(8,128)}, f32[8,1536]{1,0:T(8,128)}) custom-call(bf16[16,104,128]{2,1,0:T(8,128)(2,1)S(1)} %all_to_all.39.received_ref, f32[8,1536]{1,0:T(8,128)S(1)} %copy-done, f32[8,1536]{1,0:T(8,128)S(1)} %get-tuple-element.22.mid_ref, f32[1,1536]{1,0:T(1,128)S(1)} %broadcast_in_dim.3.shifted_ref), custom_call_target="tpu_custom_call" | custom-call | tf_op jit(solution)/shard_map/small_solves/pallas_call | solution.py:423
  (1 shorter events, 0.0 us)
Async XLA Ops:
  0.6 49.2 %copy-start = (f32[8,1536]{1,0:T(8,128)S(1)}, f32[8,1536]{1,0:T(8,128)}, u32[]{:S(2)}) copy-start(f32[8,1536]{1,0:T(8,128)} %base_ref.7) | copy-start | bytes 147460
  1.5 0.7 copy-start.1
  74.8 16.1 %all-to-all-start.4 = ((bf16[16,48,128]{2,1,0:T(8,128)(2,1)}), bf16[16,48,128]{2,1,0:T(8,128)(2,1)S(1)}, u32[]{:S(2)}, u32[]{:S(2)}) async-start(bf16[16,48,128]{2,1,0:T(8,128)(2,1)} %spread.1), calls=%async_computation.4 | async-start | bytes 393216 | tf_op jit(solution)/shard_map/all_to_all | solution.py:539
  92.6 14.4 %all-to-all-start.5 = ((bf16[16,104,128]{2,1,0:T(8,128)(2,1)}), bf16[16,104,128]{2,1,0:T(8,128)(2,1)S(1)}, u32[]{:S(2)}, u32[]{:S(2)}) async-start(bf16[16,104,128]{2,1,0:T(8,128)(2,1)} %get-tuple-element.26), calls=%async_computation.5 | async-start | bytes 851968 | tf_op jit(solution)/shard_map/all_to_all | solution.py:536

commit v6 on v5

--- a/solution.py
+++ b/solution.py
@@ -10,6 +10,7 @@
 F32 = jnp.float32
 BF16 = jnp.bfloat16
 SHIFT = 3.0
+STORED_FIRST = 2
 VMEM_LIMIT = 32 * 1024 * 1024
 
 
@@ -28,11 +29,13 @@
     )
 
 
-def dequantize_slot(slot, slots, codes_ref, wide_ref, slab_ref):
+def dequantize_slot(slot, slots, codes_ref, wide_ref, slab_ref, copies=()):
     rows = codes_ref.shape[0] // slots
     block_rows = wide_ref.shape[0] // slots
     order = rows // block_rows
-    for block in range(slot * block_rows, (slot + 1) * block_rows):
+    for index, block in enumerate(range(slot * block_rows, (slot + 1) * block_rows)):
+        if copies and index % (block_rows // len(copies)) == 0:
+            copies[index // (block_rows // len(copies))].wait()
         part = slice(block * order, (block + 1) * order)
         wide = wide_ref[block : block + 1, :]
         slab_ref[part, :] = (codes_ref[part, :].astype(F32) * wide).astype(BF16)
@@ -115,11 +118,11 @@
         put(jnp.zeros((rhs, tile), F32))
 
 
-def slot_copies(source_ref, target_ref, semaphores):
+def slot_copies(source_ref, target_ref, semaphores, first=0, last=None):
     slots = semaphores.shape[0]
     half = source_ref.shape[0] // slots
     copies = []
-    for slot in range(slots):
+    for slot in range(first, slots if last is None else last):
         part = pl.ds(slot * half, half)
         copies.append(
             pltpu.make_async_copy(
@@ -136,56 +139,74 @@
 def first_rows_kernel(
     place_ref,
     codes_hbm,
-    scales_ref,
-    base_ref,
-    shifted_ref,
+    scales_hbm,
+    base_hbm,
+    diagonal_hbm,
+    noise_hbm,
     slab_ref,
     stored_hbm,
     out_ref,
     extra_ref,
     scaled_ref,
+    shifted_ref,
     wide_ref,
     codes_ref,
+    scales_ref,
+    base_ref,
+    points_ref,
     arrived,
     stored,
+    small,
 ):
     slots = out_ref.shape[1]
     half = slab_ref.shape[0] // slots
+    sources = (scales_hbm, base_hbm, diagonal_hbm, noise_hbm)
+    targets = (scales_ref, base_ref, points_ref.at[0], points_ref.at[1])
+    inputs = [
+        pltpu.make_async_copy(source, target, small.at[index])
+        for index, (source, target) in enumerate(zip(sources, targets))
+    ]
     copies = slot_copies(codes_hbm, codes_ref, arrived)
-    stores = slot_copies(slab_ref, stored_hbm, stored)
-    for copy in copies:
+    stores = slot_copies(slab_ref, stored_hbm, stored, last=STORED_FIRST)
+    each = len(copies) // slots
+    for copy in inputs[:1] + copies[:each] + inputs[1:] + copies[each:]:
         copy.start()
-    spread_scales(scales_ref, wide_ref)
     rhs, tile = base_ref.shape
     size = rhs * tile // LANES
+    inputs[0].wait()
+    spread_scales(scales_ref, wide_ref)
+    extra_ref[...] = jnp.zeros_like(extra_ref)
+    dequantize_slot(0, slots, codes_ref, wide_ref, slab_ref, copies[:each])
+    stores[0].start()
+    inputs[1].wait()
+    own = base_ref[...].astype(BF16)
+    for slot in range(slots):
+        for copy in copies[(slot + 1) * each : (slot + 2) * each]:
+            copy.wait()
+
+        def beside(slot=slot):
+            if slot + 1 < slots:
+                dequantize_slot(slot + 1, slots, codes_ref, wide_ref, slab_ref)
+
+        def put(values, slot=slot):
+            tiles = to_tiles(values).astype(BF16)
+            for copy in range(slots):
+                out_ref[copy, slot, :size, :] = tiles
+
+        view = slot_of(slab_ref, slot, half)
+        toward_rows(slot, place_ref[0], view, own, put, extra_ref, beside)
+        if slot + 1 < len(stores):
+            stores[slot + 1].start()
+    for copy in inputs[2:]:
+        copy.wait()
     base = base_ref[...]
-    scaled_ref[...] = shifted_ref[...] * base
-    own = base.astype(BF16)
+    shifted = points_ref[0:1, :].astype(BF16).astype(F32) + (points_ref[1:2, :] - SHIFT)
+    shifted_ref[...] = shifted
+    scaled_ref[...] = shifted * base
     share = share_of(base, place_ref[1]).astype(BF16)
     for copy in range(slots):
         for slot in range(slots):
             out_ref[copy, slot, size:, :] = share
-    extra_ref[...] = jnp.zeros_like(extra_ref)
-    copies[0].wait()
-    dequantize_slot(0, slots, codes_ref, wide_ref, slab_ref)
-    stores[0].start()
-    for slot in range(slots):
-        if slot + 1 < slots:
-            copies[slot + 1].wait()
-
-        def beside(slot=slot):
-            if slot + 1 < slots:
-                dequantize_slot(slot + 1, slots, codes_ref, wide_ref, slab_ref)
-
-        def put(values, slot=slot):
-            tiles = to_tiles(values).astype(BF16)
-            for copy in range(slots):
-                out_ref[copy, slot, :size, :] = tiles
-
-        view = slot_of(slab_ref, slot, half)
-        toward_rows(slot, place_ref[0], view, own, put, extra_ref, beside)
-        if slot + 1 < slots:
-            stores[slot + 1].start()
     for store in stores:
         store.wait()
 
@@ -289,8 +310,12 @@
 
 
 def first_own_kernel(
-    place_ref, slab_ref, received_ref, base_ref, extra_ref, out_ref, total_ref, rows_ref
+    place_ref, slab_ref, received_ref, base_ref, extra_ref, begun_hbm,
+    out_ref, stored_hbm, total_ref, rows_ref, stored
 ):
+    stores = slot_copies(slab_ref, stored_hbm, stored, first=STORED_FIRST)
+    for store in stores:
+        store.start()
     rhs, tile = base_ref.shape
     slots = rows_ref.shape[1] // tile
     width = tile // LANES
@@ -309,6 +334,8 @@
     for copy in range(out_ref.shape[0]):
         out_ref[copy, :size, :] = tiles
         out_ref[copy, size:, :] = reduced
+    for store in stores:
+        store.wait()
 
 
 def combine_kernel(place_ref, received_ref, scaled_ref, mid_ref, own_ref, out_ref):
@@ -530,7 +557,6 @@
         for index in range(side)
     ]
     deep_count = planes * row_count
-    shifted = (lax.reduce_precision(kernel_diagonal, 8, 7) + (noise_variance - SHIFT))[None, :]
 
     def exchange_near(values):
         return lax.all_to_all(values, "col", 0, 0, axis_index_groups=near)
@@ -544,23 +570,35 @@
     scales = tile_scales.T
     out_shape = (slots, slots, size + width, LANES)
     in_vmem = pltpu.VMEM(kernel_codes.shape, BF16)
-    slabs, stored, outgoing, extra, scaled = pl.pallas_call(
+    small = len((scales, targets, kernel_diagonal, noise_variance))
+    slabs, stored, outgoing, extra, scaled, shifted = pl.pallas_call(
         first_rows_kernel,
-        in_specs=[SMEM, pl.BlockSpec(memory_space=pltpu.HBM)]
-        + [pl.BlockSpec(memory_space=pltpu.VMEM)] * 3,
+        in_specs=[SMEM] + [pl.BlockSpec(memory_space=pltpu.HBM)] * 5,
         out_specs=[pl.BlockSpec(memory_space=pltpu.VMEM), pl.BlockSpec(memory_space=pltpu.HBM)]
-        + [pl.BlockSpec(memory_space=pltpu.VMEM)] * 3,
+        + [pl.BlockSpec(memory_space=pltpu.VMEM)] * 4,
         out_shape=[in_vmem, pltpu.HBM(kernel_codes.shape, BF16), struct(out_shape, BF16)]
-        + [struct((rhs, tile), F32)] * 2,
+        + [struct((rhs, tile), F32)] * 2
+        + [struct((1, tile), F32)],
         scratch_shapes=[
             pltpu.VMEM((tile_scales.shape[0], tile), F32),
             pltpu.VMEM(kernel_codes.shape, BF16),
+            pltpu.VMEM(scales.shape, F32),
+            pltpu.VMEM(targets.shape, F32),
+            pltpu.VMEM((2, tile), F32),
+            pltpu.SemaphoreType.DMA((4 * slots,)),
             pltpu.SemaphoreType.DMA((slots,)),
-            pltpu.SemaphoreType.DMA((slots,)),
+            pltpu.SemaphoreType.DMA((small,)),
         ],
         compiler_params=PARAMS,
         name="first_rows",
-    )(place, in_hbm(kernel_codes), scales, in_hbm(targets), shifted)
+    )(
+        place,
+        in_hbm(kernel_codes),
+        in_hbm(scales),
+        in_hbm(targets),
+        in_hbm(kernel_diagonal),
+        in_hbm(noise_variance),
+    )
     received = exchange_near(outgoing.reshape(side, size + width, LANES))
     relayed = plain(
         functools.partial(relay_kernel, width),
@@ -570,17 +608,24 @@
         scalars=False,
     )
     received = exchange_deep(relayed)
-    message = plain(
+    vmem, hbm = pl.BlockSpec(memory_space=pltpu.VMEM), pl.BlockSpec(memory_space=pltpu.HBM)
+    message, stored = pl.pallas_call(
         first_own_kernel,
-        struct((row_count, size + width, LANES), BF16),
-        "first_own",
-        place,
-        in_place(slabs),
-        received,
-        targets,
-        extra,
-        scratch=[pltpu.VMEM((rhs, tile), F32), pltpu.VMEM((rhs, slots * tile), BF16)],
-    )
+        in_specs=[SMEM] + [vmem] * 4 + [hbm],
+        out_specs=[vmem, hbm],
+        out_shape=[
+            struct((row_count, size + width, LANES), BF16),
+            pltpu.HBM(kernel_codes.shape, BF16),
+        ],
+        scratch_shapes=[
+            pltpu.VMEM((rhs, tile), F32),
+            pltpu.VMEM((rhs, slots * tile), BF16),
+            pltpu.SemaphoreType.DMA((slots,)),
+        ],
+        input_output_aliases={5: 1},
+        compiler_params=PARAMS,
+        name="first_own",
+    )(place, in_place(slabs), received, targets, extra, in_hbm(stored))
     received = exchange_row(message)
     mid, own, outgoing = plain(
         combine_kernel,

time: 130 us -> 129 us (level)
  blocking collectives: 77.2 us -> 78.7 us
    pallas_call x8 -> x7, Pallas kernels: 18.8 us -> 15.2 us  [plain(): pl.pallas_call(kernel, in_specs=specs, out_shape=outs, scratch_shapes=scr...]
    pallas_call x1 -> x2, Pallas kernels: 8.63 us -> 11.3 us  [the longest x1 7.7 us: local(): pl.pallas_call(first_rows_kernel, in_specs=[SMEM] + [pl.BlockSpec(memory_...]
    all_to_all x2, blocking collectives: 26.1 us -> 27.7 us  [exchange_near(): return lax.all_to_all(values, 'col', 0, 0, axis_index_groups=near)]
where the time goes in v6:
time: 129 us; the launch traced here: 128 us
  blocking collectives  78.7 us (61%)
  Pallas kernels  28.1 us (22%)
  waiting for transfers between devices  11.1 us (9%)
  starting transfers between devices  9.29 us (7%)
    all_to_all x2, blocking collectives, exchange_deep(): return lax.all_to_all(values, ('row', 'col'), 0, 0, axis_index_groups=deep)  40.4 us
    all_to_all x2, blocking collectives, exchange_near(): return lax.all_to_all(values, 'col', 0, 0, axis_index_groups=near)  27.7 us
    pallas_call x7, Pallas kernels, plain(): pl.pallas_call(kernel, in_specs=specs, out_shape=outs, scratch_shapes=scr...  15.2 us
    all_to_all x1, blocking collectives, exchange_row(): return lax.all_to_all(values, 'row', 0, 0)  10.6 us
    pallas_call x1, Pallas kernels, local(): pl.pallas_call(first_rows_kernel, in_specs=[SMEM] + [pl.BlockSpec(memory_...  7.7 us
    all_to_all x1, starting transfers between devices, exchange_deep(): return lax.all_to_all(values, ('row', 'col'), 0, 0, axis_index_groups=deep)  5.74 us
    all_to_all x1, waiting for transfers between devices, exchange_near(): return lax.all_to_all(values, 'col', 0, 0, axis_index_groups=near)  5.64 us
    all_to_all x1, waiting for transfers between devices, exchange_deep(): return lax.all_to_all(values, ('row', 'col'), 0, 0, axis_index_groups=deep)  5.44 us
  transfers between devices with their start and end apart: 2, of which 2 were waited for; matrix products, arithmetic and copies ran while one was open for 0% of the time, Pallas kernels for 8%

profile of v6, /device:TPU:1, one launch (start us, length us, event | category | flops | bytes accessed | tf_op | source)
XLA Modules:
  0.0 128.1 jit_solution(2207368985477083557)
XLA Ops:
  0.6 0.0 copy-start
  0.7 0.1 stack.35.place_ref
  0.8 7.7 %first_rows.1 = (bf16[3072,1536]{1,0:T(8,128)(2,1)S(1)}, bf16[3072,1536]{1,0:T(8,128)(2,1)}, bf16[4,4,108,128]{3,2,1,0:T(8,128)(2,1)S(1)}, f32[8,1536]{1,0:T(8,1...) custom-call(s32[8]{0:T(128)S(1)} %stack.35.place_ref, bf16[3072,1536]{1,0:T(8,128)(2,1)} %codes_hbm.1, ...), custom_call_target="tpu_custom_call" | custom-call | tf_op jit(solution)/shard_map/first_rows/pallas_call | solution.py:574
  8.5 18.2 %all_to_all.35.received_ref = bf16[16,108,128]{2,1,0:T(8,128)(2,1)S(1)} all-to-all(bf16[16,108,128]{2,1,0:T(8,128)(2,1)S(1)} %bitcast.10), channel_id=1, replica_groups={{0,1,2,3,4,5,6,7,8,9,10,11,12,13,14,15},{16,17,18,19,20,21,22,23,24,25,..., dimensions={0} | all-to-all | bytes 884736 | tf_op jit(solution)/shard_map/all_to_all | solution.py:562
  26.7 0.1 relay.1
  26.7 22.2 %all_to_all.36.received_ref = bf16[16,60,128]{2,1,0:T(8,128)(2,1)S(1)} all-to-all(bf16[16,60,128]{2,1,0:T(8,128)(2,1)S(1)} %relay.1), channel_id=1, replica_groups={{0,32,64,96,128,160,192,224,16,48,80,112,144,176,208,240},{1,33,65,97,1..., dimensions={0} | all-to-all | bytes 491520 | tf_op jit(solution)/shard_map/all_to_all | solution.py:565
  48.9 0.0 copy-done
  48.9 3.6 %first_own.1 = (bf16[8,108,128]{2,1,0:T(8,128)(2,1)S(1)}, bf16[3072,1536]{1,0:T(8,128)(2,1)}) custom-call(s32[8]{0:T(128)S(1)} %stack.35.place_ref, bf16[3072,1536]{1,0:T(8,128)(2,1)S(1)} %get-tuple-element.18.slab_ref, bf16[16,60,128]{2,1,0:T(8,128)(2,1)S(1)} %all_to_all.36.received_ref, f32[8,1536]{1,0:T(8,128)S(1)} %copy-done, ...), custom_call_target="tpu_custom_call", output_to_operand_aliasing={{1}: (5, {})} | custom-call | tf_op jit(solution)/shard_map/first_own/pallas_call | solution.py:612
  52.6 10.6 %all_to_all.37.received_ref = bf16[8,108,128]{2,1,0:T(8,128)(2,1)S(1)} all-to-all(bf16[8,108,128]{2,1,0:T(8,128)(2,1)S(1)} %get-tuple-element.22), channel_id=1, replica_groups=mesh['row'=8,'col'=32] {'row'}, dimensions={0} | all-to-all | bytes 442368 | tf_op jit(solution)/shard_map/all_to_all | solution.py:568
  63.2 0.6 combine.1
  63.8 9.5 %all_to_all.38.received_ref = bf16[16,12,128]{2,1,0:T(8,128)(2,1)S(1)} all-to-all(bf16[16,12,128]{2,1,0:T(8,128)(2,1)S(1)} %get-tuple-element.24), channel_id=1, replica_groups={{0,1,2,3,4,5,6,7,8,9,10,11,12,13,14,15},{16,17,18,19,20,21,22,23,24,25,..., dimensions={0} | all-to-all | bytes 98304 | tf_op jit(solution)/shard_map/all_to_all | solution.py:562
  73.3 0.7 spread.1
  74.0 5.7 %all-to-all-start.4 = ((bf16[16,48,128]{2,1,0:T(8,128)(2,1)}), bf16[16,48,128]{2,1,0:T(8,128)(2,1)S(1)}, u32[]{:S(2)}, u32[]{:S(2)}) async-start(bf16[16,48,128]{2,1,0:T(8,128)(2,1)} %spread.1), calls=%async_computation.4 | async-start | bytes 393216 | tf_op jit(solution)/shard_map/all_to_all | solution.py:565
  79.7 4.9 %second_rows.1 = (bf16[4,8,1536]{2,1,0:T(8,128)(2,1)S(1)}, f32[8,1536]{1,0:T(8,128)S(1)}, f32[8,128]{1,0:T(8,128)S(1)}) custom-call(s32[8]{0:T(128)S(1)} %stack.35.place_ref, bf16[3072,1536]{1,0:T(8,128)(2,1)} %get-tuple-element.26.slab_hbm, bf16[8,1536]{1,0:T(8,128)(2,1)S(1)} %get-tuple-element.25.own_ref, f32[8,1536]{1,0:T(8,128)S(1)} %copy-done, ...), custom_call_target="tpu_custom_call" | custom-call | tf_op jit(solution)/shard_map/second_rows/pallas_call | solution.py:450
  84.7 5.4 %all-to-all-done.4.received_ref = bf16[16,48,128]{2,1,0:T(8,128)(2,1)S(1)} async-done(((bf16[16,48,128]{2,1,0:T(8,128)(2,1)}), bf16[16,48,128]{2,1,0:T(8,128)(2,1)S(1)}, u32[]{:S(2)}, u32[]{:S(2)}) %all-to-all-start.4) | async-done | bytes 196640 | tf_op jit(solution)/shard_map/all_to_all | solution.py:565
  90.1 1.6 %pair.1 = (bf16[16,104,128]{2,1,0:T(8,128)(2,1)}, bf16[8,6144]{1,0:T(8,128)(2,1)S(1)}) custom-call(s32[8]{0:T(128)S(1)} %stack.35.place_ref, bf16[16,48,128]{2,1,0:T(8,128)(2,1)S(1)} %all-to-all-done.4.received_ref, bf16[8,1536]{1,0:T(8,128)(2,1)S(1)} %get-tuple-element.25.own_ref, f32[8,1536]{1,0:T(8,128)S(1)} %get-tuple-element.29.extra_ref, ...), custom_call_target="tpu_custom_call" | custom-call | tf_op jit(solution)/shard_map/pair/pallas_call | solution.py:665
  91.8 3.6 %all-to-all-start.5 = ((bf16[16,104,128]{2,1,0:T(8,128)(2,1)}), bf16[16,104,128]{2,1,0:T(8,128)(2,1)S(1)}, u32[]{:S(2)}, u32[]{:S(2)}) async-start(bf16[16,104,128]{2,1,0:T(8,128)(2,1)} %get-tuple-element.32), calls=%async_computation.5 | async-start | bytes 851968 | tf_op jit(solution)/shard_map/all_to_all | solution.py:562
  95.3 5.2 %second_own.1.own_ref = f32[96,128]{1,0:T(8,128)S(1)} custom-call(s32[8]{0:T(128)S(1)} %stack.35.place_ref, bf16[3072,1536]{1,0:T(8,128)(2,1)} %get-tuple-element.26.slab_hbm, bf16[8,6144]{1,0:T(8,128)(2,1)S(1)} %get-tuple-element.33.rows_ref, bf16[8,1536]{1,0:T(8,128)(2,1)S(1)} %get-tuple-element.25.own_ref, f32[8,1536]{1,0:T(8,128)S(1)} %get-tuple-element.29.extra_ref), custom_call_target="tpu_custom_call" | custom-call | tf_op jit(solution)/shard_map/second_own/pallas_call | solution.py:450
  100.5 5.6 %all-to-all-done.5.received_ref = bf16[16,104,128]{2,1,0:T(8,128)(2,1)S(1)} async-done(((bf16[16,104,128]{2,1,0:T(8,128)(2,1)}), bf16[16,104,128]{2,1,0:T(8,128)(2,1)S(1)}, u32[]{:S(2)}, u32[]{:S(2)}) %all-to-all-start.5) | async-done | bytes 426016 | tf_op jit(solution)/shard_map/all_to_all | solution.py:562
  106.1 0.7 join.1
  106.8 18.3 %all_to_all.39.received_ref = bf16[16,104,128]{2,1,0:T(8,128)(2,1)S(1)} all-to-all(bf16[16,104,128]{2,1,0:T(8,128)(2,1)S(1)} %join.1), channel_id=1, replica_groups={{0,32,64,96,128,160,192,224,16,48,80,112,144,176,208,240},{1,33,65,97,1..., dimensions={0} | all-to-all | bytes 851968 | tf_op jit(solution)/shard_map/all_to_all | solution.py:565
  125.1 3.0 %small_solves.1 = (f32[8,1536]{1,0:T(8,128)}, f32[8,1536]{1,0:T(8,128)}) custom-call(bf16[16,104,128]{2,1,0:T(8,128)(2,1)S(1)} %all_to_all.39.received_ref, f32[8,1536]{1,0:T(8,128)S(1)} %copy-done, f32[8,1536]{1,0:T(8,128)S(1)} %get-tuple-element.27.mid_ref, f32[1,1536]{1,0:T(1,128)S(1)} %get-tuple-element.28.shifted_ref), custom_call_target="tpu_custom_call" | custom-call | tf_op jit(solution)/shard_map/small_solves/pallas_call | solution.py:450
Async XLA Ops:
  0.6 48.3 %copy-start = (f32[8,1536]{1,0:T(8,128)S(1)}, f32[8,1536]{1,0:T(8,128)}, u32[]{:S(2)}) copy-start(f32[8,1536]{1,0:T(8,128)} %base_ref.5) | copy-start | bytes 147460
  74.0 16.1 %all-to-all-start.4 = ((bf16[16,48,128]{2,1,0:T(8,128)(2,1)}), bf16[16,48,128]{2,1,0:T(8,128)(2,1)S(1)}, u32[]{:S(2)}, u32[]{:S(2)}) async-start(bf16[16,48,128]{2,1,0:T(8,128)(2,1)} %spread.1), calls=%async_computation.4 | async-start | bytes 393216 | tf_op jit(solution)/shard_map/all_to_all | solution.py:565
  91.8 14.4 %all-to-all-start.5 = ((bf16[16,104,128]{2,1,0:T(8,128)(2,1)}), bf16[16,104,128]{2,1,0:T(8,128)(2,1)S(1)}, u32[]{:S(2)}, u32[]{:S(2)}) async-start(bf16[16,104,128]{2,1,0:T(8,128)(2,1)} %get-tuple-element.32), calls=%async_computation.5 | async-start | bytes 851968 | tf_op jit(solution)/shard_map/all_to_all | solution.py:562

commit v7 on v6

--- a/solution.py
+++ b/solution.py
@@ -19,14 +19,13 @@
     cols = wide_ref.shape[1]
     lane_block = lax.broadcasted_iota(jnp.int32, (col_blocks, cols), 1) // (cols // col_blocks)
     own_block = lax.broadcasted_iota(jnp.int32, (col_blocks, cols), 0)
-    spread = jnp.where(lane_block == own_block, 1.0, 0.0).astype(F32)
-    wide_ref[...] = lax.dot_general(
-        scales_ref[...],
-        spread,
-        (((0,), (0,)), ((), ())),
-        precision=lax.Precision.HIGHEST,
-        preferred_element_type=F32,
-    )
+    spread = jnp.where(lane_block == own_block, 1.0, 0.0).astype(BF16)
+    parts = jnp.concatenate(three_parts(scales_ref[...]), axis=1).astype(BF16)
+    wide = lax.dot_general(
+        parts, spread, (((0,), (0,)), ((), ())), preferred_element_type=F32
+    )
+    count = wide_ref.shape[0]
+    wide_ref[...] = wide[:count] + (wide[count : 2 * count] + wide[2 * count :])
 
 
 def dequantize_slot(slot, slots, codes_ref, wide_ref, slab_ref, copies=()):
@@ -98,14 +97,14 @@
 
     @pl.when(slot < offset)
     def _():
+        beside()
         second = dot_t(own, slab_ref[...])
-        beside()
         put(jnp.concatenate([second, jnp.zeros((rhs, tile - half), F32)], axis=1))
 
     @pl.when(slot > offset)
     def _():
+        beside()
         first = dot(own[:, half:], slab_ref[...])
-        beside()
         put(first)
 
     @pl.when(slot == offset)

time: 129 us -> 128 us (level)
  no operation moved by 1% of the time
where the time goes in v7:
time: 128 us; the launch traced here: 127 us
  blocking collectives  78.4 us (61%)
  Pallas kernels  27.6 us (22%)
  waiting for transfers between devices  11.1 us (9%)
  starting transfers between devices  9.29 us (7%)
    all_to_all x2, blocking collectives, exchange_deep(): return lax.all_to_all(values, ('row', 'col'), 0, 0, axis_index_groups=deep)  40.4 us
    all_to_all x2, blocking collectives, exchange_near(): return lax.all_to_all(values, 'col', 0, 0, axis_index_groups=near)  27.3 us
    pallas_call x7, Pallas kernels, plain(): pl.pallas_call(kernel, in_specs=specs, out_shape=outs, scratch_shapes=scr...  15.2 us
    all_to_all x1, blocking collectives, exchange_row(): return lax.all_to_all(values, 'row', 0, 0)  10.6 us
    pallas_call x1, Pallas kernels, local(): pl.pallas_call(first_rows_kernel, in_specs=[SMEM] + [pl.BlockSpec(memory_...  7.1 us
    all_to_all x1, starting transfers between devices, exchange_deep(): return lax.all_to_all(values, ('row', 'col'), 0, 0, axis_index_groups=deep)  5.74 us
    all_to_all x1, waiting for transfers between devices, exchange_near(): return lax.all_to_all(values, 'col', 0, 0, axis_index_groups=near)  5.64 us
    all_to_all x1, waiting for transfers between devices, exchange_deep(): return lax.all_to_all(values, ('row', 'col'), 0, 0, axis_index_groups=deep)  5.44 us
  transfers between devices with their start and end apart: 2, of which 2 were waited for; matrix products, arithmetic and copies ran while one was open for 0% of the time, Pallas kernels for 8%

profile of v7, /device:TPU:1, one launch (start us, length us, event | category | flops | bytes accessed | tf_op | source)
XLA Modules:
  0.0 127.2 jit_solution(15650855054555764968)
XLA Ops:
  0.6 0.0 copy-start
  0.7 0.1 stack.35.place_ref
  0.8 7.1 %first_rows.1 = (bf16[3072,1536]{1,0:T(8,128)(2,1)S(1)}, bf16[3072,1536]{1,0:T(8,128)(2,1)}, bf16[4,4,108,128]{3,2,1,0:T(8,128)(2,1)S(1)}, f32[8,1536]{1,0:T(8,1...) custom-call(s32[8]{0:T(128)S(1)} %stack.35.place_ref, bf16[3072,1536]{1,0:T(8,128)(2,1)} %codes_hbm.1, ...), custom_call_target="tpu_custom_call" | custom-call | tf_op jit(solution)/shard_map/first_rows/pallas_call | solution.py:573
  7.9 17.8 %all_to_all.35.received_ref = bf16[16,108,128]{2,1,0:T(8,128)(2,1)S(1)} all-to-all(bf16[16,108,128]{2,1,0:T(8,128)(2,1)S(1)} %bitcast.10), channel_id=1, replica_groups={{0,1,2,3,4,5,6,7,8,9,10,11,12,13,14,15},{16,17,18,19,20,21,22,23,24,25,..., dimensions={0} | all-to-all | bytes 884736 | tf_op jit(solution)/shard_map/all_to_all | solution.py:561
  25.7 0.1 relay.1
  25.8 22.2 %all_to_all.36.received_ref = bf16[16,60,128]{2,1,0:T(8,128)(2,1)S(1)} all-to-all(bf16[16,60,128]{2,1,0:T(8,128)(2,1)S(1)} %relay.1), channel_id=1, replica_groups={{0,32,64,96,128,160,192,224,16,48,80,112,144,176,208,240},{1,33,65,97,1..., dimensions={0} | all-to-all | bytes 491520 | tf_op jit(solution)/shard_map/all_to_all | solution.py:564
  48.0 0.0 copy-done
  48.0 3.6 %first_own.1 = (bf16[8,108,128]{2,1,0:T(8,128)(2,1)S(1)}, bf16[3072,1536]{1,0:T(8,128)(2,1)}) custom-call(s32[8]{0:T(128)S(1)} %stack.35.place_ref, bf16[3072,1536]{1,0:T(8,128)(2,1)S(1)} %get-tuple-element.18.slab_ref, bf16[16,60,128]{2,1,0:T(8,128)(2,1)S(1)} %all_to_all.36.received_ref, f32[8,1536]{1,0:T(8,128)S(1)} %copy-done, ...), custom_call_target="tpu_custom_call", output_to_operand_aliasing={{1}: (5, {})} | custom-call | tf_op jit(solution)/shard_map/first_own/pallas_call | solution.py:611
  51.6 10.6 %all_to_all.37.received_ref = bf16[8,108,128]{2,1,0:T(8,128)(2,1)S(1)} all-to-all(bf16[8,108,128]{2,1,0:T(8,128)(2,1)S(1)} %get-tuple-element.22), channel_id=1, replica_groups=mesh['row'=8,'col'=32] {'row'}, dimensions={0} | all-to-all | bytes 442368 | tf_op jit(solution)/shard_map/all_to_all | solution.py:567
  62.2 0.6 combine.1
  62.8 9.5 %all_to_all.38.received_ref = bf16[16,12,128]{2,1,0:T(8,128)(2,1)S(1)} all-to-all(bf16[16,12,128]{2,1,0:T(8,128)(2,1)S(1)} %get-tuple-element.24), channel_id=1, replica_groups={{0,1,2,3,4,5,6,7,8,9,10,11,12,13,14,15},{16,17,18,19,20,21,22,23,24,25,..., dimensions={0} | all-to-all | bytes 98304 | tf_op jit(solution)/shard_map/all_to_all | solution.py:561
  72.4 0.7 spread.1
  73.1 5.7 %all-to-all-start.4 = ((bf16[16,48,128]{2,1,0:T(8,128)(2,1)}), bf16[16,48,128]{2,1,0:T(8,128)(2,1)S(1)}, u32[]{:S(2)}, u32[]{:S(2)}) async-start(bf16[16,48,128]{2,1,0:T(8,128)(2,1)} %spread.1), calls=%async_computation.4 | async-start | bytes 393216 | tf_op jit(solution)/shard_map/all_to_all | solution.py:564
  78.8 4.9 %second_rows.1 = (bf16[4,8,1536]{2,1,0:T(8,128)(2,1)S(1)}, f32[8,1536]{1,0:T(8,128)S(1)}, f32[8,128]{1,0:T(8,128)S(1)}) custom-call(s32[8]{0:T(128)S(1)} %stack.35.place_ref, bf16[3072,1536]{1,0:T(8,128)(2,1)} %get-tuple-element.26.slab_hbm, bf16[8,1536]{1,0:T(8,128)(2,1)S(1)} %get-tuple-element.25.own_ref, f32[8,1536]{1,0:T(8,128)S(1)} %copy-done, ...), custom_call_target="tpu_custom_call" | custom-call | tf_op jit(solution)/shard_map/second_rows/pallas_call | solution.py:449
  83.7 5.4 %all-to-all-done.4.received_ref = bf16[16,48,128]{2,1,0:T(8,128)(2,1)S(1)} async-done(((bf16[16,48,128]{2,1,0:T(8,128)(2,1)}), bf16[16,48,128]{2,1,0:T(8,128)(2,1)S(1)}, u32[]{:S(2)}, u32[]{:S(2)}) %all-to-all-start.4) | async-done | bytes 196640 | tf_op jit(solution)/shard_map/all_to_all | solution.py:564
  89.2 1.6 %pair.1 = (bf16[16,104,128]{2,1,0:T(8,128)(2,1)}, bf16[8,6144]{1,0:T(8,128)(2,1)S(1)}) custom-call(s32[8]{0:T(128)S(1)} %stack.35.place_ref, bf16[16,48,128]{2,1,0:T(8,128)(2,1)S(1)} %all-to-all-done.4.received_ref, bf16[8,1536]{1,0:T(8,128)(2,1)S(1)} %get-tuple-element.25.own_ref, f32[8,1536]{1,0:T(8,128)S(1)} %get-tuple-element.29.extra_ref, ...), custom_call_target="tpu_custom_call" | custom-call | tf_op jit(solution)/shard_map/pair/pallas_call | solution.py:664
  90.8 3.6 %all-to-all-start.5 = ((bf16[16,104,128]{2,1,0:T(8,128)(2,1)}), bf16[16,104,128]{2,1,0:T(8,128)(2,1)S(1)}, u32[]{:S(2)}, u32[]{:S(2)}) async-start(bf16[16,104,128]{2,1,0:T(8,128)(2,1)} %get-tuple-element.32), calls=%async_computation.5 | async-start | bytes 851968 | tf_op jit(solution)/shard_map/all_to_all | solution.py:561
  94.4 5.2 %second_own.1.own_ref = f32[96,128]{1,0:T(8,128)S(1)} custom-call(s32[8]{0:T(128)S(1)} %stack.35.place_ref, bf16[3072,1536]{1,0:T(8,128)(2,1)} %get-tuple-element.26.slab_hbm, bf16[8,6144]{1,0:T(8,128)(2,1)S(1)} %get-tuple-element.33.rows_ref, bf16[8,1536]{1,0:T(8,128)(2,1)S(1)} %get-tuple-element.25.own_ref, f32[8,1536]{1,0:T(8,128)S(1)} %get-tuple-element.29.extra_ref), custom_call_target="tpu_custom_call" | custom-call | tf_op jit(solution)/shard_map/second_own/pallas_call | solution.py:449
  99.5 5.6 %all-to-all-done.5.received_ref = bf16[16,104,128]{2,1,0:T(8,128)(2,1)S(1)} async-done(((bf16[16,104,128]{2,1,0:T(8,128)(2,1)}), bf16[16,104,128]{2,1,0:T(8,128)(2,1)S(1)}, u32[]{:S(2)}, u32[]{:S(2)}) %all-to-all-start.5) | async-done | bytes 426016 | tf_op jit(solution)/shard_map/all_to_all | solution.py:561
  105.2 0.7 join.1
  105.9 18.3 %all_to_all.39.received_ref = bf16[16,104,128]{2,1,0:T(8,128)(2,1)S(1)} all-to-all(bf16[16,104,128]{2,1,0:T(8,128)(2,1)S(1)} %join.1), channel_id=1, replica_groups={{0,32,64,96,128,160,192,224,16,48,80,112,144,176,208,240},{1,33,65,97,1..., dimensions={0} | all-to-all | bytes 851968 | tf_op jit(solution)/shard_map/all_to_all | solution.py:564
  124.2 3.0 %small_solves.1 = (f32[8,1536]{1,0:T(8,128)}, f32[8,1536]{1,0:T(8,128)}) custom-call(bf16[16,104,128]{2,1,0:T(8,128)(2,1)S(1)} %all_to_all.39.received_ref, f32[8,1536]{1,0:T(8,128)S(1)} %copy-done, f32[8,1536]{1,0:T(8,128)S(1)} %get-tuple-element.27.mid_ref, f32[1,1536]{1,0:T(1,128)S(1)} %get-tuple-element.28.shifted_ref), custom_call_target="tpu_custom_call" | custom-call | tf_op jit(solution)/shard_map/small_solves/pallas_call | solution.py:449
Async XLA Ops:
  0.6 47.3 %copy-start = (f32[8,1536]{1,0:T(8,128)S(1)}, f32[8,1536]{1,0:T(8,128)}, u32[]{:S(2)}) copy-start(f32[8,1536]{1,0:T(8,128)} %base_ref.5) | copy-start | bytes 147460
  73.1 16.1 %all-to-all-start.4 = ((bf16[16,48,128]{2,1,0:T(8,128)(2,1)}), bf16[16,48,128]{2,1,0:T(8,128)(2,1)S(1)}, u32[]{:S(2)}, u32[]{:S(2)}) async-start(bf16[16,48,128]{2,1,0:T(8,128)(2,1)} %spread.1), calls=%async_computation.4 | async-start | bytes 393216 | tf_op jit(solution)/shard_map/all_to_all | solution.py:564
  90.8 14.4 %all-to-all-start.5 = ((bf16[16,104,128]{2,1,0:T(8,128)(2,1)}), bf16[16,104,128]{2,1,0:T(8,128)(2,1)S(1)}, u32[]{:S(2)}, u32[]{:S(2)}) async-start(bf16[16,104,128]{2,1,0:T(8,128)(2,1)} %get-tuple-element.32), calls=%async_computation.5 | async-start | bytes 851968 | tf_op jit(solution)/shard_map/all_to_all | solution.py:561

commit v8 on v7

--- a/solution.py
+++ b/solution.py
@@ -109,11 +109,11 @@
 
     @pl.when(slot == offset)
     def _():
+        beside()
         low, high = triangles(slab_ref)
         head, tail = own[:, :half], own[:, half:]
         extra_ref[:, :half] = dot_t(head, low) + dot_t(tail, slab_ref[:, half:])
         extra_ref[:, half:] = dot_t(tail, high)
-        beside()
         put(jnp.zeros((rhs, tile), F32))
 
 

time: 128 us -> 128 us (level)
  no operation moved by 1% of the time
where the time goes in v8:
time: 128 us; the launch traced here: 127 us
  blocking collectives  78.4 us (61%)
  Pallas kernels  27.6 us (22%)
  waiting for transfers between devices  11.1 us (9%)
  starting transfers between devices  9.29 us (7%)
    all_to_all x2, blocking collectives, exchange_deep(): return lax.all_to_all(values, ('row', 'col'), 0, 0, axis_index_groups=deep)  40.4 us
    all_to_all x2, blocking collectives, exchange_near(): return lax.all_to_all(values, 'col', 0, 0, axis_index_groups=near)  27.3 us
    pallas_call x7, Pallas kernels, plain(): pl.pallas_call(kernel, in_specs=specs, out_shape=outs, scratch_shapes=scr...  15.2 us
    all_to_all x1, blocking collectives, exchange_row(): return lax.all_to_all(values, 'row', 0, 0)  10.6 us
    pallas_call x1, Pallas kernels, local(): pl.pallas_call(first_rows_kernel, in_specs=[SMEM] + [pl.BlockSpec(memory_...  7.1 us
    all_to_all x1, starting transfers between devices, exchange_deep(): return lax.all_to_all(values, ('row', 'col'), 0, 0, axis_index_groups=deep)  5.74 us
    all_to_all x1, waiting for transfers between devices, exchange_near(): return lax.all_to_all(values, 'col', 0, 0, axis_index_groups=near)  5.64 us
    all_to_all x1, waiting for transfers between devices, exchange_deep(): return lax.all_to_all(values, ('row', 'col'), 0, 0, axis_index_groups=deep)  5.44 us
  transfers between devices with their start and end apart: 2, of which 2 were waited for; matrix products, arithmetic and copies ran while one was open for 0% of the time, Pallas kernels for 8%

profile of v8, /device:TPU:1, one launch (start us, length us, event | category | flops | bytes accessed | tf_op | source)
XLA Modules:
  0.0 127.2 jit_solution(2077097176718198770)
XLA Ops:
  0.6 0.0 copy-start
  0.7 0.1 stack.35.place_ref
  0.8 7.1 %first_rows.1 = (bf16[3072,1536]{1,0:T(8,128)(2,1)S(1)}, bf16[3072,1536]{1,0:T(8,128)(2,1)}, bf16[4,4,108,128]{3,2,1,0:T(8,128)(2,1)S(1)}, f32[8,1536]{1,0:T(8,1...) custom-call(s32[8]{0:T(128)S(1)} %stack.35.place_ref, bf16[3072,1536]{1,0:T(8,128)(2,1)} %codes_hbm.1, ...), custom_call_target="tpu_custom_call" | custom-call | tf_op jit(solution)/shard_map/first_rows/pallas_call | solution.py:573
  7.9 17.8 %all_to_all.35.received_ref = bf16[16,108,128]{2,1,0:T(8,128)(2,1)S(1)} all-to-all(bf16[16,108,128]{2,1,0:T(8,128)(2,1)S(1)} %bitcast.10), channel_id=1, replica_groups={{0,1,2,3,4,5,6,7,8,9,10,11,12,13,14,15},{16,17,18,19,20,21,22,23,24,25,..., dimensions={0} | all-to-all | bytes 884736 | tf_op jit(solution)/shard_map/all_to_all | solution.py:561
  25.7 0.1 relay.1
  25.8 22.2 %all_to_all.36.received_ref = bf16[16,60,128]{2,1,0:T(8,128)(2,1)S(1)} all-to-all(bf16[16,60,128]{2,1,0:T(8,128)(2,1)S(1)} %relay.1), channel_id=1, replica_groups={{0,32,64,96,128,160,192,224,16,48,80,112,144,176,208,240},{1,33,65,97,1..., dimensions={0} | all-to-all | bytes 491520 | tf_op jit(solution)/shard_map/all_to_all | solution.py:564
  48.0 0.0 copy-done
  48.0 3.6 %first_own.1 = (bf16[8,108,128]{2,1,0:T(8,128)(2,1)S(1)}, bf16[3072,1536]{1,0:T(8,128)(2,1)}) custom-call(s32[8]{0:T(128)S(1)} %stack.35.place_ref, bf16[3072,1536]{1,0:T(8,128)(2,1)S(1)} %get-tuple-element.18.slab_ref, bf16[16,60,128]{2,1,0:T(8,128)(2,1)S(1)} %all_to_all.36.received_ref, f32[8,1536]{1,0:T(8,128)S(1)} %copy-done, ...), custom_call_target="tpu_custom_call", output_to_operand_aliasing={{1}: (5, {})} | custom-call | tf_op jit(solution)/shard_map/first_own/pallas_call | solution.py:611
  51.6 10.6 %all_to_all.37.received_ref = bf16[8,108,128]{2,1,0:T(8,128)(2,1)S(1)} all-to-all(bf16[8,108,128]{2,1,0:T(8,128)(2,1)S(1)} %get-tuple-element.22), channel_id=1, replica_groups=mesh['row'=8,'col'=32] {'row'}, dimensions={0} | all-to-all | bytes 442368 | tf_op jit(solution)/shard_map/all_to_all | solution.py:567
  62.2 0.6 combine.1
  62.8 9.5 %all_to_all.38.received_ref = bf16[16,12,128]{2,1,0:T(8,128)(2,1)S(1)} all-to-all(bf16[16,12,128]{2,1,0:T(8,128)(2,1)S(1)} %get-tuple-element.24), channel_id=1, replica_groups={{0,1,2,3,4,5,6,7,8,9,10,11,12,13,14,15},{16,17,18,19,20,21,22,23,24,25,..., dimensions={0} | all-to-all | bytes 98304 | tf_op jit(solution)/shard_map/all_to_all | solution.py:561
  72.4 0.7 spread.1
  73.1 5.7 %all-to-all-start.4 = ((bf16[16,48,128]{2,1,0:T(8,128)(2,1)}), bf16[16,48,128]{2,1,0:T(8,128)(2,1)S(1)}, u32[]{:S(2)}, u32[]{:S(2)}) async-start(bf16[16,48,128]{2,1,0:T(8,128)(2,1)} %spread.1), calls=%async_computation.4 | async-start | bytes 393216 | tf_op jit(solution)/shard_map/all_to_all | solution.py:564
  78.8 4.9 %second_rows.1 = (bf16[4,8,1536]{2,1,0:T(8,128)(2,1)S(1)}, f32[8,1536]{1,0:T(8,128)S(1)}, f32[8,128]{1,0:T(8,128)S(1)}) custom-call(s32[8]{0:T(128)S(1)} %stack.35.place_ref, bf16[3072,1536]{1,0:T(8,128)(2,1)} %get-tuple-element.26.slab_hbm, bf16[8,1536]{1,0:T(8,128)(2,1)S(1)} %get-tuple-element.25.own_ref, f32[8,1536]{1,0:T(8,128)S(1)} %copy-done, ...), custom_call_target="tpu_custom_call" | custom-call | tf_op jit(solution)/shard_map/second_rows/pallas_call | solution.py:449
  83.7 5.4 %all-to-all-done.4.received_ref = bf16[16,48,128]{2,1,0:T(8,128)(2,1)S(1)} async-done(((bf16[16,48,128]{2,1,0:T(8,128)(2,1)}), bf16[16,48,128]{2,1,0:T(8,128)(2,1)S(1)}, u32[]{:S(2)}, u32[]{:S(2)}) %all-to-all-start.4) | async-done | bytes 196640 | tf_op jit(solution)/shard_map/all_to_all | solution.py:564
  89.2 1.6 %pair.1 = (bf16[16,104,128]{2,1,0:T(8,128)(2,1)}, bf16[8,6144]{1,0:T(8,128)(2,1)S(1)}) custom-call(s32[8]{0:T(128)S(1)} %stack.35.place_ref, bf16[16,48,128]{2,1,0:T(8,128)(2,1)S(1)} %all-to-all-done.4.received_ref, bf16[8,1536]{1,0:T(8,128)(2,1)S(1)} %get-tuple-element.25.own_ref, f32[8,1536]{1,0:T(8,128)S(1)} %get-tuple-element.29.extra_ref, ...), custom_call_target="tpu_custom_call" | custom-call | tf_op jit(solution)/shard_map/pair/pallas_call | solution.py:664
  90.8 3.6 %all-to-all-start.5 = ((bf16[16,104,128]{2,1,0:T(8,128)(2,1)}), bf16[16,104,128]{2,1,0:T(8,128)(2,1)S(1)}, u32[]{:S(2)}, u32[]{:S(2)}) async-start(bf16[16,104,128]{2,1,0:T(8,128)(2,1)} %get-tuple-element.32), calls=%async_computation.5 | async-start | bytes 851968 | tf_op jit(solution)/shard_map/all_to_all | solution.py:561
  94.4 5.2 %second_own.1.own_ref = f32[96,128]{1,0:T(8,128)S(1)} custom-call(s32[8]{0:T(128)S(1)} %stack.35.place_ref, bf16[3072,1536]{1,0:T(8,128)(2,1)} %get-tuple-element.26.slab_hbm, bf16[8,6144]{1,0:T(8,128)(2,1)S(1)} %get-tuple-element.33.rows_ref, bf16[8,1536]{1,0:T(8,128)(2,1)S(1)} %get-tuple-element.25.own_ref, f32[8,1536]{1,0:T(8,128)S(1)} %get-tuple-element.29.extra_ref), custom_call_target="tpu_custom_call" | custom-call | tf_op jit(solution)/shard_map/second_own/pallas_call | solution.py:449
  99.5 5.6 %all-to-all-done.5.received_ref = bf16[16,104,128]{2,1,0:T(8,128)(2,1)S(1)} async-done(((bf16[16,104,128]{2,1,0:T(8,128)(2,1)}), bf16[16,104,128]{2,1,0:T(8,128)(2,1)S(1)}, u32[]{:S(2)}, u32[]{:S(2)}) %all-to-all-start.5) | async-done | bytes 426016 | tf_op jit(solution)/shard_map/all_to_all | solution.py:561
  105.2 0.7 join.1
  105.9 18.3 %all_to_all.39.received_ref = bf16[16,104,128]{2,1,0:T(8,128)(2,1)S(1)} all-to-all(bf16[16,104,128]{2,1,0:T(8,128)(2,1)S(1)} %join.1), channel_id=1, replica_groups={{0,32,64,96,128,160,192,224,16,48,80,112,144,176,208,240},{1,33,65,97,1..., dimensions={0} | all-to-all | bytes 851968 | tf_op jit(solution)/shard_map/all_to_all | solution.py:564
  124.2 3.0 %small_solves.1 = (f32[8,1536]{1,0:T(8,128)}, f32[8,1536]{1,0:T(8,128)}) custom-call(bf16[16,104,128]{2,1,0:T(8,128)(2,1)S(1)} %all_to_all.39.received_ref, f32[8,1536]{1,0:T(8,128)S(1)} %copy-done, f32[8,1536]{1,0:T(8,128)S(1)} %get-tuple-element.27.mid_ref, f32[1,1536]{1,0:T(1,128)S(1)} %get-tuple-element.28.shifted_ref), custom_call_target="tpu_custom_call" | custom-call | tf_op jit(solution)/shard_map/small_solves/pallas_call | solution.py:449
Async XLA Ops:
  0.6 47.3 %copy-start = (f32[8,1536]{1,0:T(8,128)S(1)}, f32[8,1536]{1,0:T(8,128)}, u32[]{:S(2)}) copy-start(f32[8,1536]{1,0:T(8,128)} %base_ref.5) | copy-start | bytes 147460
  73.1 16.1 %all-to-all-start.4 = ((bf16[16,48,128]{2,1,0:T(8,128)(2,1)}), bf16[16,48,128]{2,1,0:T(8,128)(2,1)S(1)}, u32[]{:S(2)}, u32[]{:S(2)}) async-start(bf16[16,48,128]{2,1,0:T(8,128)(2,1)} %spread.1), calls=%async_computation.4 | async-start | bytes 393216 | tf_op jit(solution)/shard_map/all_to_all | solution.py:564
  90.8 14.4 %all-to-all-start.5 = ((bf16[16,104,128]{2,1,0:T(8,128)(2,1)}), bf16[16,104,128]{2,1,0:T(8,128)(2,1)S(1)}, u32[]{:S(2)}, u32[]{:S(2)}) async-start(bf16[16,104,128]{2,1,0:T(8,128)(2,1)} %get-tuple-element.32), calls=%async_computation.5 | async-start | bytes 851968 | tf_op jit(solution)/shard_map/all_to_all | solution.py:561
